TPU v7x, 128 devices: a whole 4x4x4 slice. The times are simulated.
128 devices in a mesh: gx: 4 (over x), gy: 4 (over y), gz: 8 (over z, core).
Axes of the slice: x: 4, y: 4, z: 4, core: 2. Of those that a mesh axis runs over, the one named last changes fastest.
Arguments:
- source: float32 [128, 128, 512], P('gz', 'gx', 'gy'), may hold values from -24 to 24
- conductivity: float32 [128, 128, 512], P('gz', 'gx', 'gy'), may hold values from 1 to 10
- cell_kind: int32 [128, 128, 512], P('gz', 'gx', 'gy'), may hold values from 0 to 2
Outputs:
- potential: float32 [128, 128, 512], P('gz', 'gx', 'gy')
- residual: float32 [128, 128, 512], P('gz', 'gx', 'gy')
All inputs are finite; a program needn't handle non-finite values.
Results may differ from a plain program's by a relative error of at most 0.0003.
Values sent between devices are 32-bit elements; how exact they have to be, the bound alone decides.
No kernel may reach another device: no remote copies, remote signals or barrier semaphores. Data moves between devices by JAX's collectives and lax.ppermute only.
A program may use at most 128 MiB of HBM per device.

v0:
```python
import jax
import jax.numpy as jnp
from jax import lax
from jax.sharding import PartitionSpec as P

LEVELS = 4
PRE = 4
POST = 4
CSWEEPS = 32


damping_factor = 0.8
vertical_weight = 4.0
shift_term = 0.005
surface_term = 8.0
dry_term = 0.02
face_weights = (vertical_weight, vertical_weight, 1.0, 1.0, 1.0, 1.0)


def padded_2(block, sides, width):
    for axis, dim in sides:
        count = lax.axis_size(axis)
        forward = [(i, i + 1) for i in range(count - 1)]
        backward = [(target, source) for source, target in forward]
        low = lax.ppermute(
            lax.slice_in_dim(block, block.shape[dim] - width, None, axis=dim), axis, forward
        )
        high = lax.ppermute(lax.slice_in_dim(block, 0, width, axis=dim), axis, backward)
        block = jnp.concatenate([low, block, high], axis=dim)
    return block


def fold_cells(values):
    height, across, along = values.shape
    return values.reshape(height // 2, 2, across // 2, 2, along // 2, 2).sum(axis=(1, 3, 5))


def spread_cells(values):
    height, across, along = values.shape
    spread_out = jnp.broadcast_to(
        values[:, None, :, None, :, None], (height, 2, across, 2, along, 2)
    )
    return spread_out.reshape(height * 2, across * 2, along * 2)


def neighbours(padded):
    return [
        padded[:-2, 1:-1, 1:-1],
        padded[2:, 1:-1, 1:-1],
        padded[1:-1, :-2, 1:-1],
        padded[1:-1, 2:, 1:-1],
        padded[1:-1, 1:-1, :-2],
        padded[1:-1, 1:-1, 2:],
    ]


def couplings_of(stiffness, padded_stiffness):
    return [
        weight * jnp.minimum(stiffness, beside)
        for weight, beside in zip(face_weights, neighbours(padded_stiffness))
    ]


def diagonal_of(mass, couplings):
    diagonal = mass
    for coupling in couplings:
        diagonal = diagonal + coupling
    return diagonal


def apply_operator(potential, padded_potential, couplings, diagonal):
    applied = diagonal * potential
    for coupling, beside in zip(couplings, neighbours(padded_potential)):
        applied = applied - coupling * beside
    return applied


def relax(potential, forcing, couplings, diagonal, extend):
    applied = apply_operator(potential, extend(potential), couplings, diagonal)
    return potential + damping_factor * (forcing - applied) / diagonal


def zero_rim(values):
    return jnp.pad(values, 1)


def rim_stiffness(values):
    return padded_2(values, (("gx", 1), ("gy", 2), ("gz", 0)), 1)


def rim_potential(values):
    return padded_2(values, (("gx", 1), ("gy", 2), ("gz", 0)), 1)


def cycle(level_index, forcing, operators, extend, coarse_step):
    if level_index == len(operators):
        return coarse_step(forcing)
    couplings, diagonal = operators[level_index]
    potential = damping_factor * forcing / diagonal
    for sweep_index in range(PRE - 1):
        potential = relax(potential, forcing, couplings, diagonal, extend)
    remainder = forcing - apply_operator(potential, extend(potential), couplings, diagonal)
    correction = cycle(level_index + 1, fold_cells(remainder), operators, extend, coarse_step)
    potential = potential + spread_cells(correction)
    for sweep_index in range(POST):
        potential = relax(potential, forcing, couplings, diagonal, extend)
    return potential


def collect(forcing, stiffness, mass):
    pieces = (
        lax.all_gather(forcing, "gz", axis=0, tiled=True),
        lax.all_gather(stiffness, "gz", axis=0, tiled=True),
        lax.all_gather(mass, "gz", axis=0, tiled=True),
    )
    pieces = (
        lax.all_gather(pieces[0], "gx", axis=1, tiled=True),
        lax.all_gather(pieces[1], "gx", axis=1, tiled=True),
        lax.all_gather(pieces[2], "gx", axis=1, tiled=True),
    )
    return (
        lax.all_gather(pieces[0], "gy", axis=2, tiled=True),
        lax.all_gather(pieces[1], "gy", axis=2, tiled=True),
        lax.all_gather(pieces[2], "gy", axis=2, tiled=True),
    )


def shards(source, conductivity, cell_kind):
    wet = jnp.where(cell_kind > 0, 1.0, 0.0).astype(jnp.float32)
    surface = jnp.where(cell_kind == 2, 1.0, 0.0).astype(jnp.float32)
    stiffness = conductivity * wet
    mass = shift_term * stiffness + surface_term * stiffness * surface + dry_term * (1.0 - wet)
    forcing = source * wet
    gathered_level = LEVELS
    operators = []
    for level_index in range(gathered_level):
        couplings = couplings_of(stiffness, rim_stiffness(stiffness))
        operators.append((couplings, diagonal_of(mass, couplings)))
        stiffness = 0.25 * fold_cells(stiffness)
        mass = fold_cells(mass)
    coarse_stiffness = stiffness
    coarse_mass = mass

    def coarse_step(coarse_forcing):
        whole_forcing, whole_stiffness, whole_mass = collect(
            coarse_forcing, coarse_stiffness, coarse_mass
        )
        global_operators = []
        last_couplings = couplings_of(whole_stiffness, zero_rim(whole_stiffness))
        last_diagonal = diagonal_of(whole_mass, last_couplings)

        def solve_coarsest(coarse_source):

            def sweep(step_index, current):
                return relax(current, coarse_source, last_couplings, last_diagonal, zero_rim)

            return lax.fori_loop(0, CSWEEPS, sweep, jnp.zeros_like(coarse_source))

        whole_correction = cycle(0, whole_forcing, global_operators, zero_rim, solve_coarsest)
        height, across, along = coarse_forcing.shape
        starts = (
            lax.axis_index("gz") * height,
            lax.axis_index("gx") * across,
            lax.axis_index("gy") * along,
        )
        return lax.dynamic_slice(whole_correction, starts, (height, across, along))

    potential = cycle(0, forcing, operators, rim_potential, coarse_step)
    couplings, diagonal = operators[0]
    residual = forcing - apply_operator(potential, rim_potential(potential), couplings, diagonal)
    return (potential, residual)


def solution(mesh):
    return jax.shard_map(
        shards,
        mesh=mesh,
        in_specs=(P("gz", "gx", "gy"), P("gz", "gx", "gy"), P("gz", "gx", "gy")),
        out_specs=(P("gz", "gx", "gy"), P("gz", "gx", "gy")),
        check_vma=False,
    )
```

profile of v0, /device:TPU:1, one launch (start us, length us, event | category | flops | bytes accessed | tf_op | source)
XLA Modules:
  0.0 1073.0 jit_solution(11232991458983253500)
XLA Ops:
  20.4 6.7 collective-permute-start.4
  41.6 4.8 collective-permute-start.8
  46.3 5.1 collective-permute-done.9
  69.2 4.8 collective-permute-start.14
  74.0 5.2 collective-permute-done.15
  94.3 18.1 %reshape.75 = f32[8,2,16,2,64,2]{5,4,3,2,1,0:T(8,128)} reshape(f32[16,32,128]{2,1,0:T(8,128)S(1)} %get-tuple-element.241) | data formatting | bytes 524288 | tf_op jit(solution)/shard_map/reshape | solution.py:35
  112.4 7.0 reduce_sum.127
  121.0 4.8 collective-permute-start.20
  125.7 5.0 collective-permute-done.21
  143.4 18.1 %reshape.74 = f32[8,2,16,2,64,2]{5,4,3,2,1,0:T(8,128)} reshape(f32[16,32,128]{2,1,0:T(8,128)S(1)} %get-tuple-element.199) | data formatting | bytes 524288 | tf_op jit(solution)/shard_map/reshape | solution.py:35
  161.5 7.0 reduce_sum.126
  170.4 4.9 collective-permute-start.24
  200.9 18.1 %reshape.73 = f32[8,2,16,2,64,2]{5,4,3,2,1,0:T(8,128)} reshape(f32[16,32,128]{2,1,0:T(8,128)S(1)} %fusion.97) | data formatting | bytes 524288 | tf_op jit(solution)/shard_map/reshape | solution.py:35
  219.0 7.0 reduce_sum.125
  268.8 5.3 collective-permute-start.46
  295.6 5.6 collective-permute-start.52
  314.4 4.9 collective-permute-start.54
  371.7 8.5 all-gather.3
  380.2 10.4 all_gather.28
  396.1 11.1 %all_gather.29 = f32[8,8,32]{1,0,2:T(8,128)S(1)} all-gather(f32[8,8,8]{1,0,2:T(8,128)S(1)} %copy.6), channel_id=1, replica_groups=mesh['gx'=4,'gy'=4,'gz'=8] {'gy'}, dimensions={2}, use_global_device_ids=true | all-gather | bytes 10240 | tf_op jit(solution)/shard_map/all_gather | solution.py:124
  407.3 13.8 %all-gather.4 = f32[8,2,8]{2,1,0:T(2,128)S(1)} all-gather(f32[1,2,8]{2,1,0:T(2,128)S(1)} %multiply_bitcast_fusion), channel_id=3, replica_groups=mesh['gx'=4,'gy'=4,'gz'=8] {'gz'}, dimensions={0}, use_global_device_ids=true | all-gather | bytes 576 | tf_op jit(solution)/shard_map/all_gather | solution.py:113
  426.8 9.0 all_gather.31
  436.0 5.3 collective-permute-start.77
  444.8 9.1 all_gather.32
  466.9 5.5 collective-permute-start.83
  497.7 5.3 collective-permute-start.88
  548.5 5.1 collective-permute-start.106
  593.4 5.9 collective-permute-start.118
  600.9 10.3 all-gather.5
  611.2 10.9 %all_gather.34 = f32[8,8,8]{2,0,1:T(8,128)S(1)} all-gather(f32[8,2,8]{2,0,1:T(8,128)S(1)} %copy.9), channel_id=1, replica_groups=mesh['gx'=4,'gy'=4,'gz'=8] {'gx'}, dimensions={1}, use_global_device_ids=true | all-gather | bytes 2560 | tf_op jit(solution)/shard_map/all_gather | solution.py:117
  622.2 11.0 %all_gather.35 = f32[8,8,32]{1,0,2:T(8,128)S(1)} all-gather(f32[8,8,8]{1,0,2:T(8,128)S(1)} %copy.10), channel_id=1, replica_groups=mesh['gx'=4,'gy'=4,'gz'=8] {'gy'}, dimensions={2}, use_global_device_ids=true | all-gather | bytes 10240 | tf_op jit(solution)/shard_map/all_gather | solution.py:122
  650.3 9.4 collective-permute-start.125
  701.5 5.3 collective-permute-start.136
  723.5 5.9 collective-permute-start.142
  746.7 5.9 collective-permute-start.148
  769.0 5.9 collective-permute-start.154
  791.3 5.9 collective-permute-start.160
  813.7 6.1 collective-permute-start.166
  841.6 5.9 collective-permute-start.172
  864.9 5.9 collective-permute-start.178
  888.1 5.9 collective-permute-start.184
  911.4 5.9 collective-permute-start.190
  918.3 6.4 broadcast_in_dim.52
  924.8 12.6 %reshape.82 = f32[16,32,128]{2,1,0:T(8,128)S(1)} reshape(f32[8,2,16,2,64,2]{5,4,3,2,1,0:T(8,128)} %broadcast_in_dim.52) | data formatting | bytes 524288 | tf_op jit(solution)/shard_map/reshape | solution.py:43
  957.1 5.4 collective-permute-start.196
  998.6 4.8 collective-permute-start.206
  1029.9 5.4 collective-permute-done.213
  1057.3 6.2 collective-permute-done.219
  (743 shorter events, 709.2 us)
Async XLA Ops:
  40.3 11.2 %collective-permute-start.9 = (f32[16,34,1]{2,1,0:T(8,128)S(1)}, f32[16,34,1]{2,1,0:T(8,128)S(1)}, u32[]{:S(2)}, u32[]{:S(2)}) collective-permute-start(f32[16,34,1]{2,1,0:T(8,128)S(1)} %get-tuple-element.259), channel_id=1, source_target_pairs={{8,0},{16,8},{24,16},{9,1},{17,9},{25,17},{10,2},{18,10},{26,18},{... | collective-permute-start | bytes 6536 | tf_op jit(solution)/shard_map/ppermute | solution.py:28
  41.6 11.7 %collective-permute-start.8 = (f32[16,34,1]{2,1,0:T(8,128)S(1)}, f32[16,34,1]{2,1,0:T(8,128)S(1)}, u32[]{:S(2)}, u32[]{:S(2)}) collective-permute-start(f32[16,34,1]{2,1,0:T(8,128)S(1)} %get-tuple-element.258), channel_id=1, source_target_pairs={{0,8},{8,16},{16,24},{1,9},{9,17},{17,25},{2,10},{10,18},{18,26},{... | collective-permute-start | bytes 6536 | tf_op jit(solution)/shard_map/ppermute | solution.py:25
  67.9 11.2 %collective-permute-start.15 = (f32[16,34,1]{2,1,0:T(8,128)S(1)}, f32[16,34,1]{2,1,0:T(8,128)S(1)}, u32[]{:S(2)}, u32[]{:S(2)}) collective-permute-start(f32[16,34,1]{2,1,0:T(8,128)S(1)} %get-tuple-element.257), channel_id=1, source_target_pairs={{8,0},{16,8},{24,16},{9,1},{17,9},{25,17},{10,2},{18,10},{26,18},{... | collective-permute-start | bytes 6536 | tf_op jit(solution)/shard_map/ppermute | solution.py:28
  69.2 11.7 %collective-permute-start.14 = (f32[16,34,1]{2,1,0:T(8,128)S(1)}, f32[16,34,1]{2,1,0:T(8,128)S(1)}, u32[]{:S(2)}, u32[]{:S(2)}) collective-permute-start(f32[16,34,1]{2,1,0:T(8,128)S(1)} %get-tuple-element.256), channel_id=1, source_target_pairs={{0,8},{8,16},{16,24},{1,9},{9,17},{17,25},{2,10},{10,18},{18,26},{... | collective-permute-start | bytes 6536 | tf_op jit(solution)/shard_map/ppermute | solution.py:25
  88.8 30.7 %collective-permute-start.19 = (f32[16,1,128]{2,1,0:T(1,128)S(1)}, f32[16,1,128]{2,1,0:T(1,128)S(1)}, u32[]{:S(2)}, u32[]{:S(2)}) collective-permute-start(f32[16,1,128]{2,1,0:T(1,128)S(1)} %get-tuple-element.293), channel_id=1, source_target_pairs={{32,0},{64,32},{96,64},{33,1},{65,33},{97,65},{34,2},{66,34},{98,6... | collective-permute-start | bytes 24584 | tf_op jit(solution)/shard_map/ppermute | solution.py:28
  90.1 29.4 %collective-permute-start.18 = (f32[16,1,128]{2,1,0:T(1,128)S(1)}, f32[16,1,128]{2,1,0:T(1,128)S(1)}, u32[]{:S(2)}, u32[]{:S(2)}) collective-permute-start(f32[16,1,128]{2,1,0:T(1,128)S(1)} %get-tuple-element.292), channel_id=1, source_target_pairs={{0,32},{32,64},{64,96},{1,33},{33,65},{65,97},{2,34},{34,66},{66,9... | collective-permute-start | bytes 24584 | tf_op jit(solution)/shard_map/ppermute | solution.py:25
  119.7 11.1 %collective-permute-start.21 = (f32[16,34,1]{2,1,0:T(8,128)S(1)}, f32[16,34,1]{2,1,0:T(8,128)S(1)}, u32[]{:S(2)}, u32[]{:S(2)}) collective-permute-start(f32[16,34,1]{2,1,0:T(8,128)S(1)} %get-tuple-element.255), channel_id=1, source_target_pairs={{8,0},{16,8},{24,16},{9,1},{17,9},{25,17},{10,2},{18,10},{26,18},{... | collective-permute-start | bytes 6536 | tf_op jit(solution)/shard_map/ppermute | solution.py:28
  121.0 11.5 %collective-permute-start.20 = (f32[16,34,1]{2,1,0:T(8,128)S(1)}, f32[16,34,1]{2,1,0:T(8,128)S(1)}, u32[]{:S(2)}, u32[]{:S(2)}) collective-permute-start(f32[16,34,1]{2,1,0:T(8,128)S(1)} %get-tuple-element.254), channel_id=1, source_target_pairs={{0,8},{8,16},{16,24},{1,9},{9,17},{17,25},{2,10},{10,18},{18,26},{... | collective-permute-start | bytes 6536 | tf_op jit(solution)/shard_map/ppermute | solution.py:25
  132.6 35.9 %collective-permute-start.23 = (f32[1,34,130]{2,1,0:T(8,128)S(1)}, f32[1,34,130]{2,1,0:T(8,128)S(1)}, u32[]{:S(2)}, u32[]{:S(2)}) collective-permute-start(f32[1,34,130]{2,1,0:T(8,128)S(1)} %get-tuple-element.234), channel_id=1, source_target_pairs={{1,0},{2,1},{3,2},{4,3},{5,4},{6,5},{7,6},{9,8},{10,9},{11,10},{12... | collective-permute-start | bytes 53048 | tf_op jit(solution)/shard_map/ppermute | solution.py:28
  134.5 34.0 %collective-permute-start.22 = (f32[1,34,130]{2,1,0:T(8,128)S(1)}, f32[1,34,130]{2,1,0:T(8,128)S(1)}, u32[]{:S(2)}, u32[]{:S(2)}) collective-permute-start(f32[1,34,130]{2,1,0:T(8,128)S(1)} %get-tuple-element.233), channel_id=1, source_target_pairs={{0,1},{1,2},{2,3},{3,4},{4,5},{5,6},{6,7},{8,9},{9,10},{10,11},{11... | collective-permute-start | bytes 53048 | tf_op jit(solution)/shard_map/ppermute | solution.py:25
  138.7 36.6 %collective-permute-start.30 = (f32[8,1,64]{2,1,0:T(1,128)S(1)}, f32[8,1,64]{2,1,0:T(1,128)S(1)}, u32[]{:S(2)}, u32[]{:S(2)}) collective-permute-start(f32[8,1,64]{2,1,0:T(1,128)S(1)} %get-tuple-element.353), channel_id=1, source_target_pairs={{0,32},{32,64},{64,96},{1,33},{33,65},{65,97},{2,34},{34,66},{66,9... | collective-permute-start | bytes 6152 | tf_op jit(solution)/shard_map/ppermute | solution.py:25
  142.1 33.3 %collective-permute-start.31 = (f32[8,1,64]{2,1,0:T(1,128)S(1)}, f32[8,1,64]{2,1,0:T(1,128)S(1)}, u32[]{:S(2)}, u32[]{:S(2)}) collective-permute-start(f32[8,1,64]{2,1,0:T(1,128)S(1)} %get-tuple-element.352), channel_id=1, source_target_pairs={{32,0},{64,32},{96,64},{33,1},{65,33},{97,65},{34,2},{66,34},{98,6... | collective-permute-start | bytes 6152 | tf_op jit(solution)/shard_map/ppermute | solution.py:28
  176.3 11.9 %collective-permute-start.27 = (f32[16,34,1]{2,1,0:T(8,128)S(1)}, f32[16,34,1]{2,1,0:T(8,128)S(1)}, u32[]{:S(2)}, u32[]{:S(2)}) collective-permute-start(f32[16,34,1]{2,1,0:T(8,128)S(1)} %get-tuple-element.253), channel_id=1, source_target_pairs={{8,0},{16,8},{24,16},{9,1},{17,9},{25,17},{10,2},{18,10},{26,18},{... | collective-permute-start | bytes 6536 | tf_op jit(solution)/shard_map/ppermute | solution.py:28
  177.6 11.5 %collective-permute-start.26 = (f32[16,34,1]{2,1,0:T(8,128)S(1)}, f32[16,34,1]{2,1,0:T(8,128)S(1)}, u32[]{:S(2)}, u32[]{:S(2)}) collective-permute-start(f32[16,34,1]{2,1,0:T(8,128)S(1)} %get-tuple-element.252), channel_id=1, source_target_pairs={{0,8},{8,16},{16,24},{1,9},{9,17},{17,25},{2,10},{10,18},{18,26},{... | collective-permute-start | bytes 6536 | tf_op jit(solution)/shard_map/ppermute | solution.py:25
  182.4 13.0 %collective-permute-start.33 = (f32[8,18,1]{2,1,0:T(8,128)S(1)}, f32[8,18,1]{2,1,0:T(8,128)S(1)}, u32[]{:S(2)}, u32[]{:S(2)}) collective-permute-start(f32[8,18,1]{2,1,0:T(8,128)S(1)} %get-tuple-element.317), channel_id=1, source_target_pairs={{8,0},{16,8},{24,16},{9,1},{17,9},{25,17},{10,2},{18,10},{26,18},{... | collective-permute-start | bytes 1736 | tf_op jit(solution)/shard_map/ppermute | solution.py:28
  183.7 11.7 %collective-permute-start.32 = (f32[8,18,1]{2,1,0:T(8,128)S(1)}, f32[8,18,1]{2,1,0:T(8,128)S(1)}, u32[]{:S(2)}, u32[]{:S(2)}) collective-permute-start(f32[8,18,1]{2,1,0:T(8,128)S(1)} %get-tuple-element.316), channel_id=1, source_target_pairs={{0,8},{8,16},{16,24},{1,9},{9,17},{17,25},{2,10},{10,18},{18,26},{... | collective-permute-start | bytes 1736 | tf_op jit(solution)/shard_map/ppermute | solution.py:25
  189.2 11.1 %collective-permute-start.29 = (f32[1,34,130]{2,1,0:T(8,128)S(1)}, f32[1,34,130]{2,1,0:T(8,128)S(1)}, u32[]{:S(2)}, u32[]{:S(2)}) collective-permute-start(f32[1,34,130]{2,1,0:T(8,128)S(1)} %get-tuple-element.232), channel_id=1, source_target_pairs={{1,0},{2,1},{3,2},{4,3},{5,4},{6,5},{7,6},{9,8},{10,9},{11,10},{12... | collective-permute-start | bytes 53048 | tf_op jit(solution)/shard_map/ppermute | solution.py:28
  195.5 30.5 %collective-permute-start.34 = (f32[1,18,66]{2,1,0:T(8,128)S(1)}, f32[1,18,66]{2,1,0:T(8,128)S(1)}, u32[]{:S(2)}, u32[]{:S(2)}) collective-permute-start(f32[1,18,66]{2,1,0:T(8,128)S(1)} %get-tuple-element.279), channel_id=1, source_target_pairs={{0,1},{1,2},{2,3},{3,4},{4,5},{5,6},{6,7},{8,9},{9,10},{10,11},{11... | collective-permute-start | bytes 14264 | tf_op jit(solution)/shard_map/ppermute | solution.py:25
  197.9 28.1 %collective-permute-start.35 = (f32[1,18,66]{2,1,0:T(8,128)S(1)}, f32[1,18,66]{2,1,0:T(8,128)S(1)}, u32[]{:S(2)}, u32[]{:S(2)}) collective-permute-start(f32[1,18,66]{2,1,0:T(8,128)S(1)} %get-tuple-element.278), channel_id=1, source_target_pairs={{1,0},{2,1},{3,2},{4,3},{5,4},{6,5},{7,6},{9,8},{10,9},{11,10},{12... | collective-permute-start | bytes 14264 | tf_op jit(solution)/shard_map/ppermute | solution.py:28
  255.4 11.3 %collective-permute-start.45 = (f32[8,18,1]{2,1,0:T(8,128)S(1)}, f32[8,18,1]{2,1,0:T(8,128)S(1)}, u32[]{:S(2)}, u32[]{:S(2)}) collective-permute-start(f32[8,18,1]{2,1,0:T(8,128)S(1)} %get-tuple-element.313), channel_id=1, source_target_pairs={{8,0},{16,8},{24,16},{9,1},{17,9},{25,17},{10,2},{18,10},{26,18},{... | collective-permute-start | bytes 1736 | tf_op jit(solution)/shard_map/ppermute | solution.py:28
  275.2 11.1 %collective-permute-start.49 = (f32[8,1,64]{2,1,0:T(1,128)S(1)}, f32[8,1,64]{2,1,0:T(1,128)S(1)}, u32[]{:S(2)}, u32[]{:S(2)}) collective-permute-start(f32[8,1,64]{2,1,0:T(1,128)S(1)} %get-tuple-element.347), channel_id=1, source_target_pairs={{32,0},{64,32},{96,64},{33,1},{65,33},{97,65},{34,2},{66,34},{98,6... | collective-permute-start | bytes 6152 | tf_op jit(solution)/shard_map/ppermute | solution.py:28
  281.0 33.4 %collective-permute-start.60 = (f32[4,1,32]{2,1,0:T(1,128)S(1)}, f32[4,1,32]{2,1,0:T(1,128)S(1)}, u32[]{:S(2)}, u32[]{:S(2)}) collective-permute-start(f32[4,1,32]{2,1,0:T(1,128)S(1)} %get-tuple-element.389), channel_id=1, source_target_pairs={{0,32},{32,64},{64,96},{1,33},{33,65},{65,97},{2,34},{34,66},{66,9... | collective-permute-start | bytes 1544 | tf_op jit(solution)/shard_map/ppermute | solution.py:25
  284.7 34.7 %collective-permute-start.61 = (f32[4,1,32]{2,1,0:T(1,128)S(1)}, f32[4,1,32]{2,1,0:T(1,128)S(1)}, u32[]{:S(2)}, u32[]{:S(2)}) collective-permute-start(f32[4,1,32]{2,1,0:T(1,128)S(1)} %get-tuple-element.388), channel_id=1, source_target_pairs={{32,0},{64,32},{96,64},{33,1},{65,33},{97,65},{34,2},{66,34},{98,6... | collective-permute-start | bytes 1544 | tf_op jit(solution)/shard_map/ppermute | solution.py:28
  293.7 17.9 %collective-permute-start.53 = (f32[1,18,66]{2,1,0:T(8,128)S(1)}, f32[1,18,66]{2,1,0:T(8,128)S(1)}, u32[]{:S(2)}, u32[]{:S(2)}) collective-permute-start(f32[1,18,66]{2,1,0:T(8,128)S(1)} %get-tuple-element.273), channel_id=1, source_target_pairs={{1,0},{2,1},{3,2},{4,3},{5,4},{6,5},{7,6},{9,8},{10,9},{11,10},{12... | collective-permute-start | bytes 14264 | tf_op jit(solution)/shard_map/ppermute | solution.py:28
  295.6 17.3 %collective-permute-start.52 = (f32[1,18,66]{2,1,0:T(8,128)S(1)}, f32[1,18,66]{2,1,0:T(8,128)S(1)}, u32[]{:S(2)}, u32[]{:S(2)}) collective-permute-start(f32[1,18,66]{2,1,0:T(8,128)S(1)} %get-tuple-element.272), channel_id=1, source_target_pairs={{0,1},{1,2},{2,3},{3,4},{4,5},{5,6},{6,7},{8,9},{9,10},{10,11},{11... | collective-permute-start | bytes 14264 | tf_op jit(solution)/shard_map/ppermute | solution.py:25
  301.8 174.2 %collective-permute-start.90 = (f32[2,1,16]{2,1,0:T(1,128)}, f32[2,1,16]{2,1,0:T(1,128)S(1)}, u32[]{:S(2)}, u32[]{:S(2)}) collective-permute-start(f32[2,1,16]{2,1,0:T(1,128)} %get-tuple-element.445), channel_id=1, source_target_pairs={{0,32},{32,64},{64,96},{1,33},{33,65},{65,97},{2,34},{34,66},{66,9... | collective-permute-start | bytes 392 | tf_op jit(solution)/shard_map/ppermute | solution.py:25
  311.6 164.4 %collective-permute-start.91 = (f32[2,1,16]{2,1,0:T(1,128)}, f32[2,1,16]{2,1,0:T(1,128)}, u32[]{:S(2)}, u32[]{:S(2)}) collective-permute-start(f32[2,1,16]{2,1,0:T(1,128)} %get-tuple-element.444), channel_id=1, source_target_pairs={{32,0},{64,32},{96,64},{33,1},{65,33},{97,65},{34,2},{66,34},{98,6... | collective-permute-start | bytes 392 | tf_op jit(solution)/shard_map/ppermute | solution.py:28
  364.8 25.9 %collective-permute-start.71 = (f32[1,10,34]{2,1,0:T(8,128)S(1)}, f32[1,10,34]{2,1,0:T(8,128)S(1)}, u32[]{:S(2)}, u32[]{:S(2)}) collective-permute-start(f32[1,10,34]{2,1,0:T(8,128)S(1)} %get-tuple-element.333), channel_id=1, source_target_pairs={{1,0},{2,1},{3,2},{4,3},{5,4},{6,5},{7,6},{9,8},{10,9},{11,10},{12... | collective-permute-start | bytes 4088 | tf_op jit(solution)/shard_map/ppermute | solution.py:28
  367.2 23.5 %collective-permute-start.70 = (f32[1,10,34]{2,1,0:T(8,128)S(1)}, f32[1,10,34]{2,1,0:T(8,128)S(1)}, u32[]{:S(2)}, u32[]{:S(2)}) collective-permute-start(f32[1,10,34]{2,1,0:T(8,128)S(1)} %get-tuple-element.332), channel_id=1, source_target_pairs={{0,1},{1,2},{2,3},{3,4},{4,5},{5,6},{6,7},{8,9},{9,10},{10,11},{11... | collective-permute-start | bytes 4088 | tf_op jit(solution)/shard_map/ppermute | solution.py:25
  390.8 30.3 %collective-permute-start.73 = (f32[4,1,32]{2,1,0:T(1,128)S(1)}, f32[4,1,32]{2,1,0:T(1,128)S(1)}, u32[]{:S(2)}, u32[]{:S(2)}) collective-permute-start(f32[4,1,32]{2,1,0:T(1,128)S(1)} %get-tuple-element.385), channel_id=1, source_target_pairs={{32,0},{64,32},{96,64},{33,1},{65,33},{97,65},{34,2},{66,34},{98,6... | collective-permute-start | bytes 1544 | tf_op jit(solution)/shard_map/ppermute | solution.py:28
  392.1 29.0 %collective-permute-start.72 = (f32[4,1,32]{2,1,0:T(1,128)S(1)}, f32[4,1,32]{2,1,0:T(1,128)S(1)}, u32[]{:S(2)}, u32[]{:S(2)}) collective-permute-start(f32[4,1,32]{2,1,0:T(1,128)S(1)} %get-tuple-element.384), channel_id=1, source_target_pairs={{0,32},{32,64},{64,96},{1,33},{33,65},{65,97},{2,34},{34,66},{66,9... | collective-permute-start | bytes 1544 | tf_op jit(solution)/shard_map/ppermute | solution.py:25
  421.2 14.7 %collective-permute-start.75 = (f32[4,10,1]{2,1,0:T(8,128)S(1)}, f32[4,10,1]{2,1,0:T(8,128)S(1)}, u32[]{:S(2)}, u32[]{:S(2)}) collective-permute-start(f32[4,10,1]{2,1,0:T(8,128)S(1)} %get-tuple-element.367), channel_id=1, source_target_pairs={{8,0},{16,8},{24,16},{9,1},{17,9},{25,17},{10,2},{18,10},{26,18},{... | collective-permute-start | bytes 488 | tf_op jit(solution)/shard_map/ppermute | solution.py:28
  422.5 13.4 %collective-permute-start.74 = (f32[4,10,1]{2,1,0:T(8,128)S(1)}, f32[4,10,1]{2,1,0:T(8,128)S(1)}, u32[]{:S(2)}, u32[]{:S(2)}) collective-permute-start(f32[4,10,1]{2,1,0:T(8,128)S(1)} %get-tuple-element.366), channel_id=1, source_target_pairs={{0,8},{8,16},{16,24},{1,9},{9,17},{17,25},{2,10},{10,18},{18,26},{... | collective-permute-start | bytes 488 | tf_op jit(solution)/shard_map/ppermute | solution.py:25
  436.0 17.9 %collective-permute-start.77 = (f32[1,10,34]{2,1,0:T(8,128)S(1)}, f32[1,10,34]{2,1,0:T(8,128)S(1)}, u32[]{:S(2)}, u32[]{:S(2)}) collective-permute-start(f32[1,10,34]{2,1,0:T(8,128)S(1)} %get-tuple-element.331), channel_id=1, source_target_pairs={{1,0},{2,1},{3,2},{4,3},{5,4},{6,5},{7,6},{9,8},{10,9},{11,10},{12... | collective-permute-start | bytes 4088 | tf_op jit(solution)/shard_map/ppermute | solution.py:28
  441.3 12.6 %collective-permute-start.76 = (f32[1,10,34]{2,1,0:T(8,128)S(1)}, f32[1,10,34]{2,1,0:T(8,128)S(1)}, u32[]{:S(2)}, u32[]{:S(2)}) collective-permute-start(f32[1,10,34]{2,1,0:T(8,128)S(1)} %get-tuple-element.330), channel_id=1, source_target_pairs={{0,1},{1,2},{2,3},{3,4},{4,5},{5,6},{6,7},{8,9},{9,10},{10,11},{11... | collective-permute-start | bytes 4088 | tf_op jit(solution)/shard_map/ppermute | solution.py:25
  476.9 11.8 %collective-permute-start.85 = (f32[4,1,32]{2,1,0:T(1,128)S(1)}, f32[4,1,32]{2,1,0:T(1,128)S(1)}, u32[]{:S(2)}, u32[]{:S(2)}) collective-permute-start(f32[4,1,32]{2,1,0:T(1,128)S(1)} %get-tuple-element.381), channel_id=1, source_target_pairs={{32,0},{64,32},{96,64},{33,1},{65,33},{97,65},{34,2},{66,34},{98,6... | collective-permute-start | bytes 1544 | tf_op jit(solution)/shard_map/ppermute | solution.py:28
  478.2 10.5 collective-permute-start.84
  482.8 11.3 %collective-permute-start.93 = (f32[2,6,1]{2,1,0:T(8,128)S(1)}, f32[2,6,1]{2,1,0:T(8,128)S(1)}, u32[]{:S(2)}, u32[]{:S(2)}) collective-permute-start(f32[2,6,1]{2,1,0:T(8,128)S(1)} %get-tuple-element.425), channel_id=1, source_target_pairs={{8,0},{16,8},{24,16},{9,1},{17,9},{25,17},{10,2},{18,10},{26,18},{... | collective-permute-start | bytes 152 | tf_op jit(solution)/shard_map/ppermute | solution.py:28
  495.2 13.3 %collective-permute-start.89 = (f32[1,10,34]{2,1,0:T(8,128)S(1)}, f32[1,10,34]{2,1,0:T(8,128)S(1)}, u32[]{:S(2)}, u32[]{:S(2)}) collective-permute-start(f32[1,10,34]{2,1,0:T(8,128)S(1)} %get-tuple-element.327), channel_id=1, source_target_pairs={{1,0},{2,1},{3,2},{4,3},{5,4},{6,5},{7,6},{9,8},{10,9},{11,10},{12... | collective-permute-start | bytes 4088 | tf_op jit(solution)/shard_map/ppermute | solution.py:28
  497.7 10.8 %collective-permute-start.88 = (f32[1,10,34]{2,1,0:T(8,128)S(1)}, f32[1,10,34]{2,1,0:T(8,128)S(1)}, u32[]{:S(2)}, u32[]{:S(2)}) collective-permute-start(f32[1,10,34]{2,1,0:T(8,128)S(1)} %get-tuple-element.326), channel_id=1, source_target_pairs={{0,1},{1,2},{2,3},{3,4},{4,5},{5,6},{6,7},{8,9},{9,10},{10,11},{11... | collective-permute-start | bytes 4088 | tf_op jit(solution)/shard_map/ppermute | solution.py:25
  545.8 10.8 %collective-permute-start.107 = (f32[1,6,18]{2,1,0:T(8,128)S(1)}, f32[1,6,18]{2,1,0:T(8,128)S(1)}, u32[]{:S(2)}, u32[]{:S(2)}) collective-permute-start(f32[1,6,18]{2,1,0:T(8,128)S(1)} %get-tuple-element.415), channel_id=1, source_target_pairs={{1,0},{2,1},{3,2},{4,3},{5,4},{6,5},{7,6},{9,8},{10,9},{11,10},{12... | collective-permute-start | bytes 1304 | tf_op jit(solution)/shard_map/ppermute | solution.py:28
  650.3 11.3 %collective-permute-start.125 = (f32[1,6,18]{2,1,0:T(8,128)S(1)}, f32[1,6,18]{2,1,0:T(8,128)S(1)}, u32[]{:S(2)}, u32[]{:S(2)}) collective-permute-start(f32[1,6,18]{2,1,0:T(8,128)S(1)} %get-tuple-element.403), channel_id=1, source_target_pairs={{1,0},{2,1},{3,2},{4,3},{5,4},{6,5},{7,6},{9,8},{10,9},{11,10},{12... | collective-permute-start | bytes 1304 | tf_op jit(solution)/shard_map/ppermute | solution.py:28
  997.3 10.7 collective-permute-start.207
  998.6 11.1 %collective-permute-start.206 = (f32[16,34,1]{2,1,0:T(8,128)S(1)}, f32[16,34,1]{2,1,0:T(8,128)S(1)}, u32[]{:S(2)}, u32[]{:S(2)}) collective-permute-start(f32[16,34,1]{2,1,0:T(8,128)S(1)} %get-tuple-element.246), channel_id=1, source_target_pairs={{0,8},{8,16},{16,24},{1,9},{9,17},{17,25},{2,10},{10,18},{18,26},{... | collective-permute-start | bytes 6536 | tf_op jit(solution)/shard_map/ppermute | solution.py:25
  1023.9 11.4 %collective-permute-start.213 = (f32[16,34,1]{2,1,0:T(8,128)S(1)}, f32[16,34,1]{2,1,0:T(8,128)S(1)}, u32[]{:S(2)}, u32[]{:S(2)}) collective-permute-start(f32[16,34,1]{2,1,0:T(8,128)S(1)} %get-tuple-element.245), channel_id=1, source_target_pairs={{8,0},{16,8},{24,16},{9,1},{17,9},{25,17},{10,2},{18,10},{26,18},{... | collective-permute-start | bytes 6536 | tf_op jit(solution)/shard_map/ppermute | solution.py:28
  1025.2 11.8 %collective-permute-start.212 = (f32[16,34,1]{2,1,0:T(8,128)S(1)}, f32[16,34,1]{2,1,0:T(8,128)S(1)}, u32[]{:S(2)}, u32[]{:S(2)}) collective-permute-start(f32[16,34,1]{2,1,0:T(8,128)S(1)} %get-tuple-element.244), channel_id=1, source_target_pairs={{0,8},{8,16},{16,24},{1,9},{9,17},{17,25},{2,10},{10,18},{18,26},{... | collective-permute-start | bytes 6536 | tf_op jit(solution)/shard_map/ppermute | solution.py:25
  1051.4 12.1 %collective-permute-start.219 = (f32[16,34,1]{2,1,0:T(8,128)S(1)}, f32[16,34,1]{2,1,0:T(8,128)S(1)}, u32[]{:S(2)}, u32[]{:S(2)}) collective-permute-start(f32[16,34,1]{2,1,0:T(8,128)S(1)} %get-tuple-element.243), channel_id=1, source_target_pairs={{8,0},{16,8},{24,16},{9,1},{17,9},{25,17},{10,2},{18,10},{26,18},{... | collective-permute-start | bytes 6536 | tf_op jit(solution)/shard_map/ppermute | solution.py:28
  1052.7 11.8 %collective-permute-start.218 = (f32[16,34,1]{2,1,0:T(8,128)S(1)}, f32[16,34,1]{2,1,0:T(8,128)S(1)}, u32[]{:S(2)}, u32[]{:S(2)}) collective-permute-start(f32[16,34,1]{2,1,0:T(8,128)S(1)} %get-tuple-element.242), channel_id=1, source_target_pairs={{0,8},{8,16},{16,24},{1,9},{9,17},{17,25},{2,10},{10,18},{18,26},{... | collective-permute-start | bytes 6536 | tf_op jit(solution)/shard_map/ppermute | solution.py:25
  (181 other events, 2492.5 us)
where the time goes:
time: 1090 us; the launch traced here: 1070 us
  starting transfers between devices  686 us (63%)
  waiting for transfers between devices  127 us (12%)
  local copies, waits for them, and re-layouts  103 us (9%)
  blocking collectives  94.2 us (9%)
  other arithmetic  57.3 us (5%)
    ppermute x111, starting transfers between devices, padded_2(): lax.ppermute(lax.slice_in_dim(block, block.shape[dim] - width, None, axis...  496 us
    ppermute x111, starting transfers between devices, padded_2(): lax.ppermute(lax.slice_in_dim(block, 0, width, axis=dim), axis, backward)  190 us
    ppermute x111, waiting for transfers between devices, padded_2(): lax.ppermute(lax.slice_in_dim(block, block.shape[dim] - width, None, axis...  75.1 us
    reshape x7, local copies, waits for them, and re-layouts, fold_cells(): values.reshape(height // 2, 2, across // 2, 2, along // 2, 2)  62.4 us
    ppermute x111, waiting for transfers between devices, padded_2(): lax.ppermute(lax.slice_in_dim(block, 0, width, axis=dim), axis, backward)  51.6 us
    reduce_sum x18, other arithmetic, fold_cells(): values.reshape(height // 2, 2, across // 2, 2, along // 2, 2)  30.5 us
  transfers between devices with their start and end apart: 222, of which 100 were waited for; matrix products, arithmetic and copies ran while one was open for 10% of the time, Pallas kernels for 0%

commit v1 on v0

v1 whole, which is shorter than its diff:
```python
import math

import jax
import jax.numpy as jnp
from jax import lax
from jax.experimental import pallas as pl
from jax.experimental.pallas import tpu as pltpu
from jax.sharding import PartitionSpec as P

CSWEEPS = 32
DAMP = 0.8
KEEP = 1.0 - DAMP
W0 = 5
W1 = 7
G1 = 6
S1, F1 = 11, 10
Z0, X0, Y0 = 16, 32, 128
Z1, X1, Y1 = 8, 16, 64
ZT0, XT0 = Z0 + 2 * W0, 48
ZT1, XT1 = Z1 + 2 * W1, 40
LANES = 128
MIB = 1024 * 1024
F32 = jnp.float32


def lane_of(shape):
    return lax.broadcasted_iota(jnp.int32, shape, len(shape) - 1)


def row_of(shape):
    return lax.broadcasted_iota(jnp.int32, shape, len(shape) - 2)


def roll(x, shift, axis):
    size = x.shape[axis]
    shift = shift % size
    return x if shift == 0 else pltpu.roll(x, shift, axis)


def loop(first, last, body, step):
    chunks = (last - first) // step

    def chunk(c, carry):
        for k in range(step):
            body(first + c * step + k)
        return carry

    if chunks > 1:
        lax.fori_loop(0, chunks, chunk, 0)
    elif chunks:
        chunk(0, 0)
    for z in range(first + chunks * step, last):
        body(z)


def pick(x, index):
    return jnp.take_along_axis(x, index, axis=1)


def fold_lanes(x, first, count, target):
    to = lane_of(x.shape) - target
    index = (first + 2 * to) % LANES
    pairs = pick(x, index) + pick(x, (index + 1) % LANES)
    return jnp.where((to >= 0) & (to < count // 2), pairs, 0.0)


def spread_lanes(x, first=0):
    return pick(x, first + lane_of(x.shape) // 2)


class Far:
    def __init__(self, ins, outs, late):
        self.ins = {k: pltpu.make_async_copy(*pair) for k, pair in ins.items()}
        self.outs = {k: pltpu.make_async_copy(*pair) for k, pair in outs.items()}
        self.started = []
        self.start(*[k for k in self.ins if k not in late])

    def start(self, *keys):
        for k in keys:
            self.ins[k].start()

    def wait(self, *keys):
        for k in keys or tuple(self.ins):
            self.ins.pop(k).wait()

    def flush(self, *keys):
        for k in keys:
            self.outs[k].start()
            self.started.append(k)

    def finish(self):
        self.flush(*[k for k in self.outs if k not in self.started])
        for copy in self.outs.values():
            copy.wait()


def padded(shape):
    plane = 4 * math.prod(shape[1:])
    return (max(shape[0], -(-7 * MIB // plane)), *shape[1:])


def call(body, outs, scratch, *args, place=None, far_in={}, far_out=(), late=(), grant=48):
    shapes = [
        jax.ShapeDtypeStruct(padded(shape) if k in far_out else shape, F32)
        for k, shape in enumerate(outs)
    ]
    vmem = pl.BlockSpec(memory_space=pltpu.VMEM)
    hbm = pl.BlockSpec(memory_space=pltpu.HBM)
    specs = [hbm if k in far_in else vmem for k in range(len(args))]
    out_specs = [hbm if k in far_out else vmem for k in range(len(outs))]
    held = [pltpu.VMEM(shape, F32) for shape in far_in.values()]
    held += [pltpu.VMEM(outs[k], F32) for k in far_out]
    extra = len(far_in) + len(far_out)
    if extra:
        held.append(pltpu.SemaphoreType.DMA((extra,)))
    placed = place is not None
    count = len(args)

    def wrapped(*refs):
        refs = list(refs)
        head = [refs.pop(0)] if placed else []
        ins, results = refs[:count], refs[count : count + len(outs)]
        rest = refs[count + len(outs) :]
        mine, rest = rest[: len(scratch)], rest[len(scratch) :]
        copies_in, copies_out = {}, {}
        for j, k in enumerate(far_in):
            copies_in[k] = (ins[k].at[0 : far_in[k][0]], rest[j], rest[extra].at[j])
            ins[k] = rest[j]
        for j, k in enumerate(far_out, len(far_in)):
            copies_out[k] = (rest[j], results[k].at[0 : outs[k][0]], rest[extra].at[j])
            results[k] = rest[j]
        far = Far(copies_in, copies_out, late)
        body(far, *head, *ins, *results, *mine)
        far.finish()

    if placed:
        specs = [pl.BlockSpec(memory_space=pltpu.SMEM)] + specs
        args = (place,) + args
    return pl.pallas_call(
        wrapped,
        out_shape=shapes,
        in_specs=specs,
        out_specs=out_specs,
        scratch_shapes=[pltpu.VMEM(shape, F32) for shape in scratch] + held,
        compiler_params=pltpu.CompilerParams(vmem_limit_bytes=grant * MIB),
    )(*args)


class Item:
    def __init__(self, fields, planes, rows, rows_out, width, kind, trim=False, width_z=None, edge=0):
        self.n, self.z, self.x, self.xt, self.w, self.kind = fields, planes, rows, rows_out, width, kind
        self.wz = width if width_z is None else width_z
        self.zt = planes + 2 * self.wz
        self.edge = edge
        self.trim = trim
        self.tall = rows + 8 if trim else rows_out
        self.virtual = 2 * fields if kind == "pair" else fields
        self.own = LANES if kind == "full" else LANES // 2
        self.slots = LANES // width
        self.groups = -(-self.virtual * (self.zt - 2 * edge) // self.slots)
        self.rows_x = fields * planes * width
        self.rows_z = fields * self.wz * self.tall
        self.rows_y = self.groups * self.tall

    def narrow(self, plane):
        if not self.trim:
            return plane
        upper, lower = plane[self.x : self.x + 8], plane[self.xt - 8 : self.xt]
        rim = jnp.where(row_of(upper.shape) < 4, upper, lower)
        return jnp.concatenate([plane[: self.x], rim], axis=0)

    def widen(self, plane):
        if not self.trim:
            return plane
        rim = plane[self.x :]
        upper = jnp.where(row_of(rim.shape) < 4, rim, 0.0)
        return jnp.concatenate([plane[: self.x], upper, rim - upper], axis=0)


def total(counts):
    count = sum(counts)
    return -(-count // 8) * 8


def pack_x(items, refs, low, high):
    at = 0
    for item, ref in zip(items, refs):
        for n in range(item.n):
            for z in range(item.z):
                low[at : at + item.w, :] = ref[n, z, 0 : item.w, :]
                high[at : at + item.w, :] = ref[n, z, item.x - item.w : item.x, :]
                at += item.w


def unpack_x(items, refs, from_low, from_high, outs):
    at = 0
    for item, ref, out in zip(items, refs, outs):
        out[:, :, item.x :, :] = jnp.zeros((item.n, item.z, item.xt - item.x, LANES), F32)
        for n in range(item.n):
            for z in range(item.z):
                out[n, z, 0 : item.x, :] = ref[n, z]
                out[n, z, item.x : item.x + item.w, :] = from_high[at : at + item.w, :]
                out[n, z, item.xt - item.w :, :] = from_low[at : at + item.w, :]
                at += item.w


def pack_z(items, refs, low, high):
    at = 0
    for item, ref in zip(items, refs):
        for n in range(item.n):
            for w in range(item.wz):
                low[at : at + item.tall, :] = item.narrow(ref[n, w])
                high[at : at + item.tall, :] = item.narrow(ref[n, item.z - item.wz + w])
                at += item.tall


def unpack_z(items, refs, from_low, from_high, outs):
    at = 0
    for item, ref, out in zip(items, refs, outs):
        for n in range(item.n):
            for w in range(item.wz):
                out[n, w] = item.widen(from_low[at : at + item.tall, :])
                out[n, item.wz + item.z + w] = item.widen(from_high[at : at + item.tall, :])
                at += item.tall
            for z in range(item.z):
                out[n, item.wz + z] = ref[n, z]


def pack_y(items, refs, low, high):
    at = 0
    for item, ref in zip(items, refs):
        lane = lane_of((item.tall, LANES))
        pairs = [(v, z) for v in range(item.virtual) for z in range(item.edge, item.zt - item.edge)]
        for g in range(item.groups):
            lows = jnp.zeros((item.tall, LANES), F32)
            highs = lows
            for k, (v, z) in enumerate(pairs[g * item.slots : (g + 1) * item.slots]):
                n, first = (v // 2, (v % 2) * item.own) if item.kind == "pair" else (v, 0)
                plane = item.narrow(ref[n, z])
                place = k * item.w
                mask = (lane >= place) & (lane < place + item.w)
                lows = jnp.where(mask, roll(plane, place - first, 1), lows)
                highs = jnp.where(mask, roll(plane, place - first - item.own + item.w, 1), highs)
            low[at : at + item.tall, :] = lows
            high[at : at + item.tall, :] = highs
            at += item.tall


def unpack_y(items, refs, from_low, from_high, outs):
    at = 0
    for item, ref, fields in zip(items, refs, outs):
        lane = lane_of((item.tall, LANES))
        for v in range(item.virtual if item.edge else 0):
            for z in [*range(item.edge), *range(item.zt - item.edge, item.zt)]:
                fields[v][z, :, 0:LANES] = ref[v, z]
                fields[v][z, :, LANES:] = jnp.zeros((item.xt, LANES), F32)
        pairs = [(v, z) for v in range(item.virtual) for z in range(item.edge, item.zt - item.edge)]
        for g in range(item.groups):
            lows = from_low[at : at + item.tall, :]
            highs = from_high[at : at + item.tall, :]
            at += item.tall
            for k, (v, z) in enumerate(pairs[g * item.slots : (g + 1) * item.slots]):
                place = k * item.w
                start = item.own % LANES
                upper = roll(highs, start - place, 1)
                lower = roll(lows, LANES - item.w - place, 1)
                rim = jnp.where(
                    lane < start + item.w, upper, jnp.where(lane >= LANES - item.w, lower, 0.0)
                )
                if item.kind == "full":
                    fields[v][z, :, 0:LANES] = ref[v, z]
                    fields[v][z, :, LANES:] = item.widen(rim)
                else:
                    plane = ref[v // 2, z] if item.kind == "pair" else ref[v, z]
                    if item.kind == "pair" and v % 2:
                        plane = roll(plane, item.own, 1)
                    fields[v][z] = jnp.where(lane < item.own, plane, rim)


def shift(low, high, axis):
    count = lax.axis_size(axis)
    forward = [(i, i + 1) for i in range(count - 1)]
    backward = [(target, source) for source, target in forward]
    return lax.ppermute(high, axis, forward), lax.ppermute(low, axis, backward)


def exchange(items, arrays, low, high):
    count = len(items)
    from_low, from_high = shift(low, high, "gx")
    shapes = [(item.n, item.z, item.xt, LANES) for item in items]
    message = (total(item.rows_z for item in items), LANES)

    def after_x(far, *refs):
        ins, (a, b), outs, (c, d) = refs[:count], refs[count : count + 2], refs[count + 2 : 2 * count + 2], refs[2 * count + 2 :]
        unpack_x(items, ins, a, b, outs)
        pack_z(items, outs, c, d)

    *arrays, low, high = call(after_x, shapes + [message] * 2, [], *arrays, from_low, from_high)
    from_low, from_high = shift(low, high, "gz")
    shapes = [(item.n, item.zt, item.xt, LANES) for item in items]
    message = (total(item.rows_y for item in items), LANES)

    def after_z(far, *refs):
        ins, (a, b), outs, (c, d) = refs[:count], refs[count : count + 2], refs[count + 2 : 2 * count + 2], refs[2 * count + 2 :]
        unpack_z(items, ins, a, b, outs)
        pack_y(items, outs, c, d)

    *arrays, low, high = call(after_z, shapes + [message] * 2, [], *arrays, from_low, from_high)
    from_low, from_high = shift(low, high, "gy")
    return arrays, from_low, from_high


STIFFNESS = Item(1, Z0, X0, XT0, W0, "full", True, edge=1)
INNER = Item(1, Z0, X0, XT0, W0 - 1, "full", True)
COARSE = Item(1, Z1, X1, XT1, S1, "pair", False, W1)
FORCING1 = Item(1, Z1, X1, XT1, F1, "half", False, G1)
POTENTIAL0 = Item(1, Z0, X0, XT0, W0, "full", False, 0)
FIRST, SECOND = (STIFFNESS, INNER, INNER, COARSE), (FORCING1, POTENTIAL0)


def x_message(items):
    return (total(item.rows_x for item in items), LANES)


def couple(s, m, r, cx, cy, cz, first, last, step, edges=False, start=None):
    planes, rows, lanes = s.shape

    def vertical(z):
        return 4.0 * jnp.minimum(s[z], s[z + 1])

    def one(z, below, above):
        here = s[z]
        x_face = jnp.minimum(here, roll(here, -1, 0))
        y_face = jnp.minimum(here, roll(here, -1, 1))
        if edges:
            x_face = jnp.where(row_of(here.shape) < rows - 1, x_face, 0.0)
            y_face = jnp.where(lane_of(here.shape) < lanes - 1, y_face, 0.0)
        cx[z] = x_face
        cy[z] = y_face
        cz[z] = above
        d = m[z] + below + above + x_face + roll(x_face, 1, 0) + y_face + roll(y_face, 1, 1)
        scale = DAMP / jnp.where(d > 0.0, d, 1.0)
        r[z] = scale
        if start:
            start[1][z] = scale * start[0][z]

    if edges:
        zero = jnp.zeros((rows, lanes), F32)
        one(0, zero, vertical(0))
        one(planes - 1, vertical(planes - 2), zero)
    else:
        cz[first - 1] = vertical(first - 1)
    loop(first + edges, last - edges, lambda z: one(z, vertical(z - 1), vertical(z)), step)


def gathered(v, f, cx, cy, cz, z, low=True, high=True):
    here = v[z]
    x_face, y_face = cx[z], cy[z]
    out = f[z]
    if high:
        out = out + cz[z] * v[z + 1]
    if low:
        out = out + cz[z - 1] * v[z - 1]
    out = out + x_face * roll(here, -1, 0) + roll(x_face * here, 1, 0)
    return here, out + y_face * roll(here, -1, 1) + roll(y_face * here, 1, 1)


def sweep(v, into, op, first, last, unroll, edges=False):
    r, f, cx, cy, cz = op

    def step(z, low=True, high=True):
        here, out = gathered(v, f, cx, cy, cz, z, low, high)
        into[z] = KEEP * here + r[z] * out

    if edges:
        step(first, low=False)
        step(last - 1, high=False)
        loop(first + 1, last - 1, step, unroll)
    else:
        loop(first, last, step, unroll)


def remain(v, op, z, low=True, high=True):
    r, f, cx, cy, cz = op
    here, out = gathered(v, f, cx, cy, cz, z, low, high)
    return out - here * (DAMP / r[z])


def first_sweep(v, op, first, last):
    r, f = op[:2]

    def step(z):
        v[z] = r[z] * f[z]

    loop(first, last, step, 4)


def prepare(far, stiffness, forcing, mass, coarse, low, high, tall):
    out = None
    for ref, scale, target in ((stiffness, 0.25, 0), (mass, 1.0, Y1)):
        for z in range(Z1):
            tall[z * X0 : (z + 1) * X0, :] = ref[0, 2 * z] + ref[0, 2 * z + 1]
        rows = tall[pl.ds(0, Z1 * X1, stride=2), :] + tall[pl.ds(1, Z1 * X1, stride=2), :]
        part = scale * fold_lanes(rows, 0, LANES, target)
        out = part if out is None else out + part
    for z in range(Z1):
        coarse[0, z] = out[z * X1 : (z + 1) * X1, :]
    pack_x(FIRST, (stiffness, forcing, mass, coarse), low, high)


def prepare_coarse(far, coarse, packed2, tall):
    for part, scale in ((0, 0.25), (1, 1.0)):
        packed2[part * 8 : part * 8 + 8, :] = scale * pack_coarse(
            lambda z: coarse[0, z], part * Y1, tall
        )


def pack_coarse(plane, first, tall):
    for z in range(Z1 // 2):
        tall[z * X1 : (z + 1) * X1, :] = plane(2 * z) + plane(2 * z + 1)
    count = Z1 // 2 * X1 // 2
    rows = tall[pl.ds(0, count, stride=2), :] + tall[pl.ds(1, count, stride=2), :]
    out = jnp.zeros((X1 // 2, LANES), F32)
    for z in range(Z1 // 2):
        part = rows[z * X1 // 2 : (z + 1) * X1 // 2, :]
        out = out + fold_lanes(part, first, Y1, z * Y1 // 2)
    return out


def parts(ref, planes, count=5):
    return [ref.at[k * planes : (k + 1) * planes] for k in range(count)]


def presmooth0(
    far, zx_s, zx_f, zx_m, zx_coarse, from_low, from_high,
    v_own, g_own, op, s1, m1, low, high,
    s, m, va, vb, tall,
):
    r, f, cx, cy, cz = parts(op, ZT0)
    inner = slice(1, ZT0 - 1)
    unpack_y(
        FIRST, (zx_s, zx_f, zx_m, zx_coarse), from_low, from_high,
        ([s], [f.at[inner]], [m.at[inner]], [s1, m1]),
    )
    couple(s, m, r, cx, cy, cz, 1, ZT0 - 1, 4, start=(f, va))
    far.flush(2)
    op = (r, f, cx, cy, cz)
    sweep(va, vb, op, 2, ZT0 - 2, 4)
    sweep(vb, va, op, 3, ZT0 - 3, 4)
    sweep(va, vb, op, 4, ZT0 - 4, 4)
    for z in range(Z1):
        a, b = W0 + 2 * z, W0 + 2 * z + 1
        plane = remain(vb, op, a) + remain(vb, op, b)
        tall[z * X0 : (z + 1) * X0, :] = plane[0:X0, 0:Y0]
    rows = tall[pl.ds(0, Z1 * X1, stride=2), :] + tall[pl.ds(1, Z1 * X1, stride=2), :]
    out = fold_lanes(rows, 0, LANES, 0)
    for z in range(Z1):
        g_own[0, z] = out[z * X1 : (z + 1) * X1, :]
    for z in range(Z0):
        v_own[0, z] = vb[W0 + z, 0:X0, 0:Y0]
    pack_x(SECOND, (g_own, v_own), low, high)


def presmooth1(
    far, g_zx, v0_zx, s, m, from_low, from_high,
    v_own, v0, copies, op, low, high,
    va, vb, tall,
):
    r, g, cx, cy, cz = parts(op, ZT1)
    for k in range(W1 - G1):
        g[k] = jnp.zeros((XT1, LANES), F32)
        g[ZT1 - 1 - k] = jnp.zeros((XT1, LANES), F32)
    inner = g.at[W1 - G1 : ZT1 - (W1 - G1)]
    unpack_y(SECOND, (g_zx, v0_zx), from_low, from_high, ([inner], [v0]))
    couple(s, m, r, cx, cy, cz, 1, ZT1 - 1, 10, start=(g, va))
    far.flush(3)
    op = (r, g, cx, cy, cz)
    sweep(va, vb, op, 4, ZT1 - 4, 10)
    sweep(vb, va, op, 5, ZT1 - 5, 10)
    sweep(va, vb, op, 6, ZT1 - 6, 10)
    packed = pack_coarse(lambda z: remain(vb, op, W1 + z)[0:X1, :], 0, tall)
    for d in range(copies.shape[0]):
        copies[d] = packed
    for z in range(Z1):
        v_own[z] = vb[W1 + z]
    lane = lane_of((XT0, LANES))
    base = (W0 + 1) * XT0
    for message, first0, first1 in ((low, 0, 0), (high, Z0 - W0, Z1 - W1)):
        rims = jnp.zeros((XT0, LANES), F32)
        for w in range(W0):
            message[w * XT0 : (w + 1) * XT0, :] = v0[first0 + w, :, 0:LANES]
            here = (lane >= 2 * W0 * w) & (lane < 2 * W0 * (w + 1))
            rims = jnp.where(here, roll(v0[first0 + w, :, LANES:], W0 + 2 * W0 * w, 1), rims)
        message[W0 * XT0 : base, :] = rims
        for w in range(W1):
            message[base + w * XT1 : base + (w + 1) * XT1, :] = v_own[first1 + w]


def unpack_whole(blocks, first, out):
    group = lane_of((8, LANES)) // 32

    def body(step):
        gz, gx = step // 4, step % 4
        for z in range(4):
            plane = None
            for gy in range(4):
                block = blocks[step * 4 + gy, first : first + 8, :]
                moved = roll(block, (gy - z) * 32, 1)
                plane = moved if plane is None else jnp.where(group == gy, moved, plane)
            out[gz * 4 + z, pl.ds(pl.multiple_of(gx * 8, 8), 8), :] = plane

    loop(0, 32, body, 4)


def fold_whole(plane, planes, rows, scale, tall, out):
    half = rows // 2
    for z in range(planes // 2):
        tall[z * rows : (z + 1) * rows, :] = plane(2 * z) + plane(2 * z + 1)
    count = planes // 2 * half
    folded = tall[pl.ds(0, count, stride=2), :] + tall[pl.ds(1, count, stride=2), :]
    folded = scale * fold_lanes(folded, 0, LANES, 0)
    for z in range(planes // 2):
        out[z] = folded[z * half : (z + 1) * half, :]


def spread_whole(v, planes, rows, tall, add):
    count = planes * rows
    flat = spread_lanes(jnp.concatenate([v[z] for z in range(planes)], axis=0))
    tall[pl.ds(0, count, stride=2), :] = flat
    tall[pl.ds(1, count, stride=2), :] = flat
    for z in range(planes):
        spread = tall[z * 2 * rows : (z + 1) * 2 * rows, :]
        add[2 * z] = add[2 * z] + spread
        add[2 * z + 1] = add[2 * z + 1] + spread


def coarsest(out, op):
    r, f, cx, cy, cz = op
    forced, upper, lower = [], [], []
    for z in range(8):
        scale = r[z]
        forced.append(scale * f[z])
        above = scale * cz[z]
        below = scale * cz[z - 1] if z else None
        upper.append((above, scale * cx[z], scale * cy[z]))
        lower.append((below, scale * roll(cx[z], 1, 0), scale * roll(cy[z], 1, 1)))

    def step(k, v):
        new = []
        for z in range(8):
            here = v[z]
            east = upper[z][2] * roll(here, -1, 1) + lower[z][2] * roll(here, 1, 1)
            north = upper[z][1] * roll(here, -1, 0) + lower[z][1] * roll(here, 1, 0)
            base = KEEP * here + forced[z]
            if z < 7:
                base = base + upper[z][0] * v[z + 1]
            if z:
                base = base + lower[z][0] * v[z - 1]
            new.append((base + north) + east)
        return tuple(new)

    v = lax.fori_loop(0, CSWEEPS - 1, step, tuple(forced), unroll=True)
    for z in range(8):
        out[z] = v[z]


def levels(stacked):
    level3 = [stacked.at[128 + 16 * (k // 2) : 144 + 16 * (k // 2), 16 * (k % 2) : 16 * (k % 2) + 16, :] for k in range(4)]
    level4 = [stacked.at[160:168, 8 * k : 8 * k + 8, :] for k in range(4)]
    return parts(stacked, 32, 4), level3, level4


def coarse_operators(
    far, operators,
    stacked,
    s2, m2, s3, m3, s4, m4, tall,
):
    (r2, cx2, cy2, cz2), (r3, cx3, cy3, cz3), (r4, cx4, cy4, cz4) = levels(stacked)
    far.wait()
    unpack_whole(operators, 0, s2)
    unpack_whole(operators, 8, m2)
    couple(s2, m2, r2, cx2, cy2, cz2, 0, 32, 10, True)
    fold_whole(lambda z: s2[z], 32, 32, 0.25, tall, s3)
    fold_whole(lambda z: m2[z], 32, 32, 1.0, tall, m3)
    couple(s3, m3, r3, cx3, cy3, cz3, 0, 16, 14, True)
    fold_whole(lambda z: s3[z], 16, 16, 0.25, tall, s4)
    fold_whole(lambda z: m3[z], 16, 16, 1.0, tall, m4)
    couple(s4, m4, r4, cx4, cy4, cz4, 0, 8, 6, True)


def coarse_cycle(
    far, forcing, stacked, out,
    f2, vb2, f3, va3, vb3, f4, vb4, tall,
):
    unpack_whole(forcing, 0, f2)
    far.wait()
    (r2, cx2, cy2, cz2), (r3, cx3, cy3, cz3), (r4, cx4, cy4, cz4) = levels(stacked)
    op2 = (r2, f2, cx2, cy2, cz2)
    op3 = (r3, f3, cx3, cy3, cz3)
    op4 = (r4, f4, cx4, cy4, cz4)
    va2 = out

    def four(va, vb, op, planes):
        sweep(va, vb, op, 0, planes, 15, True)
        sweep(vb, va, op, 0, planes, 15, True)

    def residue(v, op, planes):
        return lambda z: remain(v, op, z, z > 0, z < planes - 1)

    first_sweep(vb2, op2, 0, 32)
    sweep(vb2, va2, op2, 0, 32, 15, True)
    four(va2, vb2, op2, 32)
    fold_whole(residue(va2, op2, 32), 32, 32, 1.0, tall, f3)
    first_sweep(vb3, op3, 0, 16)
    sweep(vb3, va3, op3, 0, 16, 15, True)
    four(va3, vb3, op3, 16)
    fold_whole(residue(va3, op3, 16), 16, 16, 1.0, tall, f4)
    coarsest(vb4, op4)
    spread_whole(vb4, 8, 8, tall, va3)
    four(va3, vb3, op3, 16)
    four(va3, vb3, op3, 16)
    spread_whole(va3, 16, 16, tall, va2)
    four(va2, vb2, op2, 32)
    four(va2, vb2, op2, 32)


def postsmooth(
    far, place, v1, v0_zx, from_low, from_high, stacked1, stacked0, correction,
    potential, residual,
    va1, vb1, v0, vb0, tall,
):
    base = (W0 + 1) * XT0
    for message, first0, first1 in ((from_low, 0, 0), (from_high, W0 + Z0, W1 + Z1)):
        rims = message[W0 * XT0 : base, :]
        for w in range(W0):
            v0[first0 + w, :, 0:LANES] = message[w * XT0 : (w + 1) * XT0, :]
            v0[first0 + w, :, LANES:] = roll(rims, -W0 - 2 * W0 * w, 1)
        for w in range(W1):
            va1[first1 + w] = message[base + w * XT1 : base + (w + 1) * XT1, :]
    for z in range(Z0):
        v0[W0 + z] = v0_zx[z]
    for z in range(Z1):
        va1[W1 + z] = v1[z]
    gz, gx, gy = place[0], place[1], place[2]
    planes = []
    for k in range(12):
        plane = correction[(gz * 4 + 28 + k) % 32]
        plane = pltpu.roll(plane, (32 - gx * 8) % 32, 0)
        plane = pltpu.roll(plane, (LANES - gy * 32) % LANES, 1)
        planes += [plane[0:14], plane[26:32]]
    flat = jnp.concatenate(planes, axis=0)
    fine = lane_of(flat.shape)
    flat = pick(flat, fine // 2 + jnp.where(fine < 96, 0, 64))
    count = 12 * 20
    tall[pl.ds(0, count, stride=2), :] = flat
    tall[pl.ds(1, count, stride=2), :] = flat
    for z in range(ZT1):
        k = (z + 1) // 2
        va1[z] = va1[z] + tall[k * XT1 : (k + 1) * XT1, :]
    far.wait(4)
    far.start(5)
    op1 = parts(stacked1, ZT1)
    sweep(va1, vb1, op1, 1, ZT1 - 1, 10)
    sweep(vb1, va1, op1, 2, ZT1 - 2, 10)
    sweep(va1, vb1, op1, 3, ZT1 - 3, 10)
    sweep(vb1, va1, op1, 4, ZT1 - 4, 10)
    planes = []
    for k in range(14):
        planes += [va1[4 + k, 0:20, :], va1[4 + k, XT1 - 4 : XT1, :]]
    flat = jnp.concatenate(planes, axis=0)
    count = 14 * 24
    for half in range(2):
        part = spread_lanes(flat, 64 * half)
        tall[pl.ds(0, count, stride=2), :] = part
        tall[pl.ds(1, count, stride=2), :] = part
        for z in range(ZT0):
            k = (z + 1) // 2
            at = slice(half * LANES, (half + 1) * LANES)
            v0[z, :, at] = v0[z, :, at] + tall[k * XT0 : (k + 1) * XT0, :]
    far.wait(5)
    op0 = parts(stacked0, ZT0)
    sweep(v0, vb0, op0, 1, ZT0 - 1, 4)
    sweep(vb0, v0, op0, 2, ZT0 - 2, 4)
    sweep(v0, vb0, op0, 3, ZT0 - 3, 4)
    sweep(vb0, v0, op0, 4, ZT0 - 4, 4)
    for z in range(Z0):
        potential[z] = v0[W0 + z, 0:X0, 0:Y0]
    for z in range(Z0):
        residual[z] = remain(v0, op0, W0 + z)[0:X0, 0:Y0]


def shards(source, conductivity, cell_kind):
    own0, own1 = (1, Z0, X0, Y0), (1, Z1, X1, LANES)
    ext0, ext1 = (ZT0, XT0, 2 * LANES), (ZT1, XT1, LANES)
    everywhere = ("gz", "gx", "gy")
    devices = math.prod(lax.axis_size(axis) for axis in everywhere)
    place = jnp.stack([lax.axis_index(axis) for axis in everywhere]).astype(jnp.int32)
    wet = jnp.where(cell_kind > 0, 1.0, 0.0).astype(F32)
    surface = jnp.where(cell_kind == 2, 1.0, 0.0).astype(F32)
    stiffness = conductivity * wet
    mass = 0.005 * stiffness + 8.0 * stiffness * surface + 0.02 * (1.0 - wet)
    fields = [array.reshape(own0) for array in (stiffness, source * wet, mass)]
    coarse, low, high = call(
        prepare, [own1] + [x_message(FIRST)] * 2, [(Z1 * X0, LANES)], *fields
    )
    (packed2,) = call(prepare_coarse, [(16, LANES)], [(Z1 // 2 * X1, LANES)], coarse)
    operators2 = lax.all_gather(packed2, everywhere, axis=0)
    arrays, from_low, from_high = exchange(FIRST, (*fields, coarse), low, high)
    v0, g1, op0, s1, m1, low, high = call(
        presmooth0,
        [own0, own1, (5 * ZT0, XT0, 2 * LANES)] + [ext1] * 2 + [x_message(SECOND)] * 2,
        [ext0] * 4 + [(Z1 * X0, LANES)],
        *arrays, from_low, from_high, far_out=(2,),
    )
    arrays, from_low, from_high = exchange(SECOND, (g1, v0), low, high)
    stack0, stack1, stack2 = (5 * ZT0, XT0, 2 * LANES), (5 * ZT1, XT1, LANES), (168, 32, LANES)
    message = ((W0 + 1) * XT0 + W1 * XT1, LANES)
    v1, v0, copies, op1, low, high = call(
        presmooth1,
        [(Z1, XT1, LANES), (Z0, XT0, 2 * LANES), (devices, 8, LANES), stack1] + [message] * 2,
        [ext1] * 2 + [(Z1 // 2 * X1, LANES)],
        arrays[0], arrays[1], s1, m1, from_low, from_high, far_out=(3,),
    )
    copies, operators2 = lax.optimization_barrier((copies, operators2))
    forcing2 = lax.all_to_all(copies, everywhere, 0, 0)
    from_low, from_high = shift(low, high, "gz")
    level2, level3, level4 = (32, 32, LANES), (16, 16, LANES), (8, 8, LANES)
    (operators,) = call(
        coarse_operators,
        [stack2],
        [level2] * 2 + [level3] * 2 + [level4] * 2 + [(512, LANES)],
        operators2, far_in={0: operators2.shape}, far_out=(0,),
    )
    (correction,) = call(
        coarse_cycle,
        [level2],
        [level2] * 2 + [level3] * 3 + [level4] * 2 + [(512, LANES)],
        forcing2, operators, far_in={1: stack2},
    )
    return call(
        postsmooth,
        [(Z0, X0, Y0)] * 2,
        [ext1, ext1, ext0, ext0, (14 * XT0, LANES)],
        v1, v0, from_low, from_high, op1, op0, correction,
        place=place, far_in={4: stack1, 5: stack0}, late=(5,),
    )


def solution(mesh):
    spec = P("gz", "gx", "gy")
    return jax.shard_map(
        shards, mesh=mesh, in_specs=(spec,) * 3, out_specs=(spec,) * 2, check_vma=False
    )
```

time: 1090 us -> 131 us (0.12); the launches traced: 1070 us -> 130 us
  starting transfers between devices: 686 us -> 45.3 us
  local copies, waits for them, and re-layouts: 103 us -> 1.23 us
  waiting for transfers between devices: 127 us -> 31.2 us
  blocking collectives: 94.2 us -> 0 us
  other arithmetic: 57.3 us -> 1.31 us
  Pallas kernels: 0 us -> 37.1 us
    ppermute x222 -> x14, starting transfers between devices: 686 us -> 39 us  [the longest x7 27.9 us: shift(): lax.ppermute(high, axis, forward)]
    ppermute x222 -> x14, waiting for transfers between devices: 127 us -> 29.8 us  [the longest x7 24.6 us: shift(): lax.ppermute(low, axis, backward)]
    all_gather x9 -> x0, blocking collectives: 94.2 us -> none  [the longest x1 13.8 us: collect(): lax.all_gather(stiffness, 'gz', axis=0, tiled=True)]
    reshape x10 -> x0, local copies, waits for them, and re-layouts: 78.4 us -> none  [the longest x7 62.4 us: fold_cells(): values.reshape(height // 2, 2, across // 2, 2, along // 2, 2)]
    pallas_call x0 -> x11, Pallas kernels: none -> 37.1 us  [call(): pl.pallas_call(wrapped, out_shape=shapes, in_specs=specs, out_specs=out_s...]
    reduce_sum x18 -> x0, other arithmetic: 30.5 us -> none  [fold_cells(): values.reshape(height // 2, 2, across // 2, 2, along // 2, 2)]
    add x65 -> x0, other arithmetic: 15.7 us -> none  [the longest x60 14.8 us: relax(): return potential + damping_factor * (forcing - applied) / diagonal]
  transfers between devices with their start and end apart: 222 -> 16, of which waited for: 100 -> 11; matrix products, arithmetic and copies ran while one was open for 10% -> 0% of each run, Pallas kernels for 0% -> 19%
where the time goes in v1:
time: 131 us; the launch traced here: 130 us
  starting transfers between devices  45.3 us (35%)
  Pallas kernels  37.1 us (28%)
  waiting for transfers between devices  31.2 us (24%)
  between operations  14.3 us (11%)
  other arithmetic  1.31 us (1%)
    pallas_call x11, Pallas kernels, call(): pl.pallas_call(wrapped, out_shape=shapes, in_specs=specs, out_specs=out_s...  37.1 us
    ppermute x7, starting transfers between devices, shift(): lax.ppermute(high, axis, forward)  27.9 us
    ppermute x7, waiting for transfers between devices, shift(): lax.ppermute(low, axis, backward)  24.6 us
    ppermute x7, starting transfers between devices, shift(): lax.ppermute(low, axis, backward)  11.1 us
    all_to_all x1, starting transfers between devices, shards(): forcing2 = lax.all_to_all(copies, everywhere, 0, 0)  6.32 us
    ppermute x7, waiting for transfers between devices, shift(): lax.ppermute(high, axis, forward)  5.16 us
  transfers between devices with their start and end apart: 16, of which 11 were waited for; matrix products, arithmetic and copies ran while one was open for 0% of the time, Pallas kernels for 19%

profile of v1, /device:TPU:1, one launch (start us, length us, event | category | flops | bytes accessed | tf_op | source)
XLA Modules:
  0.0 130.4 jit_solution(6665337692397563860)
XLA Ops:
  7.2 0.0 all-gather.3.cloned.1.call-start
  7.2 1.2 fusion.3
  8.5 0.2 shard_map.50
  8.6 0.7 shard_map.57
  9.4 0.0 all-gather.3.cloned.1.call-update
  9.4 4.0 %collective-permute-start = (f32[296,128]{1,0:T(8,128)S(1)}, f32[296,128]{1,0:T(8,128)S(1)}, u32[]{:S(2)}, u32[]{:S(2)}) collective-permute-start(f32[296,128]{1,0:T(8,128)S(1)} %get-tuple-element.41), channel_id=1, source_target_pairs={{0,32},{32,64},{64,96},{1,33},{33,65},{65,97},{2,34},{34,66},{66,9... | collective-permute-start | bytes 454664 | tf_op jit(solution)/shard_map/ppermute | solution.py:284
  13.4 1.3 collective-permute-start.1
  14.7 1.3 collective-permute-done.refs_4_
  15.9 3.8 %collective-permute-done.1.refs_5_ = f32[296,128]{1,0:T(8,128)S(1)} collective-permute-done((f32[296,128]{1,0:T(8,128)S(1)}, f32[296,128]{1,0:T(8,128)S(1)}, u32[]{:S(2)}, u32[]{:S(2)}) %collective-permute-start.1) | collective-permute-done | bytes 151584 | tf_op jit(solution)/shard_map/ppermute | solution.py:284
  19.7 0.2 shard_map.51
  19.9 5.3 %collective-permute-start.2 = (f32[800,128]{1,0:T(8,128)S(1)}, f32[800,128]{1,0:T(8,128)S(1)}, u32[]{:S(2)}, u32[]{:S(2)}) collective-permute-start(f32[800,128]{1,0:T(8,128)S(1)} %get-tuple-element.47), channel_id=1, source_target_pairs={{0,1},{1,2},{2,3},{3,4},{4,5},{5,6},{6,7},{8,9},{9,10},{10,11},{11... | collective-permute-start | bytes 1228808 | tf_op jit(solution)/shard_map/ppermute | solution.py:284
  25.2 1.9 %collective-permute-start.3 = (f32[800,128]{1,0:T(8,128)S(1)}, f32[800,128]{1,0:T(8,128)S(1)}, u32[]{:S(2)}, u32[]{:S(2)}) collective-permute-start(f32[800,128]{1,0:T(8,128)S(1)} %get-tuple-element.48), channel_id=1, source_target_pairs={{1,0},{2,1},{3,2},{4,3},{5,4},{6,5},{7,6},{9,8},{10,9},{11,10},{12... | collective-permute-start | bytes 1228808 | tf_op jit(solution)/shard_map/ppermute | solution.py:284
  27.2 3.0 %collective-permute-done.2.refs_4_ = f32[800,128]{1,0:T(8,128)S(1)} collective-permute-done((f32[800,128]{1,0:T(8,128)S(1)}, f32[800,128]{1,0:T(8,128)S(1)}, u32[]{:S(2)}, u32[]{:S(2)}) %collective-permute-start.2) | collective-permute-done | bytes 409632 | tf_op jit(solution)/shard_map/ppermute | solution.py:284
  30.1 4.4 %collective-permute-done.3.refs_5_ = f32[800,128]{1,0:T(8,128)S(1)} collective-permute-done((f32[800,128]{1,0:T(8,128)S(1)}, f32[800,128]{1,0:T(8,128)S(1)}, u32[]{:S(2)}, u32[]{:S(2)}) %collective-permute-start.3) | collective-permute-done | bytes 409632 | tf_op jit(solution)/shard_map/ppermute | solution.py:284
  34.5 1.3 shard_map.52
  35.8 3.2 %collective-permute-start.4 = (f32[280,128]{1,0:T(8,128)S(1)}, f32[280,128]{1,0:T(8,128)S(1)}, u32[]{:S(2)}, u32[]{:S(2)}) collective-permute-start(f32[280,128]{1,0:T(8,128)S(1)} %get-tuple-element.53), channel_id=1, source_target_pairs={{0,8},{8,16},{16,24},{1,9},{9,17},{17,25},{2,10},{10,18},{18,26},{... | collective-permute-start | bytes 430088 | tf_op jit(solution)/shard_map/ppermute | solution.py:284
  39.1 1.3 collective-permute-start.5
  40.4 0.7 collective-permute-done.4.refs_4_
  41.1 4.0 %collective-permute-done.5.refs_5_ = f32[280,128]{1,0:T(8,128)S(1)} collective-permute-done((f32[280,128]{1,0:T(8,128)S(1)}, f32[280,128]{1,0:T(8,128)S(1)}, u32[]{:S(2)}, u32[]{:S(2)}) %collective-permute-start.5) | collective-permute-done | bytes 143392 | tf_op jit(solution)/shard_map/ppermute | solution.py:284
  45.1 6.1 %shard_map.53 = (f32[1,16,32,128]{3,2,1,0:T(8,128)S(1)}, f32[1,8,16,128]{3,2,1,0:T(8,128)S(1)}, f32[150,48,256]{2,1,0:T(8,128)}, f32[22,40,128]{2,1,0:T(8,128)S(...) custom-call(f32[1,26,48,128]{3,2,1,0:T(8,128)S(1)} %get-tuple-element.49.refs_0_, ...), custom_call_target="tpu_custom_call" | custom-call | tf_op jit(solution)/shard_map/pallas_call | solution.py:139
  51.2 3.0 %collective-permute-start.6 = (f32[160,128]{1,0:T(8,128)S(1)}, f32[160,128]{1,0:T(8,128)S(1)}, u32[]{:S(2)}, u32[]{:S(2)}) collective-permute-start(f32[160,128]{1,0:T(8,128)S(1)} %get-tuple-element.57), channel_id=1, source_target_pairs={{0,32},{32,64},{64,96},{1,33},{33,65},{65,97},{2,34},{34,66},{66,9... | collective-permute-start | bytes 245768 | tf_op jit(solution)/shard_map/ppermute | solution.py:284
  54.2 1.3 collective-permute-start.7
  55.5 0.2 collective-permute-done.6.refs_2_
  55.7 3.7 %collective-permute-done.7.refs_3_ = f32[160,128]{1,0:T(8,128)S(1)} collective-permute-done((f32[160,128]{1,0:T(8,128)S(1)}, f32[160,128]{1,0:T(8,128)S(1)}, u32[]{:S(2)}, u32[]{:S(2)}) %collective-permute-start.7) | collective-permute-done | bytes 81952 | tf_op jit(solution)/shard_map/ppermute | solution.py:284
  59.4 0.1 shard_map.54
  59.5 5.4 %collective-permute-start.8 = (f32[240,128]{1,0:T(8,128)S(1)}, f32[240,128]{1,0:T(8,128)S(1)}, u32[]{:S(2)}, u32[]{:S(2)}) collective-permute-start(f32[240,128]{1,0:T(8,128)S(1)} %get-tuple-element.61), channel_id=1, source_target_pairs={{0,1},{1,2},{2,3},{3,4},{4,5},{5,6},{6,7},{8,9},{9,10},{10,11},{11... | collective-permute-start | bytes 368648 | tf_op jit(solution)/shard_map/ppermute | solution.py:284
  64.9 1.9 %collective-permute-start.9 = (f32[240,128]{1,0:T(8,128)S(1)}, f32[240,128]{1,0:T(8,128)S(1)}, u32[]{:S(2)}, u32[]{:S(2)}) collective-permute-start(f32[240,128]{1,0:T(8,128)S(1)} %get-tuple-element.62), channel_id=1, source_target_pairs={{1,0},{2,1},{3,2},{4,3},{5,4},{6,5},{7,6},{9,8},{10,9},{11,10},{12... | collective-permute-start | bytes 368648 | tf_op jit(solution)/shard_map/ppermute | solution.py:284
  66.8 0.0 collective-permute-done.8.refs_2_
  66.9 4.9 %collective-permute-done.9.refs_3_ = f32[240,128]{1,0:T(8,128)S(1)} collective-permute-done((f32[240,128]{1,0:T(8,128)S(1)}, f32[240,128]{1,0:T(8,128)S(1)}, u32[]{:S(2)}, u32[]{:S(2)}) %collective-permute-start.9) | collective-permute-done | bytes 122912 | tf_op jit(solution)/shard_map/ppermute | solution.py:284
  71.8 0.5 shard_map.55
  72.3 3.4 %collective-permute-start.10 = (f32[128,128]{1,0:T(8,128)S(1)}, f32[128,128]{1,0:T(8,128)S(1)}, u32[]{:S(2)}, u32[]{:S(2)}) collective-permute-start(f32[128,128]{1,0:T(8,128)S(1)} %get-tuple-element.67), channel_id=1, source_target_pairs={{0,8},{8,16},{16,24},{1,9},{9,17},{17,25},{2,10},{10,18},{18,26},{... | collective-permute-start | bytes 196616 | tf_op jit(solution)/shard_map/ppermute | solution.py:284
  75.6 1.3 collective-permute-start.11
  76.9 0.0 collective-permute-done.10.refs_4_
  76.9 3.7 %collective-permute-done.11.refs_5_ = f32[128,128]{1,0:T(8,128)S(1)} collective-permute-done((f32[128,128]{1,0:T(8,128)S(1)}, f32[128,128]{1,0:T(8,128)S(1)}, u32[]{:S(2)}, u32[]{:S(2)}) %collective-permute-start.11) | collective-permute-done | bytes 65568 | tf_op jit(solution)/shard_map/ppermute | solution.py:284
  80.6 3.1 %shard_map.56 = (f32[8,40,128]{2,1,0:T(8,128)S(1)}, f32[16,48,256]{2,1,0:T(8,128)S(1)}, f32[128,8,128]{2,1,0:T(8,128)}, f32[359,40,128]{2,1,0:T(8,128)}, f32[568,128]{1,0:T(8,128)S(1)}, /*index=5*/f32[568,128]{1,0:T(8,128)S(1)}) custom-call(f32[1,20,40,128]{3,2,1,0:T(8,128)S(1)} %get-tuple-element.63.refs_0_, ...), custom_call_target="tpu_custom_call" | custom-call | tf_op jit(solution)/shard_map/pallas_call | solution.py:139
  83.8 0.0 all-gather.3.cloned.1.call-done
  83.8 6.3 %all-to-all-start = ((f32[128,8,128]{2,1,0:T(8,128)}), f32[128,8,128]{2,1,0:T(8,128)S(1)}, u32[]{:S(2)}, u32[]{:S(2)}) async-start(f32[128,8,128]{2,1,0:T(8,128)} %get-tuple-element.76), calls=%async_computation | async-start | bytes 1048576 | tf_op jit(solution)/shard_map/all_to_all | solution.py:725
  90.1 3.7 %collective-permute-start.12 = (f32[568,128]{1,0:T(8,128)S(1)}, f32[568,128]{1,0:T(8,128)S(1)}, u32[]{:S(2)}, u32[]{:S(2)}) collective-permute-start(f32[568,128]{1,0:T(8,128)S(1)} %get-tuple-element.71), channel_id=1, source_target_pairs={{0,1},{1,2},{2,3},{3,4},{4,5},{5,6},{6,7},{8,9},{9,10},{10,11},{11... | collective-permute-start | bytes 872456 | tf_op jit(solution)/shard_map/ppermute | solution.py:284
  93.8 2.1 %collective-permute-start.13 = (f32[568,128]{1,0:T(8,128)S(1)}, f32[568,128]{1,0:T(8,128)S(1)}, u32[]{:S(2)}, u32[]{:S(2)}) collective-permute-start(f32[568,128]{1,0:T(8,128)S(1)} %get-tuple-element.72), channel_id=1, source_target_pairs={{1,0},{2,1},{3,2},{4,3},{5,4},{6,5},{7,6},{9,8},{10,9},{11,10},{12... | collective-permute-start | bytes 872456 | tf_op jit(solution)/shard_map/ppermute | solution.py:284
  95.9 0.1 pad_add_fusion.refs_0_
  96.0 0.0 copy-start
  96.0 1.2 copy-done
  97.2 4.9 %shard_map.58.refs_1_ = f32[448,32,128]{2,1,0:T(8,128)} custom-call(f32[128,16,128]{2,1,0:T(8,128)S(1)} %bitcast.10), custom_call_target="tpu_custom_call" | custom-call | tf_op jit(solution)/shard_map/pallas_call | solution.py:139
  102.1 1.4 %all-to-all-done.refs_0_ = f32[128,8,128]{2,1,0:T(8,128)S(1)} async-done(((f32[128,8,128]{2,1,0:T(8,128)}), f32[128,8,128]{2,1,0:T(8,128)S(1)}, u32[]{:S(2)}, u32[]{:S(2)}) %all-to-all-start) | async-done | bytes 524320 | tf_op jit(solution)/shard_map/all_to_all | solution.py:725
  103.5 9.1 %shard_map.59.refs_7_ = f32[32,32,128]{2,1,0:T(8,128)S(1)} custom-call(f32[128,8,128]{2,1,0:T(8,128)S(1)} %all-to-all-done.refs_0_, f32[448,32,128]{2,1,0:T(8,128)} %shard_map.58.refs_1_), custom_call_target="tpu_custom_call" | custom-call | tf_op jit(solution)/shard_map/pallas_call | solution.py:139
  112.6 0.0 collective-permute-done.12.refs_3_
  112.6 0.0 collective-permute-done.13.refs_4_
  112.6 10.9 %shard_map.60 = (f32[16,32,128]{2,1,0:T(8,128)}, f32[16,32,128]{2,1,0:T(8,128)}) custom-call(s32[3]{0:T(128)S(1)} %pad_add_fusion.refs_0_, f32[8,40,128]{2,1,0:T(8,128)S(1)} %get-tuple-element.69.refs_1_, f32[16,48,256]{2,1,0:T(8,128)S(1)} %get-tuple-element.70.refs_2_, f32[568,128]{1,0:T(8,128)S(1)} %collective-permute-done.12.refs_3_, ...), custom_call_target="tpu_custom_call" | custom-call | tf_op jit(solution)/shard_map/pallas_call | solution.py:139
Async XLA Ops:
  7.2 76.6 %all-gather.3.cloned.1.call-start = ((), (), s32[]{:S(2)}) async-start(), calls=%async_computation.1 | async-start | bytes 1056768 | tf_op jit(solution)/shard_map/all_gather | solution.py:707
  9.4 6.5 %collective-permute-start = (f32[296,128]{1,0:T(8,128)S(1)}, f32[296,128]{1,0:T(8,128)S(1)}, u32[]{:S(2)}, u32[]{:S(2)}) collective-permute-start(f32[296,128]{1,0:T(8,128)S(1)} %get-tuple-element.41), channel_id=1, source_target_pairs={{0,32},{32,64},{64,96},{1,33},{33,65},{65,97},{2,34},{34,66},{66,9... | collective-permute-start | bytes 454664 | tf_op jit(solution)/shard_map/ppermute | solution.py:284
  13.4 6.4 %collective-permute-start.1 = (f32[296,128]{1,0:T(8,128)S(1)}, f32[296,128]{1,0:T(8,128)S(1)}, u32[]{:S(2)}, u32[]{:S(2)}) collective-permute-start(f32[296,128]{1,0:T(8,128)S(1)} %get-tuple-element.42), channel_id=1, source_target_pairs={{32,0},{64,32},{96,64},{33,1},{65,33},{97,65},{34,2},{66,34},{98,6... | collective-permute-start | bytes 454664 | tf_op jit(solution)/shard_map/ppermute | solution.py:284
  19.9 10.2 %collective-permute-start.2 = (f32[800,128]{1,0:T(8,128)S(1)}, f32[800,128]{1,0:T(8,128)S(1)}, u32[]{:S(2)}, u32[]{:S(2)}) collective-permute-start(f32[800,128]{1,0:T(8,128)S(1)} %get-tuple-element.47), channel_id=1, source_target_pairs={{0,1},{1,2},{2,3},{3,4},{4,5},{5,6},{6,7},{8,9},{9,10},{10,11},{11... | collective-permute-start | bytes 1228808 | tf_op jit(solution)/shard_map/ppermute | solution.py:284
  25.2 9.3 %collective-permute-start.3 = (f32[800,128]{1,0:T(8,128)S(1)}, f32[800,128]{1,0:T(8,128)S(1)}, u32[]{:S(2)}, u32[]{:S(2)}) collective-permute-start(f32[800,128]{1,0:T(8,128)S(1)} %get-tuple-element.48), channel_id=1, source_target_pairs={{1,0},{2,1},{3,2},{4,3},{5,4},{6,5},{7,6},{9,8},{10,9},{11,10},{12... | collective-permute-start | bytes 1228808 | tf_op jit(solution)/shard_map/ppermute | solution.py:284
  35.8 5.3 %collective-permute-start.4 = (f32[280,128]{1,0:T(8,128)S(1)}, f32[280,128]{1,0:T(8,128)S(1)}, u32[]{:S(2)}, u32[]{:S(2)}) collective-permute-start(f32[280,128]{1,0:T(8,128)S(1)} %get-tuple-element.53), channel_id=1, source_target_pairs={{0,8},{8,16},{16,24},{1,9},{9,17},{17,25},{2,10},{10,18},{18,26},{... | collective-permute-start | bytes 430088 | tf_op jit(solution)/shard_map/ppermute | solution.py:284
  39.1 6.1 %collective-permute-start.5 = (f32[280,128]{1,0:T(8,128)S(1)}, f32[280,128]{1,0:T(8,128)S(1)}, u32[]{:S(2)}, u32[]{:S(2)}) collective-permute-start(f32[280,128]{1,0:T(8,128)S(1)} %get-tuple-element.54), channel_id=1, source_target_pairs={{8,0},{16,8},{24,16},{9,1},{17,9},{25,17},{10,2},{18,10},{26,18},{... | collective-permute-start | bytes 430088 | tf_op jit(solution)/shard_map/ppermute | solution.py:284
  51.2 4.5 %collective-permute-start.6 = (f32[160,128]{1,0:T(8,128)S(1)}, f32[160,128]{1,0:T(8,128)S(1)}, u32[]{:S(2)}, u32[]{:S(2)}) collective-permute-start(f32[160,128]{1,0:T(8,128)S(1)} %get-tuple-element.57), channel_id=1, source_target_pairs={{0,32},{32,64},{64,96},{1,33},{33,65},{65,97},{2,34},{34,66},{66,9... | collective-permute-start | bytes 245768 | tf_op jit(solution)/shard_map/ppermute | solution.py:284
  54.2 5.2 %collective-permute-start.7 = (f32[160,128]{1,0:T(8,128)S(1)}, f32[160,128]{1,0:T(8,128)S(1)}, u32[]{:S(2)}, u32[]{:S(2)}) collective-permute-start(f32[160,128]{1,0:T(8,128)S(1)} %get-tuple-element.58), channel_id=1, source_target_pairs={{32,0},{64,32},{96,64},{33,1},{65,33},{97,65},{34,2},{66,34},{98,6... | collective-permute-start | bytes 245768 | tf_op jit(solution)/shard_map/ppermute | solution.py:284
  59.5 7.3 %collective-permute-start.8 = (f32[240,128]{1,0:T(8,128)S(1)}, f32[240,128]{1,0:T(8,128)S(1)}, u32[]{:S(2)}, u32[]{:S(2)}) collective-permute-start(f32[240,128]{1,0:T(8,128)S(1)} %get-tuple-element.61), channel_id=1, source_target_pairs={{0,1},{1,2},{2,3},{3,4},{4,5},{5,6},{6,7},{8,9},{9,10},{10,11},{11... | collective-permute-start | bytes 368648 | tf_op jit(solution)/shard_map/ppermute | solution.py:284
  64.9 6.9 %collective-permute-start.9 = (f32[240,128]{1,0:T(8,128)S(1)}, f32[240,128]{1,0:T(8,128)S(1)}, u32[]{:S(2)}, u32[]{:S(2)}) collective-permute-start(f32[240,128]{1,0:T(8,128)S(1)} %get-tuple-element.62), channel_id=1, source_target_pairs={{1,0},{2,1},{3,2},{4,3},{5,4},{6,5},{7,6},{9,8},{10,9},{11,10},{12... | collective-permute-start | bytes 368648 | tf_op jit(solution)/shard_map/ppermute | solution.py:284
  72.3 4.7 %collective-permute-start.10 = (f32[128,128]{1,0:T(8,128)S(1)}, f32[128,128]{1,0:T(8,128)S(1)}, u32[]{:S(2)}, u32[]{:S(2)}) collective-permute-start(f32[128,128]{1,0:T(8,128)S(1)} %get-tuple-element.67), channel_id=1, source_target_pairs={{0,8},{8,16},{16,24},{1,9},{9,17},{17,25},{2,10},{10,18},{18,26},{... | collective-permute-start | bytes 196616 | tf_op jit(solution)/shard_map/ppermute | solution.py:284
  75.6 5.0 %collective-permute-start.11 = (f32[128,128]{1,0:T(8,128)S(1)}, f32[128,128]{1,0:T(8,128)S(1)}, u32[]{:S(2)}, u32[]{:S(2)}) collective-permute-start(f32[128,128]{1,0:T(8,128)S(1)} %get-tuple-element.68), channel_id=1, source_target_pairs={{8,0},{16,8},{24,16},{9,1},{17,9},{25,17},{10,2},{18,10},{26,18},{... | collective-permute-start | bytes 196616 | tf_op jit(solution)/shard_map/ppermute | solution.py:284
  83.8 19.7 %all-to-all-start = ((f32[128,8,128]{2,1,0:T(8,128)}), f32[128,8,128]{2,1,0:T(8,128)S(1)}, u32[]{:S(2)}, u32[]{:S(2)}) async-start(f32[128,8,128]{2,1,0:T(8,128)} %get-tuple-element.76), calls=%async_computation | async-start | bytes 1048576 | tf_op jit(solution)/shard_map/all_to_all | solution.py:725
  90.1 22.5 %collective-permute-start.12 = (f32[568,128]{1,0:T(8,128)S(1)}, f32[568,128]{1,0:T(8,128)S(1)}, u32[]{:S(2)}, u32[]{:S(2)}) collective-permute-start(f32[568,128]{1,0:T(8,128)S(1)} %get-tuple-element.71), channel_id=1, source_target_pairs={{0,1},{1,2},{2,3},{3,4},{4,5},{5,6},{6,7},{8,9},{9,10},{10,11},{11... | collective-permute-start | bytes 872456 | tf_op jit(solution)/shard_map/ppermute | solution.py:284
  93.8 18.8 %collective-permute-start.13 = (f32[568,128]{1,0:T(8,128)S(1)}, f32[568,128]{1,0:T(8,128)S(1)}, u32[]{:S(2)}, u32[]{:S(2)}) collective-permute-start(f32[568,128]{1,0:T(8,128)S(1)} %get-tuple-element.72), channel_id=1, source_target_pairs={{1,0},{2,1},{3,2},{4,3},{5,4},{6,5},{7,6},{9,8},{10,9},{11,10},{12... | collective-permute-start | bytes 872456 | tf_op jit(solution)/shard_map/ppermute | solution.py:284
  96.0 1.2 copy-start
Sparse Core Ops, SparseCore 0:
  11.4 67.2 all-gather.2

commit v2 on v1

--- a/solution.py
+++ b/solution.py
@@ -69,15 +69,12 @@
 
 
 class Far:
-    def __init__(self, ins, outs, late):
+    def __init__(self, ins, outs):
         self.ins = {k: pltpu.make_async_copy(*pair) for k, pair in ins.items()}
         self.outs = {k: pltpu.make_async_copy(*pair) for k, pair in outs.items()}
         self.started = []
-        self.start(*[k for k in self.ins if k not in late])
-
-    def start(self, *keys):
-        for k in keys:
-            self.ins[k].start()
+        for copy in self.ins.values():
+            copy.start()
 
     def wait(self, *keys):
         for k in keys or tuple(self.ins):
@@ -99,7 +96,7 @@
     return (max(shape[0], -(-7 * MIB // plane)), *shape[1:])
 
 
-def call(body, outs, scratch, *args, place=None, far_in={}, far_out=(), late=(), grant=48):
+def call(body, outs, scratch, *args, place=None, far_in={}, far_out=(), grant=48):
     shapes = [
         jax.ShapeDtypeStruct(padded(shape) if k in far_out else shape, F32)
         for k, shape in enumerate(outs)
@@ -129,7 +126,7 @@
         for j, k in enumerate(far_out, len(far_in)):
             copies_out[k] = (rest[j], results[k].at[0 : outs[k][0]], rest[extra].at[j])
             results[k] = rest[j]
-        far = Far(copies_in, copies_out, late)
+        far = Far(copies_in, copies_out)
         body(far, *head, *ins, *results, *mine)
         far.finish()
 
@@ -284,7 +281,7 @@
     return lax.ppermute(high, axis, forward), lax.ppermute(low, axis, backward)
 
 
-def exchange(items, arrays, low, high):
+def exchange(items, arrays, low, high, beside=None):
     count = len(items)
     from_low, from_high = shift(low, high, "gx")
     shapes = [(item.n, item.z, item.xt, LANES) for item in items]
@@ -296,6 +293,7 @@
         pack_z(items, outs, c, d)
 
     *arrays, low, high = call(after_x, shapes + [message] * 2, [], *arrays, from_low, from_high)
+    extra = beside(low) if beside else None
     from_low, from_high = shift(low, high, "gz")
     shapes = [(item.n, item.zt, item.xt, LANES) for item in items]
     message = (total(item.rows_y for item in items), LANES)
@@ -307,7 +305,7 @@
 
     *arrays, low, high = call(after_z, shapes + [message] * 2, [], *arrays, from_low, from_high)
     from_low, from_high = shift(low, high, "gy")
-    return arrays, from_low, from_high
+    return (arrays, from_low, from_high, extra) if beside else (arrays, from_low, from_high)
 
 
 STIFFNESS = Item(1, Z0, X0, XT0, W0, "full", True, edge=1)
@@ -442,12 +440,12 @@
         FIRST, (zx_s, zx_f, zx_m, zx_coarse), from_low, from_high,
         ([s], [f.at[inner]], [m.at[inner]], [s1, m1]),
     )
-    couple(s, m, r, cx, cy, cz, 1, ZT0 - 1, 4, start=(f, va))
+    couple(s, m, r, cx, cy, cz, 1, ZT0 - 1, 8, start=(f, va))
     far.flush(2)
     op = (r, f, cx, cy, cz)
-    sweep(va, vb, op, 2, ZT0 - 2, 4)
-    sweep(vb, va, op, 3, ZT0 - 3, 4)
-    sweep(va, vb, op, 4, ZT0 - 4, 4)
+    sweep(va, vb, op, 2, ZT0 - 2, 11)
+    sweep(vb, va, op, 3, ZT0 - 3, 10)
+    sweep(va, vb, op, 4, ZT0 - 4, 9)
     for z in range(Z1):
         a, b = W0 + 2 * z, W0 + 2 * z + 1
         plane = remain(vb, op, a) + remain(vb, op, b)
@@ -472,11 +470,11 @@
         g[ZT1 - 1 - k] = jnp.zeros((XT1, LANES), F32)
     inner = g.at[W1 - G1 : ZT1 - (W1 - G1)]
     unpack_y(SECOND, (g_zx, v0_zx), from_low, from_high, ([inner], [v0]))
-    couple(s, m, r, cx, cy, cz, 1, ZT1 - 1, 10, start=(g, va))
+    couple(s, m, r, cx, cy, cz, 1, ZT1 - 1, 20, start=(g, va))
     far.flush(3)
     op = (r, g, cx, cy, cz)
-    sweep(va, vb, op, 4, ZT1 - 4, 10)
-    sweep(vb, va, op, 5, ZT1 - 5, 10)
+    sweep(va, vb, op, 4, ZT1 - 4, 14)
+    sweep(vb, va, op, 5, ZT1 - 5, 12)
     sweep(va, vb, op, 6, ZT1 - 6, 10)
     packed = pack_coarse(lambda z: remain(vb, op, W1 + z)[0:X1, :], 0, tall)
     for d in range(copies.shape[0]):
@@ -590,10 +588,10 @@
 
 def coarse_cycle(
     far, forcing, stacked, out,
-    f2, vb2, f3, va3, vb3, f4, vb4, tall,
+    f2, vb2, f3, va3, vb3, f4, vb4, tall, meanwhile,
 ):
     unpack_whole(forcing, 0, f2)
-    far.wait()
+    far.wait(0)
     (r2, cx2, cy2, cz2), (r3, cx3, cy3, cz3), (r4, cx4, cy4, cz4) = levels(stacked)
     op2 = (r2, f2, cx2, cy2, cz2)
     op3 = (r3, f3, cx3, cy3, cz3)
@@ -601,20 +599,21 @@
     va2 = out
 
     def four(va, vb, op, planes):
-        sweep(va, vb, op, 0, planes, 15, True)
-        sweep(vb, va, op, 0, planes, 15, True)
+        sweep(va, vb, op, 0, planes, 30, True)
+        sweep(vb, va, op, 0, planes, 30, True)
 
     def residue(v, op, planes):
         return lambda z: remain(v, op, z, z > 0, z < planes - 1)
 
     first_sweep(vb2, op2, 0, 32)
-    sweep(vb2, va2, op2, 0, 32, 15, True)
+    sweep(vb2, va2, op2, 0, 32, 30, True)
     four(va2, vb2, op2, 32)
     fold_whole(residue(va2, op2, 32), 32, 32, 1.0, tall, f3)
     first_sweep(vb3, op3, 0, 16)
     sweep(vb3, va3, op3, 0, 16, 15, True)
     four(va3, vb3, op3, 16)
     fold_whole(residue(va3, op3, 16), 16, 16, 1.0, tall, f4)
+    meanwhile()
     coarsest(vb4, op4)
     spread_whole(vb4, 8, 8, tall, va3)
     four(va3, vb3, op3, 16)
@@ -624,23 +623,26 @@
     four(va2, vb2, op2, 32)
 
 
-def postsmooth(
-    far, place, v1, v0_zx, from_low, from_high, stacked1, stacked0, correction,
+def finish(
+    far, place, stacked2, stacked1, stacked0, forcing, v1, v0_zx, from_low, from_high,
     potential, residual,
-    va1, vb1, v0, vb0, tall,
+    va1, vb1, v0, vb0, correction, f2, vb2, f3, va3, vb3, f4, vb4, tall,
 ):
-    base = (W0 + 1) * XT0
-    for message, first0, first1 in ((from_low, 0, 0), (from_high, W0 + Z0, W1 + Z1)):
-        rims = message[W0 * XT0 : base, :]
-        for w in range(W0):
-            v0[first0 + w, :, 0:LANES] = message[w * XT0 : (w + 1) * XT0, :]
-            v0[first0 + w, :, LANES:] = roll(rims, -W0 - 2 * W0 * w, 1)
-        for w in range(W1):
-            va1[first1 + w] = message[base + w * XT1 : base + (w + 1) * XT1, :]
-    for z in range(Z0):
-        v0[W0 + z] = v0_zx[z]
-    for z in range(Z1):
-        va1[W1 + z] = v1[z]
+    def meanwhile():
+        base = (W0 + 1) * XT0
+        for message, first0, first1 in ((from_low, 0, 0), (from_high, W0 + Z0, W1 + Z1)):
+            rims = message[W0 * XT0 : base, :]
+            for w in range(W0):
+                v0[first0 + w, :, 0:LANES] = message[w * XT0 : (w + 1) * XT0, :]
+                v0[first0 + w, :, LANES:] = roll(rims, -W0 - 2 * W0 * w, 1)
+            for w in range(W1):
+                va1[first1 + w] = message[base + w * XT1 : base + (w + 1) * XT1, :]
+        for z in range(Z0):
+            v0[W0 + z] = v0_zx[z]
+        for z in range(Z1):
+            va1[W1 + z] = v1[z]
+
+    coarse_cycle(far, forcing, stacked2, correction, f2, vb2, f3, va3, vb3, f4, vb4, tall, meanwhile)
     gz, gx, gy = place[0], place[1], place[2]
     planes = []
     for k in range(12):
@@ -657,13 +659,12 @@
     for z in range(ZT1):
         k = (z + 1) // 2
         va1[z] = va1[z] + tall[k * XT1 : (k + 1) * XT1, :]
-    far.wait(4)
-    far.start(5)
+    far.wait(1)
     op1 = parts(stacked1, ZT1)
-    sweep(va1, vb1, op1, 1, ZT1 - 1, 10)
-    sweep(vb1, va1, op1, 2, ZT1 - 2, 10)
-    sweep(va1, vb1, op1, 3, ZT1 - 3, 10)
-    sweep(vb1, va1, op1, 4, ZT1 - 4, 10)
+    sweep(va1, vb1, op1, 1, ZT1 - 1, 20)
+    sweep(vb1, va1, op1, 2, ZT1 - 2, 18)
+    sweep(va1, vb1, op1, 3, ZT1 - 3, 16)
+    sweep(vb1, va1, op1, 4, ZT1 - 4, 14)
     planes = []
     for k in range(14):
         planes += [va1[4 + k, 0:20, :], va1[4 + k, XT1 - 4 : XT1, :]]
@@ -677,12 +678,12 @@
             k = (z + 1) // 2
             at = slice(half * LANES, (half + 1) * LANES)
             v0[z, :, at] = v0[z, :, at] + tall[k * XT0 : (k + 1) * XT0, :]
-    far.wait(5)
+    far.wait(2)
     op0 = parts(stacked0, ZT0)
-    sweep(v0, vb0, op0, 1, ZT0 - 1, 4)
-    sweep(vb0, v0, op0, 2, ZT0 - 2, 4)
-    sweep(v0, vb0, op0, 3, ZT0 - 3, 4)
-    sweep(vb0, v0, op0, 4, ZT0 - 4, 4)
+    sweep(v0, vb0, op0, 1, ZT0 - 1, 12)
+    sweep(vb0, v0, op0, 2, ZT0 - 2, 11)
+    sweep(v0, vb0, op0, 3, ZT0 - 3, 10)
+    sweep(vb0, v0, op0, 4, ZT0 - 4, 9)
     for z in range(Z0):
         potential[z] = v0[W0 + z, 0:X0, 0:Y0]
     for z in range(Z0):
@@ -703,9 +704,13 @@
     coarse, low, high = call(
         prepare, [own1] + [x_message(FIRST)] * 2, [(Z1 * X0, LANES)], *fields
     )
-    (packed2,) = call(prepare_coarse, [(16, LANES)], [(Z1 // 2 * X1, LANES)], coarse)
-    operators2 = lax.all_gather(packed2, everywhere, axis=0)
-    arrays, from_low, from_high = exchange(FIRST, (*fields, coarse), low, high)
+
+    def gather_coarse(message):
+        block, _ = lax.optimization_barrier((coarse, message))
+        (packed2,) = call(prepare_coarse, [(16, LANES)], [(Z1 // 2 * X1, LANES)], block)
+        return lax.all_gather(packed2, everywhere, axis=0)
+
+    arrays, from_low, from_high, operators2 = exchange(FIRST, (*fields, coarse), low, high, gather_coarse)
     v0, g1, op0, s1, m1, low, high = call(
         presmooth0,
         [own0, own1, (5 * ZT0, XT0, 2 * LANES)] + [ext1] * 2 + [x_message(SECOND)] * 2,
@@ -721,7 +726,7 @@
         [ext1] * 2 + [(Z1 // 2 * X1, LANES)],
         arrays[0], arrays[1], s1, m1, from_low, from_high, far_out=(3,),
     )
-    copies, operators2 = lax.optimization_barrier((copies, operators2))
+    _, operators2 = lax.optimization_barrier((copies, operators2))
     forcing2 = lax.all_to_all(copies, everywhere, 0, 0)
     from_low, from_high = shift(low, high, "gz")
     level2, level3, level4 = (32, 32, LANES), (16, 16, LANES), (8, 8, LANES)
@@ -731,18 +736,12 @@
         [level2] * 2 + [level3] * 2 + [level4] * 2 + [(512, LANES)],
         operators2, far_in={0: operators2.shape}, far_out=(0,),
     )
-    (correction,) = call(
-        coarse_cycle,
-        [level2],
-        [level2] * 2 + [level3] * 3 + [level4] * 2 + [(512, LANES)],
-        forcing2, operators, far_in={1: stack2},
-    )
     return call(
-        postsmooth,
+        finish,
         [(Z0, X0, Y0)] * 2,
-        [ext1, ext1, ext0, ext0, (14 * XT0, LANES)],
-        v1, v0, from_low, from_high, op1, op0, correction,
-        place=place, far_in={4: stack1, 5: stack0}, late=(5,),
+        [ext1, ext1, ext0, ext0] + [level2] * 3 + [level3] * 3 + [level4] * 2 + [(14 * XT0, LANES)],
+        operators, op1, op0, forcing2, v1, v0, from_low, from_high,
+        place=place, far_in={0: stack2, 1: stack1, 2: stack0},
     )
 
 

time: 131 us -> 127 us (0.969)
  Pallas kernels: 37.1 us -> 33.7 us
  waiting for transfers between devices: 31.2 us -> 28.9 us
  starting transfers between devices: 45.3 us -> 46.8 us
    pallas_call x11 -> x10, Pallas kernels: 37.1 us -> 33.7 us  [call(): pl.pallas_call(wrapped, out_shape=shapes, in_specs=specs, out_specs=out_s...]
    ppermute x7, starting transfers between devices: 11.1 us -> 13 us  [shift(): lax.ppermute(low, axis, backward)]
    ppermute x7, waiting for transfers between devices: 5.16 us -> 3.38 us  [shift(): lax.ppermute(high, axis, forward)]
    all_to_all x1, waiting for transfers between devices: 1.38 us -> 0.01 us  [shards(): forcing2 = lax.all_to_all(copies, everywhere, 0, 0)]
  transfers between devices with their start and end apart: 16 -> 16, of which waited for: 11 -> 11; matrix products, arithmetic and copies ran while one was open for 0% -> 0% of each run, Pallas kernels for 19% -> 14%
where the time goes in v2:
time: 127 us; the launch traced here: 126 us
  starting transfers between devices  46.8 us (37%)
  Pallas kernels  33.7 us (27%)
  waiting for transfers between devices  28.9 us (23%)
  between operations  14.2 us (11%)
  other arithmetic  1.3 us (1%)
    pallas_call x10, Pallas kernels, call(): pl.pallas_call(wrapped, out_shape=shapes, in_specs=specs, out_specs=out_s...  33.7 us
    ppermute x7, starting transfers between devices, shift(): lax.ppermute(high, axis, forward)  27.2 us
    ppermute x7, waiting for transfers between devices, shift(): lax.ppermute(low, axis, backward)  25.5 us
    ppermute x7, starting transfers between devices, shift(): lax.ppermute(low, axis, backward)  13 us
    all_to_all x1, starting transfers between devices, shards(): forcing2 = lax.all_to_all(copies, everywhere, 0, 0)  6.6 us
    ppermute x7, waiting for transfers between devices, shift(): lax.ppermute(high, axis, forward)  3.38 us
  transfers between devices with their start and end apart: 16, of which 11 were waited for; matrix products, arithmetic and copies ran while one was open for 0% of the time, Pallas kernels for 14%

profile of v2, /device:TPU:1, one launch (start us, length us, event | category | flops | bytes accessed | tf_op | source)
XLA Modules:
  0.0 126.2 jit_solution(7728691320994818133)
XLA Ops:
  7.2 0.0 all-gather.3.cloned.1.call-start
  7.2 1.2 fusion.3
  8.4 0.2 shard_map.50
  8.6 4.0 %collective-permute-start = (f32[296,128]{1,0:T(8,128)S(1)}, f32[296,128]{1,0:T(8,128)S(1)}, u32[]{:S(2)}, u32[]{:S(2)}) collective-permute-start(f32[296,128]{1,0:T(8,128)S(1)} %get-tuple-element.41), channel_id=1, source_target_pairs={{0,32},{32,64},{64,96},{1,33},{33,65},{65,97},{2,34},{34,66},{66,9... | collective-permute-start | bytes 454664 | tf_op jit(solution)/shard_map/ppermute | solution.py:281
  12.6 1.3 %collective-permute-start.1 = (f32[296,128]{1,0:T(8,128)S(1)}, f32[296,128]{1,0:T(8,128)S(1)}, u32[]{:S(2)}, u32[]{:S(2)}) collective-permute-start(f32[296,128]{1,0:T(8,128)S(1)} %get-tuple-element.42), channel_id=1, source_target_pairs={{32,0},{64,32},{96,64},{33,1},{65,33},{97,65},{34,2},{66,34},{98,6... | collective-permute-start | bytes 454664 | tf_op jit(solution)/shard_map/ppermute | solution.py:281
  13.9 1.3 %collective-permute-done.refs_4_ = f32[296,128]{1,0:T(8,128)S(1)} collective-permute-done((f32[296,128]{1,0:T(8,128)S(1)}, f32[296,128]{1,0:T(8,128)S(1)}, u32[]{:S(2)}, u32[]{:S(2)}) %collective-permute-start) | collective-permute-done | bytes 151584 | tf_op jit(solution)/shard_map/ppermute | solution.py:281
  15.2 3.8 %collective-permute-done.1.refs_5_ = f32[296,128]{1,0:T(8,128)S(1)} collective-permute-done((f32[296,128]{1,0:T(8,128)S(1)}, f32[296,128]{1,0:T(8,128)S(1)}, u32[]{:S(2)}, u32[]{:S(2)}) %collective-permute-start.1) | collective-permute-done | bytes 151584 | tf_op jit(solution)/shard_map/ppermute | solution.py:281
  19.0 0.2 shard_map.51
  19.2 0.7 shard_map.57
  19.9 0.0 all-gather.3.cloned.1.call-update
  19.9 3.8 %collective-permute-start.3 = (f32[800,128]{1,0:T(8,128)S(1)}, f32[800,128]{1,0:T(8,128)S(1)}, u32[]{:S(2)}, u32[]{:S(2)}) collective-permute-start(f32[800,128]{1,0:T(8,128)S(1)} %get-tuple-element.48), channel_id=1, source_target_pairs={{1,0},{2,1},{3,2},{4,3},{5,4},{6,5},{7,6},{9,8},{10,9},{11,10},{12... | collective-permute-start | bytes 1228808 | tf_op jit(solution)/shard_map/ppermute | solution.py:281
  23.7 3.4 %collective-permute-start.2 = (f32[800,128]{1,0:T(8,128)S(1)}, f32[800,128]{1,0:T(8,128)S(1)}, u32[]{:S(2)}, u32[]{:S(2)}) collective-permute-start(f32[800,128]{1,0:T(8,128)S(1)} %get-tuple-element.47), channel_id=1, source_target_pairs={{0,1},{1,2},{2,3},{3,4},{4,5},{5,6},{6,7},{8,9},{9,10},{10,11},{11... | collective-permute-start | bytes 1228808 | tf_op jit(solution)/shard_map/ppermute | solution.py:281
  27.1 3.7 %collective-permute-done.3.refs_5_ = f32[800,128]{1,0:T(8,128)S(1)} collective-permute-done((f32[800,128]{1,0:T(8,128)S(1)}, f32[800,128]{1,0:T(8,128)S(1)}, u32[]{:S(2)}, u32[]{:S(2)}) %collective-permute-start.3) | collective-permute-done | bytes 409632 | tf_op jit(solution)/shard_map/ppermute | solution.py:281
  30.8 1.2 collective-permute-done.2.refs_4_
  32.0 1.3 %shard_map.52 = (f32[1,26,48,128]{3,2,1,0:T(8,128)S(1)}, f32[1,24,48,128]{3,2,1,0:T(8,128)S(1)}, f32[1,24,48,128]{3,2,1,0:T(8,128)S(1)}, f32[1,22,40,128]{3,2,1,...) custom-call(f32[1,16,48,128]{3,2,1,0:T(8,128)S(1)} %get-tuple-element.43.refs_0_, ...), custom_call_target="tpu_custom_call" | custom-call | tf_op jit(solution)/shard_map/pallas_call | solution.py:136
  33.3 3.2 %collective-permute-start.4 = (f32[280,128]{1,0:T(8,128)S(1)}, f32[280,128]{1,0:T(8,128)S(1)}, u32[]{:S(2)}, u32[]{:S(2)}) collective-permute-start(f32[280,128]{1,0:T(8,128)S(1)} %get-tuple-element.53), channel_id=1, source_target_pairs={{0,8},{8,16},{16,24},{1,9},{9,17},{17,25},{2,10},{10,18},{18,26},{... | collective-permute-start | bytes 430088 | tf_op jit(solution)/shard_map/ppermute | solution.py:281
  36.5 1.3 %collective-permute-start.5 = (f32[280,128]{1,0:T(8,128)S(1)}, f32[280,128]{1,0:T(8,128)S(1)}, u32[]{:S(2)}, u32[]{:S(2)}) collective-permute-start(f32[280,128]{1,0:T(8,128)S(1)} %get-tuple-element.54), channel_id=1, source_target_pairs={{8,0},{16,8},{24,16},{9,1},{17,9},{25,17},{10,2},{18,10},{26,18},{... | collective-permute-start | bytes 430088 | tf_op jit(solution)/shard_map/ppermute | solution.py:281
  37.8 0.7 collective-permute-done.4.refs_4_
  38.6 4.2 %collective-permute-done.5.refs_5_ = f32[280,128]{1,0:T(8,128)S(1)} collective-permute-done((f32[280,128]{1,0:T(8,128)S(1)}, f32[280,128]{1,0:T(8,128)S(1)}, u32[]{:S(2)}, u32[]{:S(2)}) %collective-permute-start.5) | collective-permute-done | bytes 143392 | tf_op jit(solution)/shard_map/ppermute | solution.py:281
  42.8 5.8 %shard_map.53 = (f32[1,16,32,128]{3,2,1,0:T(8,128)S(1)}, f32[1,8,16,128]{3,2,1,0:T(8,128)S(1)}, f32[150,48,256]{2,1,0:T(8,128)}, f32[22,40,128]{2,1,0:T(8,128)S(...) custom-call(f32[1,26,48,128]{3,2,1,0:T(8,128)S(1)} %get-tuple-element.49.refs_0_, ...), custom_call_target="tpu_custom_call" | custom-call | tf_op jit(solution)/shard_map/pallas_call | solution.py:136
  48.6 3.1 %collective-permute-start.6 = (f32[160,128]{1,0:T(8,128)S(1)}, f32[160,128]{1,0:T(8,128)S(1)}, u32[]{:S(2)}, u32[]{:S(2)}) collective-permute-start(f32[160,128]{1,0:T(8,128)S(1)} %get-tuple-element.57), channel_id=1, source_target_pairs={{0,32},{32,64},{64,96},{1,33},{33,65},{65,97},{2,34},{34,66},{66,9... | collective-permute-start | bytes 245768 | tf_op jit(solution)/shard_map/ppermute | solution.py:281
  51.7 1.3 %collective-permute-start.7 = (f32[160,128]{1,0:T(8,128)S(1)}, f32[160,128]{1,0:T(8,128)S(1)}, u32[]{:S(2)}, u32[]{:S(2)}) collective-permute-start(f32[160,128]{1,0:T(8,128)S(1)} %get-tuple-element.58), channel_id=1, source_target_pairs={{32,0},{64,32},{96,64},{33,1},{65,33},{97,65},{34,2},{66,34},{98,6... | collective-permute-start | bytes 245768 | tf_op jit(solution)/shard_map/ppermute | solution.py:281
  53.0 0.2 collective-permute-done.6.refs_2_
  53.2 4.0 %collective-permute-done.7.refs_3_ = f32[160,128]{1,0:T(8,128)S(1)} collective-permute-done((f32[160,128]{1,0:T(8,128)S(1)}, f32[160,128]{1,0:T(8,128)S(1)}, u32[]{:S(2)}, u32[]{:S(2)}) %collective-permute-start.7) | collective-permute-done | bytes 81952 | tf_op jit(solution)/shard_map/ppermute | solution.py:281
  57.1 0.1 shard_map.54
  57.2 6.6 %collective-permute-start.8 = (f32[240,128]{1,0:T(8,128)S(1)}, f32[240,128]{1,0:T(8,128)S(1)}, u32[]{:S(2)}, u32[]{:S(2)}) collective-permute-start(f32[240,128]{1,0:T(8,128)S(1)} %get-tuple-element.61), channel_id=1, source_target_pairs={{0,1},{1,2},{2,3},{3,4},{4,5},{5,6},{6,7},{8,9},{9,10},{10,11},{11... | collective-permute-start | bytes 368648 | tf_op jit(solution)/shard_map/ppermute | solution.py:281
  63.8 1.9 %collective-permute-start.9 = (f32[240,128]{1,0:T(8,128)S(1)}, f32[240,128]{1,0:T(8,128)S(1)}, u32[]{:S(2)}, u32[]{:S(2)}) collective-permute-start(f32[240,128]{1,0:T(8,128)S(1)} %get-tuple-element.62), channel_id=1, source_target_pairs={{1,0},{2,1},{3,2},{4,3},{5,4},{6,5},{7,6},{9,8},{10,9},{11,10},{12... | collective-permute-start | bytes 368648 | tf_op jit(solution)/shard_map/ppermute | solution.py:281
  65.8 0.0 collective-permute-done.8.refs_2_
  65.8 4.3 %collective-permute-done.9.refs_3_ = f32[240,128]{1,0:T(8,128)S(1)} collective-permute-done((f32[240,128]{1,0:T(8,128)S(1)}, f32[240,128]{1,0:T(8,128)S(1)}, u32[]{:S(2)}, u32[]{:S(2)}) %collective-permute-start.9) | collective-permute-done | bytes 122912 | tf_op jit(solution)/shard_map/ppermute | solution.py:281
  70.0 0.5 shard_map.55
  70.5 3.2 %collective-permute-start.10 = (f32[128,128]{1,0:T(8,128)S(1)}, f32[128,128]{1,0:T(8,128)S(1)}, u32[]{:S(2)}, u32[]{:S(2)}) collective-permute-start(f32[128,128]{1,0:T(8,128)S(1)} %get-tuple-element.67), channel_id=1, source_target_pairs={{0,8},{8,16},{16,24},{1,9},{9,17},{17,25},{2,10},{10,18},{18,26},{... | collective-permute-start | bytes 196616 | tf_op jit(solution)/shard_map/ppermute | solution.py:281
  73.7 1.3 %collective-permute-start.11 = (f32[128,128]{1,0:T(8,128)S(1)}, f32[128,128]{1,0:T(8,128)S(1)}, u32[]{:S(2)}, u32[]{:S(2)}) collective-permute-start(f32[128,128]{1,0:T(8,128)S(1)} %get-tuple-element.68), channel_id=1, source_target_pairs={{8,0},{16,8},{24,16},{9,1},{17,9},{25,17},{10,2},{18,10},{26,18},{... | collective-permute-start | bytes 196616 | tf_op jit(solution)/shard_map/ppermute | solution.py:281
  75.0 0.0 collective-permute-done.10.refs_4_
  75.0 4.0 %collective-permute-done.11.refs_5_ = f32[128,128]{1,0:T(8,128)S(1)} collective-permute-done((f32[128,128]{1,0:T(8,128)S(1)}, f32[128,128]{1,0:T(8,128)S(1)}, u32[]{:S(2)}, u32[]{:S(2)}) %collective-permute-start.11) | collective-permute-done | bytes 65568 | tf_op jit(solution)/shard_map/ppermute | solution.py:281
  79.0 4.8 %shard_map.56 = (f32[8,40,128]{2,1,0:T(8,128)S(1)}, f32[16,48,256]{2,1,0:T(8,128)S(1)}, f32[128,8,128]{2,1,0:T(8,128)}, f32[359,40,128]{2,1,0:T(8,128)}, f32[568,128]{1,0:T(8,128)S(1)}, /*index=5*/f32[568,128]{1,0:T(8,128)S(1)}) custom-call(f32[1,20,40,128]{3,2,1,0:T(8,128)S(1)} %get-tuple-element.63.refs_0_, ...), custom_call_target="tpu_custom_call" | custom-call | tf_op jit(solution)/shard_map/pallas_call | solution.py:136
  83.7 6.6 %all-to-all-start = ((f32[128,8,128]{2,1,0:T(8,128)}), f32[128,8,128]{2,1,0:T(8,128)S(1)}, u32[]{:S(2)}, u32[]{:S(2)}) async-start(f32[128,8,128]{2,1,0:T(8,128)} %get-tuple-element.69), calls=%async_computation | async-start | bytes 1048576 | tf_op jit(solution)/shard_map/all_to_all | solution.py:730
  90.3 3.7 %collective-permute-start.12 = (f32[568,128]{1,0:T(8,128)S(1)}, f32[568,128]{1,0:T(8,128)S(1)}, u32[]{:S(2)}, u32[]{:S(2)}) collective-permute-start(f32[568,128]{1,0:T(8,128)S(1)} %get-tuple-element.76), channel_id=1, source_target_pairs={{0,1},{1,2},{2,3},{3,4},{4,5},{5,6},{6,7},{8,9},{9,10},{10,11},{11... | collective-permute-start | bytes 872456 | tf_op jit(solution)/shard_map/ppermute | solution.py:281
  94.0 2.1 %collective-permute-start.13 = (f32[568,128]{1,0:T(8,128)S(1)}, f32[568,128]{1,0:T(8,128)S(1)}, u32[]{:S(2)}, u32[]{:S(2)}) collective-permute-start(f32[568,128]{1,0:T(8,128)S(1)} %get-tuple-element.77), channel_id=1, source_target_pairs={{1,0},{2,1},{3,2},{4,3},{5,4},{6,5},{7,6},{9,8},{10,9},{11,10},{12... | collective-permute-start | bytes 872456 | tf_op jit(solution)/shard_map/ppermute | solution.py:281
  96.1 0.1 pad_add_fusion.refs_0_
  96.2 0.0 all-gather.3.cloned.1.call-done
  96.2 0.0 copy-start
  96.2 1.2 copy-done
  97.4 4.9 %shard_map.58.refs_1_ = f32[448,32,128]{2,1,0:T(8,128)} custom-call(f32[128,16,128]{2,1,0:T(8,128)S(1)} %bitcast.10), custom_call_target="tpu_custom_call" | custom-call | tf_op jit(solution)/shard_map/pallas_call | solution.py:136
  102.3 0.0 collective-permute-done.12.refs_7_
  102.3 1.6 %collective-permute-done.13.refs_8_ = f32[568,128]{1,0:T(8,128)S(1)} collective-permute-done((f32[568,128]{1,0:T(8,128)S(1)}, f32[568,128]{1,0:T(8,128)S(1)}, u32[]{:S(2)}, u32[]{:S(2)}) %collective-permute-start.13) | collective-permute-done | bytes 290848 | tf_op jit(solution)/shard_map/ppermute | solution.py:281
  103.9 0.0 all-to-all-done.refs_4_
  103.9 15.4 %shard_map.59 = (f32[16,32,128]{2,1,0:T(8,128)}, f32[16,32,128]{2,1,0:T(8,128)}) custom-call(s32[3]{0:T(128)S(1)} %pad_add_fusion.refs_0_, f32[448,32,128]{2,1,0:T(8,128)} %shard_map.58.refs_1_, f32[359,40,128]{2,1,0:T(8,128)} %get-tuple-element.72.refs_2_, f32[150,48,256]{2,1,0:T(8,128)} %get-tuple-element.73.refs_3_, ...), custom_call_target="tpu_custom_call" | custom-call | tf_op jit(solution)/shard_map/pallas_call | solution.py:136
Async XLA Ops:
  7.2 89.0 %all-gather.3.cloned.1.call-start = ((), (), s32[]{:S(2)}) async-start(), calls=%async_computation.1 | async-start | bytes 1056768 | tf_op jit(solution)/shard_map/all_gather | solution.py:711
  8.6 6.5 %collective-permute-start = (f32[296,128]{1,0:T(8,128)S(1)}, f32[296,128]{1,0:T(8,128)S(1)}, u32[]{:S(2)}, u32[]{:S(2)}) collective-permute-start(f32[296,128]{1,0:T(8,128)S(1)} %get-tuple-element.41), channel_id=1, source_target_pairs={{0,32},{32,64},{64,96},{1,33},{33,65},{65,97},{2,34},{34,66},{66,9... | collective-permute-start | bytes 454664 | tf_op jit(solution)/shard_map/ppermute | solution.py:281
  12.6 6.4 %collective-permute-start.1 = (f32[296,128]{1,0:T(8,128)S(1)}, f32[296,128]{1,0:T(8,128)S(1)}, u32[]{:S(2)}, u32[]{:S(2)}) collective-permute-start(f32[296,128]{1,0:T(8,128)S(1)} %get-tuple-element.42), channel_id=1, source_target_pairs={{32,0},{64,32},{96,64},{33,1},{65,33},{97,65},{34,2},{66,34},{98,6... | collective-permute-start | bytes 454664 | tf_op jit(solution)/shard_map/ppermute | solution.py:281
  19.9 10.9 %collective-permute-start.3 = (f32[800,128]{1,0:T(8,128)S(1)}, f32[800,128]{1,0:T(8,128)S(1)}, u32[]{:S(2)}, u32[]{:S(2)}) collective-permute-start(f32[800,128]{1,0:T(8,128)S(1)} %get-tuple-element.48), channel_id=1, source_target_pairs={{1,0},{2,1},{3,2},{4,3},{5,4},{6,5},{7,6},{9,8},{10,9},{11,10},{12... | collective-permute-start | bytes 1228808 | tf_op jit(solution)/shard_map/ppermute | solution.py:281
  23.7 8.3 %collective-permute-start.2 = (f32[800,128]{1,0:T(8,128)S(1)}, f32[800,128]{1,0:T(8,128)S(1)}, u32[]{:S(2)}, u32[]{:S(2)}) collective-permute-start(f32[800,128]{1,0:T(8,128)S(1)} %get-tuple-element.47), channel_id=1, source_target_pairs={{0,1},{1,2},{2,3},{3,4},{4,5},{5,6},{6,7},{8,9},{9,10},{10,11},{11... | collective-permute-start | bytes 1228808 | tf_op jit(solution)/shard_map/ppermute | solution.py:281
  33.3 5.3 %collective-permute-start.4 = (f32[280,128]{1,0:T(8,128)S(1)}, f32[280,128]{1,0:T(8,128)S(1)}, u32[]{:S(2)}, u32[]{:S(2)}) collective-permute-start(f32[280,128]{1,0:T(8,128)S(1)} %get-tuple-element.53), channel_id=1, source_target_pairs={{0,8},{8,16},{16,24},{1,9},{9,17},{17,25},{2,10},{10,18},{18,26},{... | collective-permute-start | bytes 430088 | tf_op jit(solution)/shard_map/ppermute | solution.py:281
  36.5 6.3 %collective-permute-start.5 = (f32[280,128]{1,0:T(8,128)S(1)}, f32[280,128]{1,0:T(8,128)S(1)}, u32[]{:S(2)}, u32[]{:S(2)}) collective-permute-start(f32[280,128]{1,0:T(8,128)S(1)} %get-tuple-element.54), channel_id=1, source_target_pairs={{8,0},{16,8},{24,16},{9,1},{17,9},{25,17},{10,2},{18,10},{26,18},{... | collective-permute-start | bytes 430088 | tf_op jit(solution)/shard_map/ppermute | solution.py:281
  48.6 4.6 %collective-permute-start.6 = (f32[160,128]{1,0:T(8,128)S(1)}, f32[160,128]{1,0:T(8,128)S(1)}, u32[]{:S(2)}, u32[]{:S(2)}) collective-permute-start(f32[160,128]{1,0:T(8,128)S(1)} %get-tuple-element.57), channel_id=1, source_target_pairs={{0,32},{32,64},{64,96},{1,33},{33,65},{65,97},{2,34},{34,66},{66,9... | collective-permute-start | bytes 245768 | tf_op jit(solution)/shard_map/ppermute | solution.py:281
  51.7 5.5 %collective-permute-start.7 = (f32[160,128]{1,0:T(8,128)S(1)}, f32[160,128]{1,0:T(8,128)S(1)}, u32[]{:S(2)}, u32[]{:S(2)}) collective-permute-start(f32[160,128]{1,0:T(8,128)S(1)} %get-tuple-element.58), channel_id=1, source_target_pairs={{32,0},{64,32},{96,64},{33,1},{65,33},{97,65},{34,2},{66,34},{98,6... | collective-permute-start | bytes 245768 | tf_op jit(solution)/shard_map/ppermute | solution.py:281
  57.2 8.6 %collective-permute-start.8 = (f32[240,128]{1,0:T(8,128)S(1)}, f32[240,128]{1,0:T(8,128)S(1)}, u32[]{:S(2)}, u32[]{:S(2)}) collective-permute-start(f32[240,128]{1,0:T(8,128)S(1)} %get-tuple-element.61), channel_id=1, source_target_pairs={{0,1},{1,2},{2,3},{3,4},{4,5},{5,6},{6,7},{8,9},{9,10},{10,11},{11... | collective-permute-start | bytes 368648 | tf_op jit(solution)/shard_map/ppermute | solution.py:281
  63.8 6.2 %collective-permute-start.9 = (f32[240,128]{1,0:T(8,128)S(1)}, f32[240,128]{1,0:T(8,128)S(1)}, u32[]{:S(2)}, u32[]{:S(2)}) collective-permute-start(f32[240,128]{1,0:T(8,128)S(1)} %get-tuple-element.62), channel_id=1, source_target_pairs={{1,0},{2,1},{3,2},{4,3},{5,4},{6,5},{7,6},{9,8},{10,9},{11,10},{12... | collective-permute-start | bytes 368648 | tf_op jit(solution)/shard_map/ppermute | solution.py:281
  70.5 4.5 %collective-permute-start.10 = (f32[128,128]{1,0:T(8,128)S(1)}, f32[128,128]{1,0:T(8,128)S(1)}, u32[]{:S(2)}, u32[]{:S(2)}) collective-permute-start(f32[128,128]{1,0:T(8,128)S(1)} %get-tuple-element.67), channel_id=1, source_target_pairs={{0,8},{8,16},{16,24},{1,9},{9,17},{17,25},{2,10},{10,18},{18,26},{... | collective-permute-start | bytes 196616 | tf_op jit(solution)/shard_map/ppermute | solution.py:281
  73.7 5.3 %collective-permute-start.11 = (f32[128,128]{1,0:T(8,128)S(1)}, f32[128,128]{1,0:T(8,128)S(1)}, u32[]{:S(2)}, u32[]{:S(2)}) collective-permute-start(f32[128,128]{1,0:T(8,128)S(1)} %get-tuple-element.68), channel_id=1, source_target_pairs={{8,0},{16,8},{24,16},{9,1},{17,9},{25,17},{10,2},{18,10},{26,18},{... | collective-permute-start | bytes 196616 | tf_op jit(solution)/shard_map/ppermute | solution.py:281
  83.7 20.2 %all-to-all-start = ((f32[128,8,128]{2,1,0:T(8,128)}), f32[128,8,128]{2,1,0:T(8,128)S(1)}, u32[]{:S(2)}, u32[]{:S(2)}) async-start(f32[128,8,128]{2,1,0:T(8,128)} %get-tuple-element.69), calls=%async_computation | async-start | bytes 1048576 | tf_op jit(solution)/shard_map/all_to_all | solution.py:730
  90.3 12.0 %collective-permute-start.12 = (f32[568,128]{1,0:T(8,128)S(1)}, f32[568,128]{1,0:T(8,128)S(1)}, u32[]{:S(2)}, u32[]{:S(2)}) collective-permute-start(f32[568,128]{1,0:T(8,128)S(1)} %get-tuple-element.76), channel_id=1, source_target_pairs={{0,1},{1,2},{2,3},{3,4},{4,5},{5,6},{6,7},{8,9},{9,10},{10,11},{11... | collective-permute-start | bytes 872456 | tf_op jit(solution)/shard_map/ppermute | solution.py:281
  94.0 9.9 %collective-permute-start.13 = (f32[568,128]{1,0:T(8,128)S(1)}, f32[568,128]{1,0:T(8,128)S(1)}, u32[]{:S(2)}, u32[]{:S(2)}) collective-permute-start(f32[568,128]{1,0:T(8,128)S(1)} %get-tuple-element.77), channel_id=1, source_target_pairs={{1,0},{2,1},{3,2},{4,3},{5,4},{6,5},{7,6},{9,8},{10,9},{11,10},{12... | collective-permute-start | bytes 872456 | tf_op jit(solution)/shard_map/ppermute | solution.py:281
  96.2 1.2 copy-start
Sparse Core Ops, SparseCore 0:
  20.0 67.2 all-gather.2

commit v3 on v2

--- a/solution.py
+++ b/solution.py
@@ -69,12 +69,15 @@
 
 
 class Far:
-    def __init__(self, ins, outs):
+    def __init__(self, ins, outs, late):
         self.ins = {k: pltpu.make_async_copy(*pair) for k, pair in ins.items()}
         self.outs = {k: pltpu.make_async_copy(*pair) for k, pair in outs.items()}
         self.started = []
-        for copy in self.ins.values():
-            copy.start()
+        self.start(*[k for k in self.ins if k not in late])
+
+    def start(self, *keys):
+        for k in keys:
+            self.ins[k].start()
 
     def wait(self, *keys):
         for k in keys or tuple(self.ins):
@@ -96,7 +99,7 @@
     return (max(shape[0], -(-7 * MIB // plane)), *shape[1:])
 
 
-def call(body, outs, scratch, *args, place=None, far_in={}, far_out=(), grant=48):
+def call(body, outs, scratch, *args, place=None, far_in={}, far_out=(), late=(), grant=48):
     shapes = [
         jax.ShapeDtypeStruct(padded(shape) if k in far_out else shape, F32)
         for k, shape in enumerate(outs)
@@ -126,7 +129,7 @@
         for j, k in enumerate(far_out, len(far_in)):
             copies_out[k] = (rest[j], results[k].at[0 : outs[k][0]], rest[extra].at[j])
             results[k] = rest[j]
-        far = Far(copies_in, copies_out)
+        far = Far(copies_in, copies_out, late)
         body(far, *head, *ins, *results, *mine)
         far.finish()
 
@@ -470,11 +473,11 @@
         g[ZT1 - 1 - k] = jnp.zeros((XT1, LANES), F32)
     inner = g.at[W1 - G1 : ZT1 - (W1 - G1)]
     unpack_y(SECOND, (g_zx, v0_zx), from_low, from_high, ([inner], [v0]))
-    couple(s, m, r, cx, cy, cz, 1, ZT1 - 1, 20, start=(g, va))
+    couple(s, m, r, cx, cy, cz, 1, ZT1 - 1, 10, start=(g, va))
     far.flush(3)
     op = (r, g, cx, cy, cz)
-    sweep(va, vb, op, 4, ZT1 - 4, 14)
-    sweep(vb, va, op, 5, ZT1 - 5, 12)
+    sweep(va, vb, op, 4, ZT1 - 4, 10)
+    sweep(vb, va, op, 5, ZT1 - 5, 10)
     sweep(va, vb, op, 6, ZT1 - 6, 10)
     packed = pack_coarse(lambda z: remain(vb, op, W1 + z)[0:X1, :], 0, tall)
     for d in range(copies.shape[0]):
@@ -562,22 +565,23 @@
         out[z] = v[z]
 
 
-def levels(stacked):
-    level3 = [stacked.at[128 + 16 * (k // 2) : 144 + 16 * (k // 2), 16 * (k % 2) : 16 * (k % 2) + 16, :] for k in range(4)]
-    level4 = [stacked.at[160:168, 8 * k : 8 * k + 8, :] for k in range(4)]
-    return parts(stacked, 32, 4), level3, level4
+def levels(stacked2, stacked34):
+    level3 = [stacked34.at[16 * (k // 2) : 16 * (k // 2) + 16, 16 * (k % 2) : 16 * (k % 2) + 16, :] for k in range(4)]
+    level4 = [stacked34.at[32:40, 8 * k : 8 * k + 8, :] for k in range(4)]
+    return parts(stacked2, 32, 4), level3, level4
 
 
 def coarse_operators(
     far, operators,
-    stacked,
+    stacked2, stacked34,
     s2, m2, s3, m3, s4, m4, tall,
 ):
-    (r2, cx2, cy2, cz2), (r3, cx3, cy3, cz3), (r4, cx4, cy4, cz4) = levels(stacked)
+    (r2, cx2, cy2, cz2), (r3, cx3, cy3, cz3), (r4, cx4, cy4, cz4) = levels(stacked2, stacked34)
     far.wait()
     unpack_whole(operators, 0, s2)
     unpack_whole(operators, 8, m2)
     couple(s2, m2, r2, cx2, cy2, cz2, 0, 32, 10, True)
+    far.flush(0)
     fold_whole(lambda z: s2[z], 32, 32, 0.25, tall, s3)
     fold_whole(lambda z: m2[z], 32, 32, 1.0, tall, m3)
     couple(s3, m3, r3, cx3, cy3, cz3, 0, 16, 14, True)
@@ -587,12 +591,13 @@
 
 
 def coarse_cycle(
-    far, forcing, stacked, out,
+    far, forcing, stacked2, stacked34, out,
     f2, vb2, f3, va3, vb3, f4, vb4, tall, meanwhile,
 ):
     unpack_whole(forcing, 0, f2)
-    far.wait(0)
-    (r2, cx2, cy2, cz2), (r3, cx3, cy3, cz3), (r4, cx4, cy4, cz4) = levels(stacked)
+    far.wait(0, 3)
+    far.start(1, 2)
+    (r2, cx2, cy2, cz2), (r3, cx3, cy3, cz3), (r4, cx4, cy4, cz4) = levels(stacked2, stacked34)
     op2 = (r2, f2, cx2, cy2, cz2)
     op3 = (r3, f3, cx3, cy3, cz3)
     op4 = (r4, f4, cx4, cy4, cz4)
@@ -624,7 +629,7 @@
 
 
 def finish(
-    far, place, stacked2, stacked1, stacked0, forcing, v1, v0_zx, from_low, from_high,
+    far, place, stacked2, stacked1, stacked0, stacked34, forcing, v1, v0_zx, from_low, from_high,
     potential, residual,
     va1, vb1, v0, vb0, correction, f2, vb2, f3, va3, vb3, f4, vb4, tall,
 ):
@@ -642,7 +647,7 @@
         for z in range(Z1):
             va1[W1 + z] = v1[z]
 
-    coarse_cycle(far, forcing, stacked2, correction, f2, vb2, f3, va3, vb3, f4, vb4, tall, meanwhile)
+    coarse_cycle(far, forcing, stacked2, stacked34, correction, f2, vb2, f3, va3, vb3, f4, vb4, tall, meanwhile)
     gz, gx, gy = place[0], place[1], place[2]
     planes = []
     for k in range(12):
@@ -661,10 +666,10 @@
         va1[z] = va1[z] + tall[k * XT1 : (k + 1) * XT1, :]
     far.wait(1)
     op1 = parts(stacked1, ZT1)
-    sweep(va1, vb1, op1, 1, ZT1 - 1, 20)
-    sweep(vb1, va1, op1, 2, ZT1 - 2, 18)
-    sweep(va1, vb1, op1, 3, ZT1 - 3, 16)
-    sweep(vb1, va1, op1, 4, ZT1 - 4, 14)
+    sweep(va1, vb1, op1, 1, ZT1 - 1, 10)
+    sweep(vb1, va1, op1, 2, ZT1 - 2, 10)
+    sweep(va1, vb1, op1, 3, ZT1 - 3, 10)
+    sweep(vb1, va1, op1, 4, ZT1 - 4, 10)
     planes = []
     for k in range(14):
         planes += [va1[4 + k, 0:20, :], va1[4 + k, XT1 - 4 : XT1, :]]
@@ -718,7 +723,8 @@
         *arrays, from_low, from_high, far_out=(2,),
     )
     arrays, from_low, from_high = exchange(SECOND, (g1, v0), low, high)
-    stack0, stack1, stack2 = (5 * ZT0, XT0, 2 * LANES), (5 * ZT1, XT1, LANES), (168, 32, LANES)
+    stack0, stack1 = (5 * ZT0, XT0, 2 * LANES), (5 * ZT1, XT1, LANES)
+    stack2, stack34 = (128, 32, LANES), (40, 32, LANES)
     message = ((W0 + 1) * XT0 + W1 * XT1, LANES)
     v1, v0, copies, op1, low, high = call(
         presmooth1,
@@ -730,18 +736,18 @@
     forcing2 = lax.all_to_all(copies, everywhere, 0, 0)
     from_low, from_high = shift(low, high, "gz")
     level2, level3, level4 = (32, 32, LANES), (16, 16, LANES), (8, 8, LANES)
-    (operators,) = call(
+    operators, operators34 = call(
         coarse_operators,
-        [stack2],
+        [stack2, stack34],
         [level2] * 2 + [level3] * 2 + [level4] * 2 + [(512, LANES)],
-        operators2, far_in={0: operators2.shape}, far_out=(0,),
+        operators2, far_in={0: operators2.shape}, far_out=(0, 1),
     )
     return call(
         finish,
         [(Z0, X0, Y0)] * 2,
         [ext1, ext1, ext0, ext0] + [level2] * 3 + [level3] * 3 + [level4] * 2 + [(14 * XT0, LANES)],
-        operators, op1, op0, forcing2, v1, v0, from_low, from_high,
-        place=place, far_in={0: stack2, 1: stack1, 2: stack0},
+        operators, op1, op0, operators34, forcing2, v1, v0, from_low, from_high,
+        place=place, far_in={0: stack2, 1: stack1, 2: stack0, 3: stack34}, late=(1, 2),
     )
 
 

time: 127 us -> 125 us (0.984)
  Pallas kernels: 33.7 us -> 31.7 us
    pallas_call x10, Pallas kernels: 33.7 us -> 31.7 us  [call(): pl.pallas_call(wrapped, out_shape=shapes, in_specs=specs, out_specs=out_s...]
  transfers between devices with their start and end apart: 16 -> 16, of which waited for: 11 -> 11; matrix products, arithmetic and copies ran while one was open for 0% -> 0% of each run, Pallas kernels for 14% -> 12%
where the time goes in v3:
time: 125 us
  starting transfers between devices  46.8 us (37%)
  Pallas kernels  31.7 us (25%)
  waiting for transfers between devices  29.6 us (24%)
  between operations  14.2 us (11%)
  other arithmetic  1.3 us (1%)
    pallas_call x10, Pallas kernels, call(): pl.pallas_call(wrapped, out_shape=shapes, in_specs=specs, out_specs=out_s...  31.7 us
    ppermute x7, starting transfers between devices, shift(): lax.ppermute(high, axis, forward)  27.2 us
    ppermute x7, waiting for transfers between devices, shift(): lax.ppermute(low, axis, backward)  26.2 us
    ppermute x7, starting transfers between devices, shift(): lax.ppermute(low, axis, backward)  13 us
    all_to_all x1, starting transfers between devices, shards(): forcing2 = lax.all_to_all(copies, everywhere, 0, 0)  6.6 us
    ppermute x7, waiting for transfers between devices, shift(): lax.ppermute(high, axis, forward)  3.38 us
  transfers between devices with their start and end apart: 16, of which 11 were waited for; matrix products, arithmetic and copies ran while one was open for 0% of the time, Pallas kernels for 12%

profile of v3, /device:TPU:1, one launch (start us, length us, event | category | flops | bytes accessed | tf_op | source)
XLA Modules:
  0.0 124.8 jit_solution(8982816900681230810)
XLA Ops:
  7.2 0.0 all-gather.3.cloned.1.call-start
  7.2 1.2 fusion.3
  8.4 0.2 shard_map.50
  8.6 4.0 %collective-permute-start = (f32[296,128]{1,0:T(8,128)S(1)}, f32[296,128]{1,0:T(8,128)S(1)}, u32[]{:S(2)}, u32[]{:S(2)}) collective-permute-start(f32[296,128]{1,0:T(8,128)S(1)} %get-tuple-element.43), channel_id=1, source_target_pairs={{0,32},{32,64},{64,96},{1,33},{33,65},{65,97},{2,34},{34,66},{66,9... | collective-permute-start | bytes 454664 | tf_op jit(solution)/shard_map/ppermute | solution.py:284
  12.6 1.3 %collective-permute-start.1 = (f32[296,128]{1,0:T(8,128)S(1)}, f32[296,128]{1,0:T(8,128)S(1)}, u32[]{:S(2)}, u32[]{:S(2)}) collective-permute-start(f32[296,128]{1,0:T(8,128)S(1)} %get-tuple-element.44), channel_id=1, source_target_pairs={{32,0},{64,32},{96,64},{33,1},{65,33},{97,65},{34,2},{66,34},{98,6... | collective-permute-start | bytes 454664 | tf_op jit(solution)/shard_map/ppermute | solution.py:284
  13.9 1.3 %collective-permute-done.refs_4_ = f32[296,128]{1,0:T(8,128)S(1)} collective-permute-done((f32[296,128]{1,0:T(8,128)S(1)}, f32[296,128]{1,0:T(8,128)S(1)}, u32[]{:S(2)}, u32[]{:S(2)}) %collective-permute-start) | collective-permute-done | bytes 151584 | tf_op jit(solution)/shard_map/ppermute | solution.py:284
  15.2 3.8 %collective-permute-done.1.refs_5_ = f32[296,128]{1,0:T(8,128)S(1)} collective-permute-done((f32[296,128]{1,0:T(8,128)S(1)}, f32[296,128]{1,0:T(8,128)S(1)}, u32[]{:S(2)}, u32[]{:S(2)}) %collective-permute-start.1) | collective-permute-done | bytes 151584 | tf_op jit(solution)/shard_map/ppermute | solution.py:284
  19.0 0.2 shard_map.51
  19.2 0.7 shard_map.57
  19.9 0.0 all-gather.3.cloned.1.call-update
  19.9 3.8 %collective-permute-start.3 = (f32[800,128]{1,0:T(8,128)S(1)}, f32[800,128]{1,0:T(8,128)S(1)}, u32[]{:S(2)}, u32[]{:S(2)}) collective-permute-start(f32[800,128]{1,0:T(8,128)S(1)} %get-tuple-element.50), channel_id=1, source_target_pairs={{1,0},{2,1},{3,2},{4,3},{5,4},{6,5},{7,6},{9,8},{10,9},{11,10},{12... | collective-permute-start | bytes 1228808 | tf_op jit(solution)/shard_map/ppermute | solution.py:284
  23.7 3.4 %collective-permute-start.2 = (f32[800,128]{1,0:T(8,128)S(1)}, f32[800,128]{1,0:T(8,128)S(1)}, u32[]{:S(2)}, u32[]{:S(2)}) collective-permute-start(f32[800,128]{1,0:T(8,128)S(1)} %get-tuple-element.49), channel_id=1, source_target_pairs={{0,1},{1,2},{2,3},{3,4},{4,5},{5,6},{6,7},{8,9},{9,10},{10,11},{11... | collective-permute-start | bytes 1228808 | tf_op jit(solution)/shard_map/ppermute | solution.py:284
  27.1 3.7 %collective-permute-done.3.refs_5_ = f32[800,128]{1,0:T(8,128)S(1)} collective-permute-done((f32[800,128]{1,0:T(8,128)S(1)}, f32[800,128]{1,0:T(8,128)S(1)}, u32[]{:S(2)}, u32[]{:S(2)}) %collective-permute-start.3) | collective-permute-done | bytes 409632 | tf_op jit(solution)/shard_map/ppermute | solution.py:284
  30.8 1.2 collective-permute-done.2.refs_4_
  32.0 1.3 %shard_map.52 = (f32[1,26,48,128]{3,2,1,0:T(8,128)S(1)}, f32[1,24,48,128]{3,2,1,0:T(8,128)S(1)}, f32[1,24,48,128]{3,2,1,0:T(8,128)S(1)}, f32[1,22,40,128]{3,2,1,...) custom-call(f32[1,16,48,128]{3,2,1,0:T(8,128)S(1)} %get-tuple-element.45.refs_0_, ...), custom_call_target="tpu_custom_call" | custom-call | tf_op jit(solution)/shard_map/pallas_call | solution.py:139
  33.3 3.2 %collective-permute-start.4 = (f32[280,128]{1,0:T(8,128)S(1)}, f32[280,128]{1,0:T(8,128)S(1)}, u32[]{:S(2)}, u32[]{:S(2)}) collective-permute-start(f32[280,128]{1,0:T(8,128)S(1)} %get-tuple-element.55), channel_id=1, source_target_pairs={{0,8},{8,16},{16,24},{1,9},{9,17},{17,25},{2,10},{10,18},{18,26},{... | collective-permute-start | bytes 430088 | tf_op jit(solution)/shard_map/ppermute | solution.py:284
  36.5 1.3 %collective-permute-start.5 = (f32[280,128]{1,0:T(8,128)S(1)}, f32[280,128]{1,0:T(8,128)S(1)}, u32[]{:S(2)}, u32[]{:S(2)}) collective-permute-start(f32[280,128]{1,0:T(8,128)S(1)} %get-tuple-element.56), channel_id=1, source_target_pairs={{8,0},{16,8},{24,16},{9,1},{17,9},{25,17},{10,2},{18,10},{26,18},{... | collective-permute-start | bytes 430088 | tf_op jit(solution)/shard_map/ppermute | solution.py:284
  37.8 0.7 collective-permute-done.4.refs_4_
  38.6 4.2 %collective-permute-done.5.refs_5_ = f32[280,128]{1,0:T(8,128)S(1)} collective-permute-done((f32[280,128]{1,0:T(8,128)S(1)}, f32[280,128]{1,0:T(8,128)S(1)}, u32[]{:S(2)}, u32[]{:S(2)}) %collective-permute-start.5) | collective-permute-done | bytes 143392 | tf_op jit(solution)/shard_map/ppermute | solution.py:284
  42.8 5.8 %shard_map.53 = (f32[1,16,32,128]{3,2,1,0:T(8,128)S(1)}, f32[1,8,16,128]{3,2,1,0:T(8,128)S(1)}, f32[150,48,256]{2,1,0:T(8,128)}, f32[22,40,128]{2,1,0:T(8,128)S(...) custom-call(f32[1,26,48,128]{3,2,1,0:T(8,128)S(1)} %get-tuple-element.51.refs_0_, ...), custom_call_target="tpu_custom_call" | custom-call | tf_op jit(solution)/shard_map/pallas_call | solution.py:139
  48.6 3.1 %collective-permute-start.6 = (f32[160,128]{1,0:T(8,128)S(1)}, f32[160,128]{1,0:T(8,128)S(1)}, u32[]{:S(2)}, u32[]{:S(2)}) collective-permute-start(f32[160,128]{1,0:T(8,128)S(1)} %get-tuple-element.59), channel_id=1, source_target_pairs={{0,32},{32,64},{64,96},{1,33},{33,65},{65,97},{2,34},{34,66},{66,9... | collective-permute-start | bytes 245768 | tf_op jit(solution)/shard_map/ppermute | solution.py:284
  51.7 1.3 %collective-permute-start.7 = (f32[160,128]{1,0:T(8,128)S(1)}, f32[160,128]{1,0:T(8,128)S(1)}, u32[]{:S(2)}, u32[]{:S(2)}) collective-permute-start(f32[160,128]{1,0:T(8,128)S(1)} %get-tuple-element.60), channel_id=1, source_target_pairs={{32,0},{64,32},{96,64},{33,1},{65,33},{97,65},{34,2},{66,34},{98,6... | collective-permute-start | bytes 245768 | tf_op jit(solution)/shard_map/ppermute | solution.py:284
  53.0 0.2 collective-permute-done.6.refs_2_
  53.2 4.0 %collective-permute-done.7.refs_3_ = f32[160,128]{1,0:T(8,128)S(1)} collective-permute-done((f32[160,128]{1,0:T(8,128)S(1)}, f32[160,128]{1,0:T(8,128)S(1)}, u32[]{:S(2)}, u32[]{:S(2)}) %collective-permute-start.7) | collective-permute-done | bytes 81952 | tf_op jit(solution)/shard_map/ppermute | solution.py:284
  57.1 0.1 shard_map.54
  57.2 6.6 %collective-permute-start.8 = (f32[240,128]{1,0:T(8,128)S(1)}, f32[240,128]{1,0:T(8,128)S(1)}, u32[]{:S(2)}, u32[]{:S(2)}) collective-permute-start(f32[240,128]{1,0:T(8,128)S(1)} %get-tuple-element.63), channel_id=1, source_target_pairs={{0,1},{1,2},{2,3},{3,4},{4,5},{5,6},{6,7},{8,9},{9,10},{10,11},{11... | collective-permute-start | bytes 368648 | tf_op jit(solution)/shard_map/ppermute | solution.py:284
  63.8 1.9 %collective-permute-start.9 = (f32[240,128]{1,0:T(8,128)S(1)}, f32[240,128]{1,0:T(8,128)S(1)}, u32[]{:S(2)}, u32[]{:S(2)}) collective-permute-start(f32[240,128]{1,0:T(8,128)S(1)} %get-tuple-element.64), channel_id=1, source_target_pairs={{1,0},{2,1},{3,2},{4,3},{5,4},{6,5},{7,6},{9,8},{10,9},{11,10},{12... | collective-permute-start | bytes 368648 | tf_op jit(solution)/shard_map/ppermute | solution.py:284
  65.8 0.0 collective-permute-done.8.refs_2_
  65.8 4.3 %collective-permute-done.9.refs_3_ = f32[240,128]{1,0:T(8,128)S(1)} collective-permute-done((f32[240,128]{1,0:T(8,128)S(1)}, f32[240,128]{1,0:T(8,128)S(1)}, u32[]{:S(2)}, u32[]{:S(2)}) %collective-permute-start.9) | collective-permute-done | bytes 122912 | tf_op jit(solution)/shard_map/ppermute | solution.py:284
  70.0 0.5 shard_map.55
  70.5 3.2 %collective-permute-start.10 = (f32[128,128]{1,0:T(8,128)S(1)}, f32[128,128]{1,0:T(8,128)S(1)}, u32[]{:S(2)}, u32[]{:S(2)}) collective-permute-start(f32[128,128]{1,0:T(8,128)S(1)} %get-tuple-element.69), channel_id=1, source_target_pairs={{0,8},{8,16},{16,24},{1,9},{9,17},{17,25},{2,10},{10,18},{18,26},{... | collective-permute-start | bytes 196616 | tf_op jit(solution)/shard_map/ppermute | solution.py:284
  73.7 1.3 %collective-permute-start.11 = (f32[128,128]{1,0:T(8,128)S(1)}, f32[128,128]{1,0:T(8,128)S(1)}, u32[]{:S(2)}, u32[]{:S(2)}) collective-permute-start(f32[128,128]{1,0:T(8,128)S(1)} %get-tuple-element.70), channel_id=1, source_target_pairs={{8,0},{16,8},{24,16},{9,1},{17,9},{25,17},{10,2},{18,10},{26,18},{... | collective-permute-start | bytes 196616 | tf_op jit(solution)/shard_map/ppermute | solution.py:284
  75.0 0.0 collective-permute-done.10.refs_4_
  75.0 4.0 %collective-permute-done.11.refs_5_ = f32[128,128]{1,0:T(8,128)S(1)} collective-permute-done((f32[128,128]{1,0:T(8,128)S(1)}, f32[128,128]{1,0:T(8,128)S(1)}, u32[]{:S(2)}, u32[]{:S(2)}) %collective-permute-start.11) | collective-permute-done | bytes 65568 | tf_op jit(solution)/shard_map/ppermute | solution.py:284
  79.0 3.2 %shard_map.56 = (f32[8,40,128]{2,1,0:T(8,128)S(1)}, f32[16,48,256]{2,1,0:T(8,128)S(1)}, f32[128,8,128]{2,1,0:T(8,128)}, f32[359,40,128]{2,1,0:T(8,128)}, f32[568,128]{1,0:T(8,128)S(1)}, /*index=5*/f32[568,128]{1,0:T(8,128)S(1)}) custom-call(f32[1,20,40,128]{3,2,1,0:T(8,128)S(1)} %get-tuple-element.65.refs_0_, ...), custom_call_target="tpu_custom_call" | custom-call | tf_op jit(solution)/shard_map/pallas_call | solution.py:139
  82.1 6.6 %all-to-all-start = ((f32[128,8,128]{2,1,0:T(8,128)}), f32[128,8,128]{2,1,0:T(8,128)S(1)}, u32[]{:S(2)}, u32[]{:S(2)}) async-start(f32[128,8,128]{2,1,0:T(8,128)} %get-tuple-element.71), calls=%async_computation | async-start | bytes 1048576 | tf_op jit(solution)/shard_map/all_to_all | solution.py:736
  88.7 3.7 %collective-permute-start.12 = (f32[568,128]{1,0:T(8,128)S(1)}, f32[568,128]{1,0:T(8,128)S(1)}, u32[]{:S(2)}, u32[]{:S(2)}) collective-permute-start(f32[568,128]{1,0:T(8,128)S(1)} %get-tuple-element.80), channel_id=1, source_target_pairs={{0,1},{1,2},{2,3},{3,4},{4,5},{5,6},{6,7},{8,9},{9,10},{10,11},{11... | collective-permute-start | bytes 872456 | tf_op jit(solution)/shard_map/ppermute | solution.py:284
  92.4 2.1 %collective-permute-start.13 = (f32[568,128]{1,0:T(8,128)S(1)}, f32[568,128]{1,0:T(8,128)S(1)}, u32[]{:S(2)}, u32[]{:S(2)}) collective-permute-start(f32[568,128]{1,0:T(8,128)S(1)} %get-tuple-element.81), channel_id=1, source_target_pairs={{1,0},{2,1},{3,2},{4,3},{5,4},{6,5},{7,6},{9,8},{10,9},{11,10},{12... | collective-permute-start | bytes 872456 | tf_op jit(solution)/shard_map/ppermute | solution.py:284
  94.5 0.1 pad_add_fusion.refs_0_
  94.6 0.0 all-gather.3.cloned.1.call-done
  94.6 0.0 copy-start
  94.6 1.2 copy-done
  95.8 4.2 %shard_map.58 = (f32[448,32,128]{2,1,0:T(8,128)}, f32[448,32,128]{2,1,0:T(8,128)}) custom-call(f32[128,16,128]{2,1,0:T(8,128)S(1)} %bitcast.10), custom_call_target="tpu_custom_call" | custom-call | tf_op jit(solution)/shard_map/pallas_call | solution.py:139
  100.0 0.0 collective-permute-done.12.refs_8_
  100.1 2.2 %collective-permute-done.13.refs_9_ = f32[568,128]{1,0:T(8,128)S(1)} collective-permute-done((f32[568,128]{1,0:T(8,128)S(1)}, f32[568,128]{1,0:T(8,128)S(1)}, u32[]{:S(2)}, u32[]{:S(2)}) %collective-permute-start.13) | collective-permute-done | bytes 290848 | tf_op jit(solution)/shard_map/ppermute | solution.py:284
  102.3 0.0 all-to-all-done.refs_5_
  102.3 15.6 %shard_map.59 = (f32[16,32,128]{2,1,0:T(8,128)}, f32[16,32,128]{2,1,0:T(8,128)}) custom-call(s32[3]{0:T(128)S(1)} %pad_add_fusion.refs_0_, f32[448,32,128]{2,1,0:T(8,128)} %get-tuple-element.74.refs_1_, f32[359,40,128]{2,1,0:T(8,128)} %get-tuple-element.75.refs_2_, f32[150,48,256]{2,1,0:T(8,128)} %get-tuple-element.76.refs_3_, ...), custom_call_target="tpu_custom_call" | custom-call | tf_op jit(solution)/shard_map/pallas_call | solution.py:139
Async XLA Ops:
  7.2 87.4 %all-gather.3.cloned.1.call-start = ((), (), s32[]{:S(2)}) async-start(), calls=%async_computation.1 | async-start | bytes 1056768 | tf_op jit(solution)/shard_map/all_gather | solution.py:716
  8.6 6.5 %collective-permute-start = (f32[296,128]{1,0:T(8,128)S(1)}, f32[296,128]{1,0:T(8,128)S(1)}, u32[]{:S(2)}, u32[]{:S(2)}) collective-permute-start(f32[296,128]{1,0:T(8,128)S(1)} %get-tuple-element.43), channel_id=1, source_target_pairs={{0,32},{32,64},{64,96},{1,33},{33,65},{65,97},{2,34},{34,66},{66,9... | collective-permute-start | bytes 454664 | tf_op jit(solution)/shard_map/ppermute | solution.py:284
  12.6 6.4 %collective-permute-start.1 = (f32[296,128]{1,0:T(8,128)S(1)}, f32[296,128]{1,0:T(8,128)S(1)}, u32[]{:S(2)}, u32[]{:S(2)}) collective-permute-start(f32[296,128]{1,0:T(8,128)S(1)} %get-tuple-element.44), channel_id=1, source_target_pairs={{32,0},{64,32},{96,64},{33,1},{65,33},{97,65},{34,2},{66,34},{98,6... | collective-permute-start | bytes 454664 | tf_op jit(solution)/shard_map/ppermute | solution.py:284
  19.9 10.9 %collective-permute-start.3 = (f32[800,128]{1,0:T(8,128)S(1)}, f32[800,128]{1,0:T(8,128)S(1)}, u32[]{:S(2)}, u32[]{:S(2)}) collective-permute-start(f32[800,128]{1,0:T(8,128)S(1)} %get-tuple-element.50), channel_id=1, source_target_pairs={{1,0},{2,1},{3,2},{4,3},{5,4},{6,5},{7,6},{9,8},{10,9},{11,10},{12... | collective-permute-start | bytes 1228808 | tf_op jit(solution)/shard_map/ppermute | solution.py:284
  23.7 8.3 %collective-permute-start.2 = (f32[800,128]{1,0:T(8,128)S(1)}, f32[800,128]{1,0:T(8,128)S(1)}, u32[]{:S(2)}, u32[]{:S(2)}) collective-permute-start(f32[800,128]{1,0:T(8,128)S(1)} %get-tuple-element.49), channel_id=1, source_target_pairs={{0,1},{1,2},{2,3},{3,4},{4,5},{5,6},{6,7},{8,9},{9,10},{10,11},{11... | collective-permute-start | bytes 1228808 | tf_op jit(solution)/shard_map/ppermute | solution.py:284
  33.3 5.3 %collective-permute-start.4 = (f32[280,128]{1,0:T(8,128)S(1)}, f32[280,128]{1,0:T(8,128)S(1)}, u32[]{:S(2)}, u32[]{:S(2)}) collective-permute-start(f32[280,128]{1,0:T(8,128)S(1)} %get-tuple-element.55), channel_id=1, source_target_pairs={{0,8},{8,16},{16,24},{1,9},{9,17},{17,25},{2,10},{10,18},{18,26},{... | collective-permute-start | bytes 430088 | tf_op jit(solution)/shard_map/ppermute | solution.py:284
  36.5 6.3 %collective-permute-start.5 = (f32[280,128]{1,0:T(8,128)S(1)}, f32[280,128]{1,0:T(8,128)S(1)}, u32[]{:S(2)}, u32[]{:S(2)}) collective-permute-start(f32[280,128]{1,0:T(8,128)S(1)} %get-tuple-element.56), channel_id=1, source_target_pairs={{8,0},{16,8},{24,16},{9,1},{17,9},{25,17},{10,2},{18,10},{26,18},{... | collective-permute-start | bytes 430088 | tf_op jit(solution)/shard_map/ppermute | solution.py:284
  48.6 4.6 %collective-permute-start.6 = (f32[160,128]{1,0:T(8,128)S(1)}, f32[160,128]{1,0:T(8,128)S(1)}, u32[]{:S(2)}, u32[]{:S(2)}) collective-permute-start(f32[160,128]{1,0:T(8,128)S(1)} %get-tuple-element.59), channel_id=1, source_target_pairs={{0,32},{32,64},{64,96},{1,33},{33,65},{65,97},{2,34},{34,66},{66,9... | collective-permute-start | bytes 245768 | tf_op jit(solution)/shard_map/ppermute | solution.py:284
  51.7 5.5 %collective-permute-start.7 = (f32[160,128]{1,0:T(8,128)S(1)}, f32[160,128]{1,0:T(8,128)S(1)}, u32[]{:S(2)}, u32[]{:S(2)}) collective-permute-start(f32[160,128]{1,0:T(8,128)S(1)} %get-tuple-element.60), channel_id=1, source_target_pairs={{32,0},{64,32},{96,64},{33,1},{65,33},{97,65},{34,2},{66,34},{98,6... | collective-permute-start | bytes 245768 | tf_op jit(solution)/shard_map/ppermute | solution.py:284
  57.2 8.6 %collective-permute-start.8 = (f32[240,128]{1,0:T(8,128)S(1)}, f32[240,128]{1,0:T(8,128)S(1)}, u32[]{:S(2)}, u32[]{:S(2)}) collective-permute-start(f32[240,128]{1,0:T(8,128)S(1)} %get-tuple-element.63), channel_id=1, source_target_pairs={{0,1},{1,2},{2,3},{3,4},{4,5},{5,6},{6,7},{8,9},{9,10},{10,11},{11... | collective-permute-start | bytes 368648 | tf_op jit(solution)/shard_map/ppermute | solution.py:284
  63.8 6.2 %collective-permute-start.9 = (f32[240,128]{1,0:T(8,128)S(1)}, f32[240,128]{1,0:T(8,128)S(1)}, u32[]{:S(2)}, u32[]{:S(2)}) collective-permute-start(f32[240,128]{1,0:T(8,128)S(1)} %get-tuple-element.64), channel_id=1, source_target_pairs={{1,0},{2,1},{3,2},{4,3},{5,4},{6,5},{7,6},{9,8},{10,9},{11,10},{12... | collective-permute-start | bytes 368648 | tf_op jit(solution)/shard_map/ppermute | solution.py:284
  70.5 4.5 %collective-permute-start.10 = (f32[128,128]{1,0:T(8,128)S(1)}, f32[128,128]{1,0:T(8,128)S(1)}, u32[]{:S(2)}, u32[]{:S(2)}) collective-permute-start(f32[128,128]{1,0:T(8,128)S(1)} %get-tuple-element.69), channel_id=1, source_target_pairs={{0,8},{8,16},{16,24},{1,9},{9,17},{17,25},{2,10},{10,18},{18,26},{... | collective-permute-start | bytes 196616 | tf_op jit(solution)/shard_map/ppermute | solution.py:284
  73.7 5.3 %collective-permute-start.11 = (f32[128,128]{1,0:T(8,128)S(1)}, f32[128,128]{1,0:T(8,128)S(1)}, u32[]{:S(2)}, u32[]{:S(2)}) collective-permute-start(f32[128,128]{1,0:T(8,128)S(1)} %get-tuple-element.70), channel_id=1, source_target_pairs={{8,0},{16,8},{24,16},{9,1},{17,9},{25,17},{10,2},{18,10},{26,18},{... | collective-permute-start | bytes 196616 | tf_op jit(solution)/shard_map/ppermute | solution.py:284
  82.1 20.2 %all-to-all-start = ((f32[128,8,128]{2,1,0:T(8,128)}), f32[128,8,128]{2,1,0:T(8,128)S(1)}, u32[]{:S(2)}, u32[]{:S(2)}) async-start(f32[128,8,128]{2,1,0:T(8,128)} %get-tuple-element.71), calls=%async_computation | async-start | bytes 1048576 | tf_op jit(solution)/shard_map/all_to_all | solution.py:736
  88.7 11.3 %collective-permute-start.12 = (f32[568,128]{1,0:T(8,128)S(1)}, f32[568,128]{1,0:T(8,128)S(1)}, u32[]{:S(2)}, u32[]{:S(2)}) collective-permute-start(f32[568,128]{1,0:T(8,128)S(1)} %get-tuple-element.80), channel_id=1, source_target_pairs={{0,1},{1,2},{2,3},{3,4},{4,5},{5,6},{6,7},{8,9},{9,10},{10,11},{11... | collective-permute-start | bytes 872456 | tf_op jit(solution)/shard_map/ppermute | solution.py:284
  92.4 9.9 %collective-permute-start.13 = (f32[568,128]{1,0:T(8,128)S(1)}, f32[568,128]{1,0:T(8,128)S(1)}, u32[]{:S(2)}, u32[]{:S(2)}) collective-permute-start(f32[568,128]{1,0:T(8,128)S(1)} %get-tuple-element.81), channel_id=1, source_target_pairs={{1,0},{2,1},{3,2},{4,3},{5,4},{6,5},{7,6},{9,8},{10,9},{11,10},{12... | collective-permute-start | bytes 872456 | tf_op jit(solution)/shard_map/ppermute | solution.py:284
  94.6 1.2 copy-start
Sparse Core Ops, SparseCore 0:
  20.0 67.2 all-gather.2

commit v4 on v3

--- a/solution.py
+++ b/solution.py
@@ -99,9 +99,9 @@
     return (max(shape[0], -(-7 * MIB // plane)), *shape[1:])
 
 
-def call(body, outs, scratch, *args, place=None, far_in={}, far_out=(), late=(), grant=48):
+def call(body, outs, scratch, *args, place=None, far_in={}, far_out=(), late=(), grant=48, pad=True):
     shapes = [
-        jax.ShapeDtypeStruct(padded(shape) if k in far_out else shape, F32)
+        jax.ShapeDtypeStruct(padded(shape) if pad and k in far_out else shape, F32)
         for k, shape in enumerate(outs)
     ]
     vmem = pl.BlockSpec(memory_space=pltpu.VMEM)
@@ -214,21 +214,38 @@
                 at += item.tall
 
 
-def unpack_z(items, refs, from_low, from_high, outs):
+class Planes:
+    def __init__(self, item, ref, from_low, from_high, base):
+        self.item, self.ref, self.low, self.high, self.base = item, ref, from_low, from_high, base
+
+    def received(self, n, z):
+        item = self.item
+        if item.wz <= z < item.wz + item.z:
+            return None
+        message, w = (self.low, z) if z < item.wz else (self.high, z - item.wz - item.z)
+        at = self.base + (n * item.wz + w) * item.tall
+        return message[at : at + item.tall, :]
+
+    def whole(self, n, z):
+        plane = self.received(n, z)
+        return self.ref[n, z - self.item.wz] if plane is None else self.item.widen(plane)
+
+    def narrow(self, n, z):
+        plane = self.received(n, z)
+        return self.item.narrow(self.ref[n, z - self.item.wz]) if plane is None else plane
+
+
+def planes_of(items, refs, from_low, from_high):
+    planes, base = [], 0
+    for item, ref in zip(items, refs):
+        planes.append(Planes(item, ref, from_low, from_high, base))
+        base += item.rows_z
+    return planes
+
+
+def pack_y(items, sources, low, high):
     at = 0
-    for item, ref, out in zip(items, refs, outs):
-        for n in range(item.n):
-            for w in range(item.wz):
-                out[n, w] = item.widen(from_low[at : at + item.tall, :])
-                out[n, item.wz + item.z + w] = item.widen(from_high[at : at + item.tall, :])
-                at += item.tall
-            for z in range(item.z):
-                out[n, item.wz + z] = ref[n, z]
-
-
-def pack_y(items, refs, low, high):
-    at = 0
-    for item, ref in zip(items, refs):
+    for item, source in zip(items, sources):
         lane = lane_of((item.tall, LANES))
         pairs = [(v, z) for v in range(item.virtual) for z in range(item.edge, item.zt - item.edge)]
         for g in range(item.groups):
@@ -236,7 +253,7 @@
             highs = lows
             for k, (v, z) in enumerate(pairs[g * item.slots : (g + 1) * item.slots]):
                 n, first = (v // 2, (v % 2) * item.own) if item.kind == "pair" else (v, 0)
-                plane = item.narrow(ref[n, z])
+                plane = source.narrow(n, z)
                 place = k * item.w
                 mask = (lane >= place) & (lane < place + item.w)
                 lows = jnp.where(mask, roll(plane, place - first, 1), lows)
@@ -246,13 +263,13 @@
             at += item.tall
 
 
-def unpack_y(items, refs, from_low, from_high, outs):
+def unpack_y(items, sources, from_low, from_high, outs):
     at = 0
-    for item, ref, fields in zip(items, refs, outs):
+    for item, source, fields in zip(items, sources, outs):
         lane = lane_of((item.tall, LANES))
         for v in range(item.virtual if item.edge else 0):
             for z in [*range(item.edge), *range(item.zt - item.edge, item.zt)]:
-                fields[v][z, :, 0:LANES] = ref[v, z]
+                fields[v][z, :, 0:LANES] = source.whole(v, z)
                 fields[v][z, :, LANES:] = jnp.zeros((item.xt, LANES), F32)
         pairs = [(v, z) for v in range(item.virtual) for z in range(item.edge, item.zt - item.edge)]
         for g in range(item.groups):
@@ -268,10 +285,10 @@
                     lane < start + item.w, upper, jnp.where(lane >= LANES - item.w, lower, 0.0)
                 )
                 if item.kind == "full":
-                    fields[v][z, :, 0:LANES] = ref[v, z]
+                    fields[v][z, :, 0:LANES] = source.whole(v, z)
                     fields[v][z, :, LANES:] = item.widen(rim)
                 else:
-                    plane = ref[v // 2, z] if item.kind == "pair" else ref[v, z]
+                    plane = source.whole(v // 2 if item.kind == "pair" else v, z)
                     if item.kind == "pair" and v % 2:
                         plane = roll(plane, item.own, 1)
                     fields[v][z] = jnp.where(lane < item.own, plane, rim)
@@ -297,18 +314,15 @@
 
     *arrays, low, high = call(after_x, shapes + [message] * 2, [], *arrays, from_low, from_high)
     extra = beside(low) if beside else None
-    from_low, from_high = shift(low, high, "gz")
-    shapes = [(item.n, item.zt, item.xt, LANES) for item in items]
+    z_low, z_high = shift(low, high, "gz")
     message = (total(item.rows_y for item in items), LANES)
 
     def after_z(far, *refs):
-        ins, (a, b), outs, (c, d) = refs[:count], refs[count : count + 2], refs[count + 2 : 2 * count + 2], refs[2 * count + 2 :]
-        unpack_z(items, ins, a, b, outs)
-        pack_y(items, outs, c, d)
-
-    *arrays, low, high = call(after_z, shapes + [message] * 2, [], *arrays, from_low, from_high)
-    from_low, from_high = shift(low, high, "gy")
-    return (arrays, from_low, from_high, extra) if beside else (arrays, from_low, from_high)
+        pack_y(items, planes_of(items, refs[:count], *refs[count : count + 2]), *refs[count + 2 :])
+
+    low, high = call(after_z, [message] * 2, [], *arrays, z_low, z_high)
+    received = (*arrays, z_low, z_high, *shift(low, high, "gy"))
+    return (received, extra) if beside else received
 
 
 STIFFNESS = Item(1, Z0, X0, XT0, W0, "full", True, edge=1)
@@ -433,14 +447,14 @@
 
 
 def presmooth0(
-    far, zx_s, zx_f, zx_m, zx_coarse, from_low, from_high,
+    far, x_s, x_f, x_m, x_coarse, z_low, z_high, from_low, from_high,
     v_own, g_own, op, s1, m1, low, high,
     s, m, va, vb, tall,
 ):
     r, f, cx, cy, cz = parts(op, ZT0)
     inner = slice(1, ZT0 - 1)
     unpack_y(
-        FIRST, (zx_s, zx_f, zx_m, zx_coarse), from_low, from_high,
+        FIRST, planes_of(FIRST, (x_s, x_f, x_m, x_coarse), z_low, z_high), from_low, from_high,
         ([s], [f.at[inner]], [m.at[inner]], [s1, m1]),
     )
     couple(s, m, r, cx, cy, cz, 1, ZT0 - 1, 8, start=(f, va))
@@ -463,7 +477,7 @@
 
 
 def presmooth1(
-    far, g_zx, v0_zx, s, m, from_low, from_high,
+    far, g_x, v0_x, z_low, z_high, from_low, from_high, s, m,
     v_own, v0, copies, op, low, high,
     va, vb, tall,
 ):
@@ -472,7 +486,7 @@
         g[k] = jnp.zeros((XT1, LANES), F32)
         g[ZT1 - 1 - k] = jnp.zeros((XT1, LANES), F32)
     inner = g.at[W1 - G1 : ZT1 - (W1 - G1)]
-    unpack_y(SECOND, (g_zx, v0_zx), from_low, from_high, ([inner], [v0]))
+    unpack_y(SECOND, planes_of(SECOND, (g_x, v0_x), z_low, z_high), from_low, from_high, ([inner], [v0]))
     couple(s, m, r, cx, cy, cz, 1, ZT1 - 1, 10, start=(g, va))
     far.flush(3)
     op = (r, g, cx, cy, cz)
@@ -666,10 +680,10 @@
         va1[z] = va1[z] + tall[k * XT1 : (k + 1) * XT1, :]
     far.wait(1)
     op1 = parts(stacked1, ZT1)
-    sweep(va1, vb1, op1, 1, ZT1 - 1, 10)
-    sweep(vb1, va1, op1, 2, ZT1 - 2, 10)
-    sweep(va1, vb1, op1, 3, ZT1 - 3, 10)
-    sweep(vb1, va1, op1, 4, ZT1 - 4, 10)
+    sweep(va1, vb1, op1, 1, ZT1 - 1, 20)
+    sweep(vb1, va1, op1, 2, ZT1 - 2, 18)
+    sweep(va1, vb1, op1, 3, ZT1 - 3, 16)
+    sweep(vb1, va1, op1, 4, ZT1 - 4, 14)
     planes = []
     for k in range(14):
         planes += [va1[4 + k, 0:20, :], va1[4 + k, XT1 - 4 : XT1, :]]
@@ -691,6 +705,7 @@
     sweep(vb0, v0, op0, 4, ZT0 - 4, 9)
     for z in range(Z0):
         potential[z] = v0[W0 + z, 0:X0, 0:Y0]
+    far.flush(0)
     for z in range(Z0):
         residual[z] = remain(v0, op0, W0 + z)[0:X0, 0:Y0]
 
@@ -715,14 +730,14 @@
         (packed2,) = call(prepare_coarse, [(16, LANES)], [(Z1 // 2 * X1, LANES)], block)
         return lax.all_gather(packed2, everywhere, axis=0)
 
-    arrays, from_low, from_high, operators2 = exchange(FIRST, (*fields, coarse), low, high, gather_coarse)
+    received, operators2 = exchange(FIRST, (*fields, coarse), low, high, gather_coarse)
     v0, g1, op0, s1, m1, low, high = call(
         presmooth0,
         [own0, own1, (5 * ZT0, XT0, 2 * LANES)] + [ext1] * 2 + [x_message(SECOND)] * 2,
         [ext0] * 4 + [(Z1 * X0, LANES)],
-        *arrays, from_low, from_high, far_out=(2,),
+        *received, far_out=(2,),
     )
-    arrays, from_low, from_high = exchange(SECOND, (g1, v0), low, high)
+    received = exchange(SECOND, (g1, v0), low, high)
     stack0, stack1 = (5 * ZT0, XT0, 2 * LANES), (5 * ZT1, XT1, LANES)
     stack2, stack34 = (128, 32, LANES), (40, 32, LANES)
     message = ((W0 + 1) * XT0 + W1 * XT1, LANES)
@@ -730,7 +745,7 @@
         presmooth1,
         [(Z1, XT1, LANES), (Z0, XT0, 2 * LANES), (devices, 8, LANES), stack1] + [message] * 2,
         [ext1] * 2 + [(Z1 // 2 * X1, LANES)],
-        arrays[0], arrays[1], s1, m1, from_low, from_high, far_out=(3,),
+        *received, s1, m1, far_out=(3,),
     )
     _, operators2 = lax.optimization_barrier((copies, operators2))
     forcing2 = lax.all_to_all(copies, everywhere, 0, 0)
@@ -748,6 +763,7 @@
         [ext1, ext1, ext0, ext0] + [level2] * 3 + [level3] * 3 + [level4] * 2 + [(14 * XT0, LANES)],
         operators, op1, op0, operators34, forcing2, v1, v0, from_low, from_high,
         place=place, far_in={0: stack2, 1: stack1, 2: stack0, 3: stack34}, late=(1, 2),
+        far_out=(0, 1), pad=False,
     )
 
 

time: 125 us -> 125 us (level)
  no operation moved by 1% of the time
where the time goes in v4:
time: 125 us
  starting transfers between devices  46.8 us (37%)
  Pallas kernels  31.5 us (25%)
  waiting for transfers between devices  29.6 us (24%)
  between operations  14.2 us (11%)
  other arithmetic  1.3 us (1%)
    pallas_call x10, Pallas kernels, call(): pl.pallas_call(wrapped, out_shape=shapes, in_specs=specs, out_specs=out_s...  31.5 us
    ppermute x7, starting transfers between devices, shift(): lax.ppermute(high, axis, forward)  27.2 us
    ppermute x7, waiting for transfers between devices, shift(): lax.ppermute(low, axis, backward)  26.2 us
    ppermute x7, starting transfers between devices, shift(): lax.ppermute(low, axis, backward)  13 us
    all_to_all x1, starting transfers between devices, shards(): forcing2 = lax.all_to_all(copies, everywhere, 0, 0)  6.61 us
    ppermute x7, waiting for transfers between devices, shift(): lax.ppermute(high, axis, forward)  3.38 us
  transfers between devices with their start and end apart: 16, of which 11 were waited for; matrix products, arithmetic and copies ran while one was open for 0% of the time, Pallas kernels for 12%

profile of v4, /device:TPU:1, one launch (start us, length us, event | category | flops | bytes accessed | tf_op | source)
XLA Modules:
  0.0 124.6 jit_solution(13895386285596718450)
XLA Ops:
  7.2 0.0 all-gather.3.cloned.1.call-start
  7.2 1.2 fusion.3
  8.4 0.2 shard_map.50
  8.6 4.0 %collective-permute-start = (f32[296,128]{1,0:T(8,128)S(1)}, f32[296,128]{1,0:T(8,128)S(1)}, u32[]{:S(2)}, u32[]{:S(2)}) collective-permute-start(f32[296,128]{1,0:T(8,128)S(1)} %get-tuple-element.37), channel_id=1, source_target_pairs={{0,32},{32,64},{64,96},{1,33},{33,65},{65,97},{2,34},{34,66},{66,9... | collective-permute-start | bytes 454664 | tf_op jit(solution)/shard_map/ppermute | solution.py:301
  12.6 1.3 %collective-permute-start.1 = (f32[296,128]{1,0:T(8,128)S(1)}, f32[296,128]{1,0:T(8,128)S(1)}, u32[]{:S(2)}, u32[]{:S(2)}) collective-permute-start(f32[296,128]{1,0:T(8,128)S(1)} %get-tuple-element.38), channel_id=1, source_target_pairs={{32,0},{64,32},{96,64},{33,1},{65,33},{97,65},{34,2},{66,34},{98,6... | collective-permute-start | bytes 454664 | tf_op jit(solution)/shard_map/ppermute | solution.py:301
  13.9 1.3 %collective-permute-done.refs_4_ = f32[296,128]{1,0:T(8,128)S(1)} collective-permute-done((f32[296,128]{1,0:T(8,128)S(1)}, f32[296,128]{1,0:T(8,128)S(1)}, u32[]{:S(2)}, u32[]{:S(2)}) %collective-permute-start) | collective-permute-done | bytes 151584 | tf_op jit(solution)/shard_map/ppermute | solution.py:301
  15.2 3.8 %collective-permute-done.1.refs_5_ = f32[296,128]{1,0:T(8,128)S(1)} collective-permute-done((f32[296,128]{1,0:T(8,128)S(1)}, f32[296,128]{1,0:T(8,128)S(1)}, u32[]{:S(2)}, u32[]{:S(2)}) %collective-permute-start.1) | collective-permute-done | bytes 151584 | tf_op jit(solution)/shard_map/ppermute | solution.py:301
  19.0 0.2 shard_map.51
  19.2 0.7 shard_map.57
  19.9 0.0 all-gather.3.cloned.1.call-update
  19.9 3.8 %collective-permute-start.3 = (f32[800,128]{1,0:T(8,128)S(1)}, f32[800,128]{1,0:T(8,128)S(1)}, u32[]{:S(2)}, u32[]{:S(2)}) collective-permute-start(f32[800,128]{1,0:T(8,128)S(1)} %get-tuple-element.44), channel_id=1, source_target_pairs={{1,0},{2,1},{3,2},{4,3},{5,4},{6,5},{7,6},{9,8},{10,9},{11,10},{12... | collective-permute-start | bytes 1228808 | tf_op jit(solution)/shard_map/ppermute | solution.py:301
  23.7 3.4 %collective-permute-start.2 = (f32[800,128]{1,0:T(8,128)S(1)}, f32[800,128]{1,0:T(8,128)S(1)}, u32[]{:S(2)}, u32[]{:S(2)}) collective-permute-start(f32[800,128]{1,0:T(8,128)S(1)} %get-tuple-element.43), channel_id=1, source_target_pairs={{0,1},{1,2},{2,3},{3,4},{4,5},{5,6},{6,7},{8,9},{9,10},{10,11},{11... | collective-permute-start | bytes 1228808 | tf_op jit(solution)/shard_map/ppermute | solution.py:301
  27.1 3.7 %collective-permute-done.3.refs_5_ = f32[800,128]{1,0:T(8,128)S(1)} collective-permute-done((f32[800,128]{1,0:T(8,128)S(1)}, f32[800,128]{1,0:T(8,128)S(1)}, u32[]{:S(2)}, u32[]{:S(2)}) %collective-permute-start.3) | collective-permute-done | bytes 409632 | tf_op jit(solution)/shard_map/ppermute | solution.py:301
  30.8 1.2 collective-permute-done.2.refs_4_
  32.0 1.3 %shard_map.52 = (f32[280,128]{1,0:T(8,128)S(1)}, f32[280,128]{1,0:T(8,128)S(1)}) custom-call(f32[1,16,48,128]{3,2,1,0:T(8,128)S(1)} %get-tuple-element.39.refs_0_, f32[1,16,48,128]{3,2,1,0:T(8,128)S(1)} %get-tuple-element.40.refs_1_, f32[1,16,48,128]{3,2,1,0:T(8,128)S(1)} %get-tuple-element.41.refs_2_, f32[1,8,40,128]{3,2,1,0:T(8,128)S(1)} %get-tuple-element.42.refs_3_, ...), custom_call_target="tpu_custom_call" | custom-call | tf_op jit(solution)/shard_map/pallas_call | solution.py:139
  33.3 3.2 %collective-permute-start.4 = (f32[280,128]{1,0:T(8,128)S(1)}, f32[280,128]{1,0:T(8,128)S(1)}, u32[]{:S(2)}, u32[]{:S(2)}) collective-permute-start(f32[280,128]{1,0:T(8,128)S(1)} %get-tuple-element.45), channel_id=1, source_target_pairs={{0,8},{8,16},{16,24},{1,9},{9,17},{17,25},{2,10},{10,18},{18,26},{... | collective-permute-start | bytes 430088 | tf_op jit(solution)/shard_map/ppermute | solution.py:301
  36.5 1.3 %collective-permute-start.5 = (f32[280,128]{1,0:T(8,128)S(1)}, f32[280,128]{1,0:T(8,128)S(1)}, u32[]{:S(2)}, u32[]{:S(2)}) collective-permute-start(f32[280,128]{1,0:T(8,128)S(1)} %get-tuple-element.46), channel_id=1, source_target_pairs={{8,0},{16,8},{24,16},{9,1},{17,9},{25,17},{10,2},{18,10},{26,18},{... | collective-permute-start | bytes 430088 | tf_op jit(solution)/shard_map/ppermute | solution.py:301
  37.8 0.7 collective-permute-done.4.refs_6_
  38.6 4.2 %collective-permute-done.5.refs_7_ = f32[280,128]{1,0:T(8,128)S(1)} collective-permute-done((f32[280,128]{1,0:T(8,128)S(1)}, f32[280,128]{1,0:T(8,128)S(1)}, u32[]{:S(2)}, u32[]{:S(2)}) %collective-permute-start.5) | collective-permute-done | bytes 143392 | tf_op jit(solution)/shard_map/ppermute | solution.py:301
  42.8 5.8 %shard_map.53 = (f32[1,16,32,128]{3,2,1,0:T(8,128)S(1)}, f32[1,8,16,128]{3,2,1,0:T(8,128)S(1)}, f32[150,48,256]{2,1,0:T(8,128)}, f32[22,40,128]{2,1,0:T(8,128)S(...) custom-call(f32[1,16,48,128]{3,2,1,0:T(8,128)S(1)} %get-tuple-element.39.refs_0_, ...), custom_call_target="tpu_custom_call" | custom-call | tf_op jit(solution)/shard_map/pallas_call | solution.py:139
  48.6 3.1 %collective-permute-start.6 = (f32[160,128]{1,0:T(8,128)S(1)}, f32[160,128]{1,0:T(8,128)S(1)}, u32[]{:S(2)}, u32[]{:S(2)}) collective-permute-start(f32[160,128]{1,0:T(8,128)S(1)} %get-tuple-element.49), channel_id=1, source_target_pairs={{0,32},{32,64},{64,96},{1,33},{33,65},{65,97},{2,34},{34,66},{66,9... | collective-permute-start | bytes 245768 | tf_op jit(solution)/shard_map/ppermute | solution.py:301
  51.7 1.3 %collective-permute-start.7 = (f32[160,128]{1,0:T(8,128)S(1)}, f32[160,128]{1,0:T(8,128)S(1)}, u32[]{:S(2)}, u32[]{:S(2)}) collective-permute-start(f32[160,128]{1,0:T(8,128)S(1)} %get-tuple-element.50), channel_id=1, source_target_pairs={{32,0},{64,32},{96,64},{33,1},{65,33},{97,65},{34,2},{66,34},{98,6... | collective-permute-start | bytes 245768 | tf_op jit(solution)/shard_map/ppermute | solution.py:301
  53.0 0.2 collective-permute-done.6.refs_2_
  53.2 4.0 %collective-permute-done.7.refs_3_ = f32[160,128]{1,0:T(8,128)S(1)} collective-permute-done((f32[160,128]{1,0:T(8,128)S(1)}, f32[160,128]{1,0:T(8,128)S(1)}, u32[]{:S(2)}, u32[]{:S(2)}) %collective-permute-start.7) | collective-permute-done | bytes 81952 | tf_op jit(solution)/shard_map/ppermute | solution.py:301
  57.1 0.1 shard_map.54
  57.2 6.6 %collective-permute-start.8 = (f32[240,128]{1,0:T(8,128)S(1)}, f32[240,128]{1,0:T(8,128)S(1)}, u32[]{:S(2)}, u32[]{:S(2)}) collective-permute-start(f32[240,128]{1,0:T(8,128)S(1)} %get-tuple-element.53), channel_id=1, source_target_pairs={{0,1},{1,2},{2,3},{3,4},{4,5},{5,6},{6,7},{8,9},{9,10},{10,11},{11... | collective-permute-start | bytes 368648 | tf_op jit(solution)/shard_map/ppermute | solution.py:301
  63.8 1.9 %collective-permute-start.9 = (f32[240,128]{1,0:T(8,128)S(1)}, f32[240,128]{1,0:T(8,128)S(1)}, u32[]{:S(2)}, u32[]{:S(2)}) collective-permute-start(f32[240,128]{1,0:T(8,128)S(1)} %get-tuple-element.54), channel_id=1, source_target_pairs={{1,0},{2,1},{3,2},{4,3},{5,4},{6,5},{7,6},{9,8},{10,9},{11,10},{12... | collective-permute-start | bytes 368648 | tf_op jit(solution)/shard_map/ppermute | solution.py:301
  65.8 0.0 collective-permute-done.8.refs_2_
  65.8 4.3 %collective-permute-done.9.refs_3_ = f32[240,128]{1,0:T(8,128)S(1)} collective-permute-done((f32[240,128]{1,0:T(8,128)S(1)}, f32[240,128]{1,0:T(8,128)S(1)}, u32[]{:S(2)}, u32[]{:S(2)}) %collective-permute-start.9) | collective-permute-done | bytes 122912 | tf_op jit(solution)/shard_map/ppermute | solution.py:301
  70.0 0.5 shard_map.55
  70.5 3.2 %collective-permute-start.10 = (f32[128,128]{1,0:T(8,128)S(1)}, f32[128,128]{1,0:T(8,128)S(1)}, u32[]{:S(2)}, u32[]{:S(2)}) collective-permute-start(f32[128,128]{1,0:T(8,128)S(1)} %get-tuple-element.55), channel_id=1, source_target_pairs={{0,8},{8,16},{16,24},{1,9},{9,17},{17,25},{2,10},{10,18},{18,26},{... | collective-permute-start | bytes 196616 | tf_op jit(solution)/shard_map/ppermute | solution.py:301
  73.7 1.3 %collective-permute-start.11 = (f32[128,128]{1,0:T(8,128)S(1)}, f32[128,128]{1,0:T(8,128)S(1)}, u32[]{:S(2)}, u32[]{:S(2)}) collective-permute-start(f32[128,128]{1,0:T(8,128)S(1)} %get-tuple-element.56), channel_id=1, source_target_pairs={{8,0},{16,8},{24,16},{9,1},{17,9},{25,17},{10,2},{18,10},{26,18},{... | collective-permute-start | bytes 196616 | tf_op jit(solution)/shard_map/ppermute | solution.py:301
  75.0 0.0 collective-permute-done.10.refs_4_
  75.0 4.0 %collective-permute-done.11.refs_5_ = f32[128,128]{1,0:T(8,128)S(1)} collective-permute-done((f32[128,128]{1,0:T(8,128)S(1)}, f32[128,128]{1,0:T(8,128)S(1)}, u32[]{:S(2)}, u32[]{:S(2)}) %collective-permute-start.11) | collective-permute-done | bytes 65568 | tf_op jit(solution)/shard_map/ppermute | solution.py:301
  78.9 3.2 %shard_map.56 = (f32[8,40,128]{2,1,0:T(8,128)S(1)}, f32[16,48,256]{2,1,0:T(8,128)S(1)}, f32[128,8,128]{2,1,0:T(8,128)}, f32[359,40,128]{2,1,0:T(8,128)}, f32[568,128]{1,0:T(8,128)S(1)}, /*index=5*/f32[568,128]{1,0:T(8,128)S(1)}) custom-call(f32[1,8,40,128]{3,2,1,0:T(8,128)S(1)} %get-tuple-element.51.refs_0_, ...), custom_call_target="tpu_custom_call" | custom-call | tf_op jit(solution)/shard_map/pallas_call | solution.py:139
  82.1 6.6 %all-to-all-start = ((f32[128,8,128]{2,1,0:T(8,128)}), f32[128,8,128]{2,1,0:T(8,128)S(1)}, u32[]{:S(2)}, u32[]{:S(2)}) async-start(f32[128,8,128]{2,1,0:T(8,128)} %get-tuple-element.59), calls=%async_computation | async-start | bytes 1048576 | tf_op jit(solution)/shard_map/all_to_all | solution.py:751
  88.8 3.7 %collective-permute-start.12 = (f32[568,128]{1,0:T(8,128)S(1)}, f32[568,128]{1,0:T(8,128)S(1)}, u32[]{:S(2)}, u32[]{:S(2)}) collective-permute-start(f32[568,128]{1,0:T(8,128)S(1)} %get-tuple-element.68), channel_id=1, source_target_pairs={{0,1},{1,2},{2,3},{3,4},{4,5},{5,6},{6,7},{8,9},{9,10},{10,11},{11... | collective-permute-start | bytes 872456 | tf_op jit(solution)/shard_map/ppermute | solution.py:301
  92.4 2.1 %collective-permute-start.13 = (f32[568,128]{1,0:T(8,128)S(1)}, f32[568,128]{1,0:T(8,128)S(1)}, u32[]{:S(2)}, u32[]{:S(2)}) collective-permute-start(f32[568,128]{1,0:T(8,128)S(1)} %get-tuple-element.69), channel_id=1, source_target_pairs={{1,0},{2,1},{3,2},{4,3},{5,4},{6,5},{7,6},{9,8},{10,9},{11,10},{12... | collective-permute-start | bytes 872456 | tf_op jit(solution)/shard_map/ppermute | solution.py:301
  94.5 0.1 pad_add_fusion.refs_0_
  94.6 0.0 all-gather.3.cloned.1.call-done
  94.6 0.0 copy-start
  94.6 1.2 copy-done
  95.8 4.2 %shard_map.58 = (f32[448,32,128]{2,1,0:T(8,128)}, f32[448,32,128]{2,1,0:T(8,128)}) custom-call(f32[128,16,128]{2,1,0:T(8,128)S(1)} %bitcast.10), custom_call_target="tpu_custom_call" | custom-call | tf_op jit(solution)/shard_map/pallas_call | solution.py:139
  100.1 0.0 collective-permute-done.12.refs_8_
  100.1 2.2 %collective-permute-done.13.refs_9_ = f32[568,128]{1,0:T(8,128)S(1)} collective-permute-done((f32[568,128]{1,0:T(8,128)S(1)}, f32[568,128]{1,0:T(8,128)S(1)}, u32[]{:S(2)}, u32[]{:S(2)}) %collective-permute-start.13) | collective-permute-done | bytes 290848 | tf_op jit(solution)/shard_map/ppermute | solution.py:301
  102.3 0.0 all-to-all-done.refs_5_
  102.3 15.4 %shard_map.59 = (f32[16,32,128]{2,1,0:T(8,128)}, f32[16,32,128]{2,1,0:T(8,128)}) custom-call(s32[3]{0:T(128)S(1)} %pad_add_fusion.refs_0_, f32[448,32,128]{2,1,0:T(8,128)} %get-tuple-element.62.refs_1_, f32[359,40,128]{2,1,0:T(8,128)} %get-tuple-element.63.refs_2_, f32[150,48,256]{2,1,0:T(8,128)} %get-tuple-element.64.refs_3_, ...), custom_call_target="tpu_custom_call" | custom-call | tf_op jit(solution)/shard_map/pallas_call | solution.py:139
Async XLA Ops:
  7.2 87.5 %all-gather.3.cloned.1.call-start = ((), (), s32[]{:S(2)}) async-start(), calls=%async_computation.1 | async-start | bytes 1056768 | tf_op jit(solution)/shard_map/all_gather | solution.py:731
  8.6 6.5 %collective-permute-start = (f32[296,128]{1,0:T(8,128)S(1)}, f32[296,128]{1,0:T(8,128)S(1)}, u32[]{:S(2)}, u32[]{:S(2)}) collective-permute-start(f32[296,128]{1,0:T(8,128)S(1)} %get-tuple-element.37), channel_id=1, source_target_pairs={{0,32},{32,64},{64,96},{1,33},{33,65},{65,97},{2,34},{34,66},{66,9... | collective-permute-start | bytes 454664 | tf_op jit(solution)/shard_map/ppermute | solution.py:301
  12.6 6.4 %collective-permute-start.1 = (f32[296,128]{1,0:T(8,128)S(1)}, f32[296,128]{1,0:T(8,128)S(1)}, u32[]{:S(2)}, u32[]{:S(2)}) collective-permute-start(f32[296,128]{1,0:T(8,128)S(1)} %get-tuple-element.38), channel_id=1, source_target_pairs={{32,0},{64,32},{96,64},{33,1},{65,33},{97,65},{34,2},{66,34},{98,6... | collective-permute-start | bytes 454664 | tf_op jit(solution)/shard_map/ppermute | solution.py:301
  19.9 10.9 %collective-permute-start.3 = (f32[800,128]{1,0:T(8,128)S(1)}, f32[800,128]{1,0:T(8,128)S(1)}, u32[]{:S(2)}, u32[]{:S(2)}) collective-permute-start(f32[800,128]{1,0:T(8,128)S(1)} %get-tuple-element.44), channel_id=1, source_target_pairs={{1,0},{2,1},{3,2},{4,3},{5,4},{6,5},{7,6},{9,8},{10,9},{11,10},{12... | collective-permute-start | bytes 1228808 | tf_op jit(solution)/shard_map/ppermute | solution.py:301
  23.7 8.3 %collective-permute-start.2 = (f32[800,128]{1,0:T(8,128)S(1)}, f32[800,128]{1,0:T(8,128)S(1)}, u32[]{:S(2)}, u32[]{:S(2)}) collective-permute-start(f32[800,128]{1,0:T(8,128)S(1)} %get-tuple-element.43), channel_id=1, source_target_pairs={{0,1},{1,2},{2,3},{3,4},{4,5},{5,6},{6,7},{8,9},{9,10},{10,11},{11... | collective-permute-start | bytes 1228808 | tf_op jit(solution)/shard_map/ppermute | solution.py:301
  33.3 5.3 %collective-permute-start.4 = (f32[280,128]{1,0:T(8,128)S(1)}, f32[280,128]{1,0:T(8,128)S(1)}, u32[]{:S(2)}, u32[]{:S(2)}) collective-permute-start(f32[280,128]{1,0:T(8,128)S(1)} %get-tuple-element.45), channel_id=1, source_target_pairs={{0,8},{8,16},{16,24},{1,9},{9,17},{17,25},{2,10},{10,18},{18,26},{... | collective-permute-start | bytes 430088 | tf_op jit(solution)/shard_map/ppermute | solution.py:301
  36.5 6.3 %collective-permute-start.5 = (f32[280,128]{1,0:T(8,128)S(1)}, f32[280,128]{1,0:T(8,128)S(1)}, u32[]{:S(2)}, u32[]{:S(2)}) collective-permute-start(f32[280,128]{1,0:T(8,128)S(1)} %get-tuple-element.46), channel_id=1, source_target_pairs={{8,0},{16,8},{24,16},{9,1},{17,9},{25,17},{10,2},{18,10},{26,18},{... | collective-permute-start | bytes 430088 | tf_op jit(solution)/shard_map/ppermute | solution.py:301
  48.6 4.6 %collective-permute-start.6 = (f32[160,128]{1,0:T(8,128)S(1)}, f32[160,128]{1,0:T(8,128)S(1)}, u32[]{:S(2)}, u32[]{:S(2)}) collective-permute-start(f32[160,128]{1,0:T(8,128)S(1)} %get-tuple-element.49), channel_id=1, source_target_pairs={{0,32},{32,64},{64,96},{1,33},{33,65},{65,97},{2,34},{34,66},{66,9... | collective-permute-start | bytes 245768 | tf_op jit(solution)/shard_map/ppermute | solution.py:301
  51.7 5.4 %collective-permute-start.7 = (f32[160,128]{1,0:T(8,128)S(1)}, f32[160,128]{1,0:T(8,128)S(1)}, u32[]{:S(2)}, u32[]{:S(2)}) collective-permute-start(f32[160,128]{1,0:T(8,128)S(1)} %get-tuple-element.50), channel_id=1, source_target_pairs={{32,0},{64,32},{96,64},{33,1},{65,33},{97,65},{34,2},{66,34},{98,6... | collective-permute-start | bytes 245768 | tf_op jit(solution)/shard_map/ppermute | solution.py:301
  57.2 8.6 %collective-permute-start.8 = (f32[240,128]{1,0:T(8,128)S(1)}, f32[240,128]{1,0:T(8,128)S(1)}, u32[]{:S(2)}, u32[]{:S(2)}) collective-permute-start(f32[240,128]{1,0:T(8,128)S(1)} %get-tuple-element.53), channel_id=1, source_target_pairs={{0,1},{1,2},{2,3},{3,4},{4,5},{5,6},{6,7},{8,9},{9,10},{10,11},{11... | collective-permute-start | bytes 368648 | tf_op jit(solution)/shard_map/ppermute | solution.py:301
  63.8 6.2 %collective-permute-start.9 = (f32[240,128]{1,0:T(8,128)S(1)}, f32[240,128]{1,0:T(8,128)S(1)}, u32[]{:S(2)}, u32[]{:S(2)}) collective-permute-start(f32[240,128]{1,0:T(8,128)S(1)} %get-tuple-element.54), channel_id=1, source_target_pairs={{1,0},{2,1},{3,2},{4,3},{5,4},{6,5},{7,6},{9,8},{10,9},{11,10},{12... | collective-permute-start | bytes 368648 | tf_op jit(solution)/shard_map/ppermute | solution.py:301
  70.5 4.5 %collective-permute-start.10 = (f32[128,128]{1,0:T(8,128)S(1)}, f32[128,128]{1,0:T(8,128)S(1)}, u32[]{:S(2)}, u32[]{:S(2)}) collective-permute-start(f32[128,128]{1,0:T(8,128)S(1)} %get-tuple-element.55), channel_id=1, source_target_pairs={{0,8},{8,16},{16,24},{1,9},{9,17},{17,25},{2,10},{10,18},{18,26},{... | collective-permute-start | bytes 196616 | tf_op jit(solution)/shard_map/ppermute | solution.py:301
  73.7 5.3 %collective-permute-start.11 = (f32[128,128]{1,0:T(8,128)S(1)}, f32[128,128]{1,0:T(8,128)S(1)}, u32[]{:S(2)}, u32[]{:S(2)}) collective-permute-start(f32[128,128]{1,0:T(8,128)S(1)} %get-tuple-element.56), channel_id=1, source_target_pairs={{8,0},{16,8},{24,16},{9,1},{17,9},{25,17},{10,2},{18,10},{26,18},{... | collective-permute-start | bytes 196616 | tf_op jit(solution)/shard_map/ppermute | solution.py:301
  82.1 20.2 %all-to-all-start = ((f32[128,8,128]{2,1,0:T(8,128)}), f32[128,8,128]{2,1,0:T(8,128)S(1)}, u32[]{:S(2)}, u32[]{:S(2)}) async-start(f32[128,8,128]{2,1,0:T(8,128)} %get-tuple-element.59), calls=%async_computation | async-start | bytes 1048576 | tf_op jit(solution)/shard_map/all_to_all | solution.py:751
  88.8 11.3 %collective-permute-start.12 = (f32[568,128]{1,0:T(8,128)S(1)}, f32[568,128]{1,0:T(8,128)S(1)}, u32[]{:S(2)}, u32[]{:S(2)}) collective-permute-start(f32[568,128]{1,0:T(8,128)S(1)} %get-tuple-element.68), channel_id=1, source_target_pairs={{0,1},{1,2},{2,3},{3,4},{4,5},{5,6},{6,7},{8,9},{9,10},{10,11},{11... | collective-permute-start | bytes 872456 | tf_op jit(solution)/shard_map/ppermute | solution.py:301
  92.4 9.9 %collective-permute-start.13 = (f32[568,128]{1,0:T(8,128)S(1)}, f32[568,128]{1,0:T(8,128)S(1)}, u32[]{:S(2)}, u32[]{:S(2)}) collective-permute-start(f32[568,128]{1,0:T(8,128)S(1)} %get-tuple-element.69), channel_id=1, source_target_pairs={{1,0},{2,1},{3,2},{4,3},{5,4},{6,5},{7,6},{9,8},{10,9},{11,10},{12... | collective-permute-start | bytes 872456 | tf_op jit(solution)/shard_map/ppermute | solution.py:301
  94.6 1.2 copy-start
Sparse Core Ops, SparseCore 0:
  20.0 67.2 all-gather.2

commit v5 on v4

--- a/solution.py
+++ b/solution.py
@@ -16,7 +16,7 @@
 S1, F1 = 11, 10
 Z0, X0, Y0 = 16, 32, 128
 Z1, X1, Y1 = 8, 16, 64
-ZT0, XT0 = Z0 + 2 * W0, 48
+ZT0, XT0, EVEN = Z0 + 2 * W0, 48, 24
 ZT1, XT1 = Z1 + 2 * W1, 40
 LANES = 128
 MIB = 1024 * 1024
@@ -165,16 +165,25 @@
     def narrow(self, plane):
         if not self.trim:
             return plane
-        upper, lower = plane[self.x : self.x + 8], plane[self.xt - 8 : self.xt]
-        rim = jnp.where(row_of(upper.shape) < 4, upper, lower)
-        return jnp.concatenate([plane[: self.x], rim], axis=0)
+        even, odd = plane[16:24], plane[40:48]
+        rim = jnp.where(reached(even), even, roll(odd, 4, 0))
+        return jnp.concatenate([plane[0:16], plane[24:40], rim], axis=0)
 
     def widen(self, plane):
         if not self.trim:
             return plane
-        rim = plane[self.x :]
-        upper = jnp.where(row_of(rim.shape) < 4, rim, 0.0)
-        return jnp.concatenate([plane[: self.x], upper, rim - upper], axis=0)
+        rim = plane[32:40]
+        even = jnp.where(reached(rim), rim, 0.0)
+        odd = jnp.where(reached(rim), roll(rim, 4, 0), 0.0)
+        return jnp.concatenate([plane[0:16], even, plane[16:32], odd], axis=0)
+
+
+def reached(rim):
+    return (row_of(rim.shape) < 2) | (row_of(rim.shape) >= 6)
+
+
+def every_other(first, count):
+    return pl.ds(first, count, stride=2)
 
 
 def total(counts):
@@ -195,13 +204,27 @@
 def unpack_x(items, refs, from_low, from_high, outs):
     at = 0
     for item, ref, out in zip(items, refs, outs):
-        out[:, :, item.x :, :] = jnp.zeros((item.n, item.z, item.xt - item.x, LANES), F32)
+        w = item.w
+        if item.kind == "full":
+            for first in (16, 40):
+                out[:, :, first : first + 8, :] = jnp.zeros((item.n, item.z, 8, LANES), F32)
+        else:
+            out[:, :, item.x :, :] = jnp.zeros((item.n, item.z, item.xt - item.x, LANES), F32)
         for n in range(item.n):
             for z in range(item.z):
-                out[n, z, 0 : item.x, :] = ref[n, z]
-                out[n, z, item.x : item.x + item.w, :] = from_high[at : at + item.w, :]
-                out[n, z, item.xt - item.w :, :] = from_low[at : at + item.w, :]
-                at += item.w
+                if item.kind == "full":
+                    more, less = (w + 1) // 2, w // 2
+                    out[n, z, 0:16, :] = ref[n, z, every_other(0, 16), :]
+                    out[n, z, 24:40, :] = ref[n, z, every_other(1, 16), :]
+                    out[n, z, 16 : 16 + more, :] = from_high[every_other(at, more), :]
+                    out[n, z, 40 : 40 + less, :] = from_high[every_other(at + 1, less), :]
+                    out[n, z, 24 - less : 24, :] = from_low[every_other(at + w % 2, less), :]
+                    out[n, z, 48 - more : 48, :] = from_low[every_other(at + 1 - w % 2, more), :]
+                else:
+                    out[n, z, 0 : item.x, :] = ref[n, z]
+                    out[n, z, item.x : item.x + w, :] = from_high[at : at + w, :]
+                    out[n, z, item.xt - w :, :] = from_low[at : at + w, :]
+                at += w
 
 
 def pack_z(items, refs, low, high):
@@ -337,6 +360,18 @@
     return (total(item.rows_x for item in items), LANES)
 
 
+def x_above(plane):
+    if plane.shape[0] != XT0:
+        return roll(plane, -1, 0)
+    return jnp.concatenate([plane[EVEN:], roll(plane[:EVEN], -1, 0)], axis=0)
+
+
+def x_below(plane):
+    if plane.shape[0] != XT0:
+        return roll(plane, 1, 0)
+    return jnp.concatenate([roll(plane[EVEN:], 1, 0), plane[:EVEN]], axis=0)
+
+
 def couple(s, m, r, cx, cy, cz, first, last, step, edges=False, start=None):
     planes, rows, lanes = s.shape
 
@@ -345,7 +380,7 @@
 
     def one(z, below, above):
         here = s[z]
-        x_face = jnp.minimum(here, roll(here, -1, 0))
+        x_face = jnp.minimum(here, x_above(here))
         y_face = jnp.minimum(here, roll(here, -1, 1))
         if edges:
             x_face = jnp.where(row_of(here.shape) < rows - 1, x_face, 0.0)
@@ -353,7 +388,7 @@
         cx[z] = x_face
         cy[z] = y_face
         cz[z] = above
-        d = m[z] + below + above + x_face + roll(x_face, 1, 0) + y_face + roll(y_face, 1, 1)
+        d = m[z] + below + above + x_face + x_below(x_face) + y_face + roll(y_face, 1, 1)
         scale = DAMP / jnp.where(d > 0.0, d, 1.0)
         r[z] = scale
         if start:
@@ -376,7 +411,7 @@
         out = out + cz[z] * v[z + 1]
     if low:
         out = out + cz[z - 1] * v[z - 1]
-    out = out + x_face * roll(here, -1, 0) + roll(x_face * here, 1, 0)
+    out = out + x_face * x_above(here) + x_below(x_face * here)
     return here, out + y_face * roll(here, -1, 1) + roll(y_face * here, 1, 1)
 
 
@@ -463,16 +498,16 @@
     sweep(va, vb, op, 2, ZT0 - 2, 11)
     sweep(vb, va, op, 3, ZT0 - 3, 10)
     sweep(va, vb, op, 4, ZT0 - 4, 9)
+    rows = []
     for z in range(Z1):
-        a, b = W0 + 2 * z, W0 + 2 * z + 1
-        plane = remain(vb, op, a) + remain(vb, op, b)
-        tall[z * X0 : (z + 1) * X0, :] = plane[0:X0, 0:Y0]
-    rows = tall[pl.ds(0, Z1 * X1, stride=2), :] + tall[pl.ds(1, Z1 * X1, stride=2), :]
-    out = fold_lanes(rows, 0, LANES, 0)
+        plane = remain(vb, op, W0 + 2 * z) + remain(vb, op, W0 + 2 * z + 1)
+        rows.append(plane[0:X1, 0:Y0] + plane[EVEN : EVEN + X1, 0:Y0])
+    out = fold_lanes(jnp.concatenate(rows, axis=0), 0, LANES, 0)
     for z in range(Z1):
         g_own[0, z] = out[z * X1 : (z + 1) * X1, :]
     for z in range(Z0):
-        v_own[0, z] = vb[W0 + z, 0:X0, 0:Y0]
+        v_own[0, z, every_other(0, X1), :] = vb[W0 + z, 0:X1, 0:Y0]
+        v_own[0, z, every_other(1, X1), :] = vb[W0 + z, EVEN : EVEN + X1, 0:Y0]
     pack_x(SECOND, (g_own, v_own), low, high)
 
 
@@ -688,15 +723,14 @@
     for k in range(14):
         planes += [va1[4 + k, 0:20, :], va1[4 + k, XT1 - 4 : XT1, :]]
     flat = jnp.concatenate(planes, axis=0)
-    count = 14 * 24
     for half in range(2):
         part = spread_lanes(flat, 64 * half)
-        tall[pl.ds(0, count, stride=2), :] = part
-        tall[pl.ds(1, count, stride=2), :] = part
+        at = slice(half * LANES, (half + 1) * LANES)
         for z in range(ZT0):
             k = (z + 1) // 2
-            at = slice(half * LANES, (half + 1) * LANES)
-            v0[z, :, at] = v0[z, :, at] + tall[k * XT0 : (k + 1) * XT0, :]
+            add = part[k * EVEN : (k + 1) * EVEN, :]
+            v0[z, 0:EVEN, at] = v0[z, 0:EVEN, at] + add
+            v0[z, EVEN:, at] = v0[z, EVEN:, at] + add
     far.wait(2)
     op0 = parts(stacked0, ZT0)
     sweep(v0, vb0, op0, 1, ZT0 - 1, 12)
@@ -704,10 +738,13 @@
     sweep(v0, vb0, op0, 3, ZT0 - 3, 10)
     sweep(vb0, v0, op0, 4, ZT0 - 4, 9)
     for z in range(Z0):
-        potential[z] = v0[W0 + z, 0:X0, 0:Y0]
+        potential[z, every_other(0, X1), :] = v0[W0 + z, 0:X1, 0:Y0]
+        potential[z, every_other(1, X1), :] = v0[W0 + z, EVEN : EVEN + X1, 0:Y0]
     far.flush(0)
     for z in range(Z0):
-        residual[z] = remain(v0, op0, W0 + z)[0:X0, 0:Y0]
+        plane = remain(v0, op0, W0 + z)
+        residual[z, every_other(0, X1), :] = plane[0:X1, 0:Y0]
+        residual[z, every_other(1, X1), :] = plane[EVEN : EVEN + X1, 0:Y0]
 
 
 def shards(source, conductivity, cell_kind):

time: 125 us -> 125 us (level)
  no operation moved by 1% of the time
where the time goes in v5:
time: 125 us; the launch traced here: 124 us
  starting transfers between devices  46.6 us (37%)
  Pallas kernels  31.3 us (25%)
  waiting for transfers between devices  29.7 us (24%)
  between operations  14.2 us (11%)
  other arithmetic  1.3 us (1%)
    pallas_call x10, Pallas kernels, call(): pl.pallas_call(wrapped, out_shape=shapes, in_specs=specs, out_specs=out_s...  31.3 us
    ppermute x7, starting transfers between devices, shift(): lax.ppermute(high, axis, forward)  27.1 us
    ppermute x7, waiting for transfers between devices, shift(): lax.ppermute(low, axis, backward)  26.3 us
    ppermute x7, starting transfers between devices, shift(): lax.ppermute(low, axis, backward)  13 us
    all_to_all x1, starting transfers between devices, shards(): forcing2 = lax.all_to_all(copies, everywhere, 0, 0)  6.54 us
    ppermute x7, waiting for transfers between devices, shift(): lax.ppermute(high, axis, forward)  3.38 us
  transfers between devices with their start and end apart: 16, of which 11 were waited for; matrix products, arithmetic and copies ran while one was open for 0% of the time, Pallas kernels for 12%

profile of v5, /device:TPU:1, one launch (start us, length us, event | category | flops | bytes accessed | tf_op | source)
XLA Modules:
  0.0 124.4 jit_solution(15426519236774077595)
XLA Ops:
  7.2 0.0 all-gather.3.cloned.1.call-start
  7.2 1.2 fusion.3
  8.4 0.2 shard_map.50
  8.6 4.0 %collective-permute-start = (f32[296,128]{1,0:T(8,128)S(1)}, f32[296,128]{1,0:T(8,128)S(1)}, u32[]{:S(2)}, u32[]{:S(2)}) collective-permute-start(f32[296,128]{1,0:T(8,128)S(1)} %get-tuple-element.37), channel_id=1, source_target_pairs={{0,32},{32,64},{64,96},{1,33},{33,65},{65,97},{2,34},{34,66},{66,9... | collective-permute-start | bytes 454664 | tf_op jit(solution)/shard_map/ppermute | solution.py:324
  12.6 1.3 %collective-permute-start.1 = (f32[296,128]{1,0:T(8,128)S(1)}, f32[296,128]{1,0:T(8,128)S(1)}, u32[]{:S(2)}, u32[]{:S(2)}) collective-permute-start(f32[296,128]{1,0:T(8,128)S(1)} %get-tuple-element.38), channel_id=1, source_target_pairs={{32,0},{64,32},{96,64},{33,1},{65,33},{97,65},{34,2},{66,34},{98,6... | collective-permute-start | bytes 454664 | tf_op jit(solution)/shard_map/ppermute | solution.py:324
  13.9 1.3 %collective-permute-done.refs_4_ = f32[296,128]{1,0:T(8,128)S(1)} collective-permute-done((f32[296,128]{1,0:T(8,128)S(1)}, f32[296,128]{1,0:T(8,128)S(1)}, u32[]{:S(2)}, u32[]{:S(2)}) %collective-permute-start) | collective-permute-done | bytes 151584 | tf_op jit(solution)/shard_map/ppermute | solution.py:324
  15.2 3.8 %collective-permute-done.1.refs_5_ = f32[296,128]{1,0:T(8,128)S(1)} collective-permute-done((f32[296,128]{1,0:T(8,128)S(1)}, f32[296,128]{1,0:T(8,128)S(1)}, u32[]{:S(2)}, u32[]{:S(2)}) %collective-permute-start.1) | collective-permute-done | bytes 151584 | tf_op jit(solution)/shard_map/ppermute | solution.py:324
  19.0 0.2 shard_map.51
  19.2 0.7 shard_map.57
  19.9 0.0 all-gather.3.cloned.1.call-update
  19.9 3.8 %collective-permute-start.3 = (f32[800,128]{1,0:T(8,128)S(1)}, f32[800,128]{1,0:T(8,128)S(1)}, u32[]{:S(2)}, u32[]{:S(2)}) collective-permute-start(f32[800,128]{1,0:T(8,128)S(1)} %get-tuple-element.44), channel_id=1, source_target_pairs={{1,0},{2,1},{3,2},{4,3},{5,4},{6,5},{7,6},{9,8},{10,9},{11,10},{12... | collective-permute-start | bytes 1228808 | tf_op jit(solution)/shard_map/ppermute | solution.py:324
  23.7 3.4 %collective-permute-start.2 = (f32[800,128]{1,0:T(8,128)S(1)}, f32[800,128]{1,0:T(8,128)S(1)}, u32[]{:S(2)}, u32[]{:S(2)}) collective-permute-start(f32[800,128]{1,0:T(8,128)S(1)} %get-tuple-element.43), channel_id=1, source_target_pairs={{0,1},{1,2},{2,3},{3,4},{4,5},{5,6},{6,7},{8,9},{9,10},{10,11},{11... | collective-permute-start | bytes 1228808 | tf_op jit(solution)/shard_map/ppermute | solution.py:324
  27.2 3.7 %collective-permute-done.3.refs_5_ = f32[800,128]{1,0:T(8,128)S(1)} collective-permute-done((f32[800,128]{1,0:T(8,128)S(1)}, f32[800,128]{1,0:T(8,128)S(1)}, u32[]{:S(2)}, u32[]{:S(2)}) %collective-permute-start.3) | collective-permute-done | bytes 409632 | tf_op jit(solution)/shard_map/ppermute | solution.py:324
  30.9 1.2 collective-permute-done.2.refs_4_
  32.0 1.3 %shard_map.52 = (f32[280,128]{1,0:T(8,128)S(1)}, f32[280,128]{1,0:T(8,128)S(1)}) custom-call(f32[1,16,48,128]{3,2,1,0:T(8,128)S(1)} %get-tuple-element.39.refs_0_, f32[1,16,48,128]{3,2,1,0:T(8,128)S(1)} %get-tuple-element.40.refs_1_, f32[1,16,48,128]{3,2,1,0:T(8,128)S(1)} %get-tuple-element.41.refs_2_, f32[1,8,40,128]{3,2,1,0:T(8,128)S(1)} %get-tuple-element.42.refs_3_, ...), custom_call_target="tpu_custom_call" | custom-call | tf_op jit(solution)/shard_map/pallas_call | solution.py:139
  33.3 3.2 %collective-permute-start.4 = (f32[280,128]{1,0:T(8,128)S(1)}, f32[280,128]{1,0:T(8,128)S(1)}, u32[]{:S(2)}, u32[]{:S(2)}) collective-permute-start(f32[280,128]{1,0:T(8,128)S(1)} %get-tuple-element.45), channel_id=1, source_target_pairs={{0,8},{8,16},{16,24},{1,9},{9,17},{17,25},{2,10},{10,18},{18,26},{... | collective-permute-start | bytes 430088 | tf_op jit(solution)/shard_map/ppermute | solution.py:324
  36.5 1.3 %collective-permute-start.5 = (f32[280,128]{1,0:T(8,128)S(1)}, f32[280,128]{1,0:T(8,128)S(1)}, u32[]{:S(2)}, u32[]{:S(2)}) collective-permute-start(f32[280,128]{1,0:T(8,128)S(1)} %get-tuple-element.46), channel_id=1, source_target_pairs={{8,0},{16,8},{24,16},{9,1},{17,9},{25,17},{10,2},{18,10},{26,18},{... | collective-permute-start | bytes 430088 | tf_op jit(solution)/shard_map/ppermute | solution.py:324
  37.8 0.7 collective-permute-done.4.refs_6_
  38.6 4.2 %collective-permute-done.5.refs_7_ = f32[280,128]{1,0:T(8,128)S(1)} collective-permute-done((f32[280,128]{1,0:T(8,128)S(1)}, f32[280,128]{1,0:T(8,128)S(1)}, u32[]{:S(2)}, u32[]{:S(2)}) %collective-permute-start.5) | collective-permute-done | bytes 143392 | tf_op jit(solution)/shard_map/ppermute | solution.py:324
  42.8 5.7 %shard_map.53 = (f32[1,16,32,128]{3,2,1,0:T(8,128)S(1)}, f32[1,8,16,128]{3,2,1,0:T(8,128)S(1)}, f32[150,48,256]{2,1,0:T(8,128)}, f32[22,40,128]{2,1,0:T(8,128)S(...) custom-call(f32[1,16,48,128]{3,2,1,0:T(8,128)S(1)} %get-tuple-element.39.refs_0_, ...), custom_call_target="tpu_custom_call" | custom-call | tf_op jit(solution)/shard_map/pallas_call | solution.py:139
  48.5 3.1 %collective-permute-start.6 = (f32[160,128]{1,0:T(8,128)S(1)}, f32[160,128]{1,0:T(8,128)S(1)}, u32[]{:S(2)}, u32[]{:S(2)}) collective-permute-start(f32[160,128]{1,0:T(8,128)S(1)} %get-tuple-element.49), channel_id=1, source_target_pairs={{0,32},{32,64},{64,96},{1,33},{33,65},{65,97},{2,34},{34,66},{66,9... | collective-permute-start | bytes 245768 | tf_op jit(solution)/shard_map/ppermute | solution.py:324
  51.6 1.3 %collective-permute-start.7 = (f32[160,128]{1,0:T(8,128)S(1)}, f32[160,128]{1,0:T(8,128)S(1)}, u32[]{:S(2)}, u32[]{:S(2)}) collective-permute-start(f32[160,128]{1,0:T(8,128)S(1)} %get-tuple-element.50), channel_id=1, source_target_pairs={{32,0},{64,32},{96,64},{33,1},{65,33},{97,65},{34,2},{66,34},{98,6... | collective-permute-start | bytes 245768 | tf_op jit(solution)/shard_map/ppermute | solution.py:324
  52.9 0.2 collective-permute-done.6.refs_2_
  53.1 4.1 %collective-permute-done.7.refs_3_ = f32[160,128]{1,0:T(8,128)S(1)} collective-permute-done((f32[160,128]{1,0:T(8,128)S(1)}, f32[160,128]{1,0:T(8,128)S(1)}, u32[]{:S(2)}, u32[]{:S(2)}) %collective-permute-start.7) | collective-permute-done | bytes 81952 | tf_op jit(solution)/shard_map/ppermute | solution.py:324
  57.2 0.1 shard_map.54
  57.2 6.6 %collective-permute-start.8 = (f32[240,128]{1,0:T(8,128)S(1)}, f32[240,128]{1,0:T(8,128)S(1)}, u32[]{:S(2)}, u32[]{:S(2)}) collective-permute-start(f32[240,128]{1,0:T(8,128)S(1)} %get-tuple-element.53), channel_id=1, source_target_pairs={{0,1},{1,2},{2,3},{3,4},{4,5},{5,6},{6,7},{8,9},{9,10},{10,11},{11... | collective-permute-start | bytes 368648 | tf_op jit(solution)/shard_map/ppermute | solution.py:324
  63.8 1.9 %collective-permute-start.9 = (f32[240,128]{1,0:T(8,128)S(1)}, f32[240,128]{1,0:T(8,128)S(1)}, u32[]{:S(2)}, u32[]{:S(2)}) collective-permute-start(f32[240,128]{1,0:T(8,128)S(1)} %get-tuple-element.54), channel_id=1, source_target_pairs={{1,0},{2,1},{3,2},{4,3},{5,4},{6,5},{7,6},{9,8},{10,9},{11,10},{12... | collective-permute-start | bytes 368648 | tf_op jit(solution)/shard_map/ppermute | solution.py:324
  65.7 0.0 collective-permute-done.8.refs_2_
  65.7 4.3 %collective-permute-done.9.refs_3_ = f32[240,128]{1,0:T(8,128)S(1)} collective-permute-done((f32[240,128]{1,0:T(8,128)S(1)}, f32[240,128]{1,0:T(8,128)S(1)}, u32[]{:S(2)}, u32[]{:S(2)}) %collective-permute-start.9) | collective-permute-done | bytes 122912 | tf_op jit(solution)/shard_map/ppermute | solution.py:324
  70.0 0.5 shard_map.55
  70.5 3.2 %collective-permute-start.10 = (f32[128,128]{1,0:T(8,128)S(1)}, f32[128,128]{1,0:T(8,128)S(1)}, u32[]{:S(2)}, u32[]{:S(2)}) collective-permute-start(f32[128,128]{1,0:T(8,128)S(1)} %get-tuple-element.55), channel_id=1, source_target_pairs={{0,8},{8,16},{16,24},{1,9},{9,17},{17,25},{2,10},{10,18},{18,26},{... | collective-permute-start | bytes 196616 | tf_op jit(solution)/shard_map/ppermute | solution.py:324
  73.6 1.3 %collective-permute-start.11 = (f32[128,128]{1,0:T(8,128)S(1)}, f32[128,128]{1,0:T(8,128)S(1)}, u32[]{:S(2)}, u32[]{:S(2)}) collective-permute-start(f32[128,128]{1,0:T(8,128)S(1)} %get-tuple-element.56), channel_id=1, source_target_pairs={{8,0},{16,8},{24,16},{9,1},{17,9},{25,17},{10,2},{18,10},{26,18},{... | collective-permute-start | bytes 196616 | tf_op jit(solution)/shard_map/ppermute | solution.py:324
  74.9 0.0 collective-permute-done.10.refs_4_
  74.9 4.0 %collective-permute-done.11.refs_5_ = f32[128,128]{1,0:T(8,128)S(1)} collective-permute-done((f32[128,128]{1,0:T(8,128)S(1)}, f32[128,128]{1,0:T(8,128)S(1)}, u32[]{:S(2)}, u32[]{:S(2)}) %collective-permute-start.11) | collective-permute-done | bytes 65568 | tf_op jit(solution)/shard_map/ppermute | solution.py:324
  79.0 3.2 %shard_map.56 = (f32[8,40,128]{2,1,0:T(8,128)S(1)}, f32[16,48,256]{2,1,0:T(8,128)S(1)}, f32[128,8,128]{2,1,0:T(8,128)}, f32[359,40,128]{2,1,0:T(8,128)}, f32[568,128]{1,0:T(8,128)S(1)}, /*index=5*/f32[568,128]{1,0:T(8,128)S(1)}) custom-call(f32[1,8,40,128]{3,2,1,0:T(8,128)S(1)} %get-tuple-element.51.refs_0_, ...), custom_call_target="tpu_custom_call" | custom-call | tf_op jit(solution)/shard_map/pallas_call | solution.py:139
  82.2 6.5 %all-to-all-start = ((f32[128,8,128]{2,1,0:T(8,128)}), f32[128,8,128]{2,1,0:T(8,128)S(1)}, u32[]{:S(2)}, u32[]{:S(2)}) async-start(f32[128,8,128]{2,1,0:T(8,128)} %get-tuple-element.59), calls=%async_computation | async-start | bytes 1048576 | tf_op jit(solution)/shard_map/all_to_all | solution.py:788
  88.7 3.7 %collective-permute-start.12 = (f32[568,128]{1,0:T(8,128)S(1)}, f32[568,128]{1,0:T(8,128)S(1)}, u32[]{:S(2)}, u32[]{:S(2)}) collective-permute-start(f32[568,128]{1,0:T(8,128)S(1)} %get-tuple-element.68), channel_id=1, source_target_pairs={{0,1},{1,2},{2,3},{3,4},{4,5},{5,6},{6,7},{8,9},{9,10},{10,11},{11... | collective-permute-start | bytes 872456 | tf_op jit(solution)/shard_map/ppermute | solution.py:324
  92.4 2.1 %collective-permute-start.13 = (f32[568,128]{1,0:T(8,128)S(1)}, f32[568,128]{1,0:T(8,128)S(1)}, u32[]{:S(2)}, u32[]{:S(2)}) collective-permute-start(f32[568,128]{1,0:T(8,128)S(1)} %get-tuple-element.69), channel_id=1, source_target_pairs={{1,0},{2,1},{3,2},{4,3},{5,4},{6,5},{7,6},{9,8},{10,9},{11,10},{12... | collective-permute-start | bytes 872456 | tf_op jit(solution)/shard_map/ppermute | solution.py:324
  94.5 0.1 pad_add_fusion.refs_0_
  94.6 0.0 all-gather.3.cloned.1.call-done
  94.6 0.0 copy-start
  94.6 1.2 copy-done
  95.8 4.2 %shard_map.58 = (f32[448,32,128]{2,1,0:T(8,128)}, f32[448,32,128]{2,1,0:T(8,128)}) custom-call(f32[128,16,128]{2,1,0:T(8,128)S(1)} %bitcast.10), custom_call_target="tpu_custom_call" | custom-call | tf_op jit(solution)/shard_map/pallas_call | solution.py:139
  100.0 0.0 collective-permute-done.12.refs_8_
  100.0 2.2 %collective-permute-done.13.refs_9_ = f32[568,128]{1,0:T(8,128)S(1)} collective-permute-done((f32[568,128]{1,0:T(8,128)S(1)}, f32[568,128]{1,0:T(8,128)S(1)}, u32[]{:S(2)}, u32[]{:S(2)}) %collective-permute-start.13) | collective-permute-done | bytes 290848 | tf_op jit(solution)/shard_map/ppermute | solution.py:324
  102.3 0.0 all-to-all-done.refs_5_
  102.3 15.3 %shard_map.59 = (f32[16,32,128]{2,1,0:T(8,128)}, f32[16,32,128]{2,1,0:T(8,128)}) custom-call(s32[3]{0:T(128)S(1)} %pad_add_fusion.refs_0_, f32[448,32,128]{2,1,0:T(8,128)} %get-tuple-element.62.refs_1_, f32[359,40,128]{2,1,0:T(8,128)} %get-tuple-element.63.refs_2_, f32[150,48,256]{2,1,0:T(8,128)} %get-tuple-element.64.refs_3_, ...), custom_call_target="tpu_custom_call" | custom-call | tf_op jit(solution)/shard_map/pallas_call | solution.py:139
Async XLA Ops:
  7.2 87.4 %all-gather.3.cloned.1.call-start = ((), (), s32[]{:S(2)}) async-start(), calls=%async_computation.1 | async-start | bytes 1056768 | tf_op jit(solution)/shard_map/all_gather | solution.py:768
  8.6 6.5 %collective-permute-start = (f32[296,128]{1,0:T(8,128)S(1)}, f32[296,128]{1,0:T(8,128)S(1)}, u32[]{:S(2)}, u32[]{:S(2)}) collective-permute-start(f32[296,128]{1,0:T(8,128)S(1)} %get-tuple-element.37), channel_id=1, source_target_pairs={{0,32},{32,64},{64,96},{1,33},{33,65},{65,97},{2,34},{34,66},{66,9... | collective-permute-start | bytes 454664 | tf_op jit(solution)/shard_map/ppermute | solution.py:324
  12.6 6.4 %collective-permute-start.1 = (f32[296,128]{1,0:T(8,128)S(1)}, f32[296,128]{1,0:T(8,128)S(1)}, u32[]{:S(2)}, u32[]{:S(2)}) collective-permute-start(f32[296,128]{1,0:T(8,128)S(1)} %get-tuple-element.38), channel_id=1, source_target_pairs={{32,0},{64,32},{96,64},{33,1},{65,33},{97,65},{34,2},{66,34},{98,6... | collective-permute-start | bytes 454664 | tf_op jit(solution)/shard_map/ppermute | solution.py:324
  19.9 10.9 %collective-permute-start.3 = (f32[800,128]{1,0:T(8,128)S(1)}, f32[800,128]{1,0:T(8,128)S(1)}, u32[]{:S(2)}, u32[]{:S(2)}) collective-permute-start(f32[800,128]{1,0:T(8,128)S(1)} %get-tuple-element.44), channel_id=1, source_target_pairs={{1,0},{2,1},{3,2},{4,3},{5,4},{6,5},{7,6},{9,8},{10,9},{11,10},{12... | collective-permute-start | bytes 1228808 | tf_op jit(solution)/shard_map/ppermute | solution.py:324
  23.7 8.3 %collective-permute-start.2 = (f32[800,128]{1,0:T(8,128)S(1)}, f32[800,128]{1,0:T(8,128)S(1)}, u32[]{:S(2)}, u32[]{:S(2)}) collective-permute-start(f32[800,128]{1,0:T(8,128)S(1)} %get-tuple-element.43), channel_id=1, source_target_pairs={{0,1},{1,2},{2,3},{3,4},{4,5},{5,6},{6,7},{8,9},{9,10},{10,11},{11... | collective-permute-start | bytes 1228808 | tf_op jit(solution)/shard_map/ppermute | solution.py:324
  33.3 5.3 %collective-permute-start.4 = (f32[280,128]{1,0:T(8,128)S(1)}, f32[280,128]{1,0:T(8,128)S(1)}, u32[]{:S(2)}, u32[]{:S(2)}) collective-permute-start(f32[280,128]{1,0:T(8,128)S(1)} %get-tuple-element.45), channel_id=1, source_target_pairs={{0,8},{8,16},{16,24},{1,9},{9,17},{17,25},{2,10},{10,18},{18,26},{... | collective-permute-start | bytes 430088 | tf_op jit(solution)/shard_map/ppermute | solution.py:324
  36.5 6.3 %collective-permute-start.5 = (f32[280,128]{1,0:T(8,128)S(1)}, f32[280,128]{1,0:T(8,128)S(1)}, u32[]{:S(2)}, u32[]{:S(2)}) collective-permute-start(f32[280,128]{1,0:T(8,128)S(1)} %get-tuple-element.46), channel_id=1, source_target_pairs={{8,0},{16,8},{24,16},{9,1},{17,9},{25,17},{10,2},{18,10},{26,18},{... | collective-permute-start | bytes 430088 | tf_op jit(solution)/shard_map/ppermute | solution.py:324
  48.5 4.6 %collective-permute-start.6 = (f32[160,128]{1,0:T(8,128)S(1)}, f32[160,128]{1,0:T(8,128)S(1)}, u32[]{:S(2)}, u32[]{:S(2)}) collective-permute-start(f32[160,128]{1,0:T(8,128)S(1)} %get-tuple-element.49), channel_id=1, source_target_pairs={{0,32},{32,64},{64,96},{1,33},{33,65},{65,97},{2,34},{34,66},{66,9... | collective-permute-start | bytes 245768 | tf_op jit(solution)/shard_map/ppermute | solution.py:324
  51.6 5.5 %collective-permute-start.7 = (f32[160,128]{1,0:T(8,128)S(1)}, f32[160,128]{1,0:T(8,128)S(1)}, u32[]{:S(2)}, u32[]{:S(2)}) collective-permute-start(f32[160,128]{1,0:T(8,128)S(1)} %get-tuple-element.50), channel_id=1, source_target_pairs={{32,0},{64,32},{96,64},{33,1},{65,33},{97,65},{34,2},{66,34},{98,6... | collective-permute-start | bytes 245768 | tf_op jit(solution)/shard_map/ppermute | solution.py:324
  57.2 8.5 %collective-permute-start.8 = (f32[240,128]{1,0:T(8,128)S(1)}, f32[240,128]{1,0:T(8,128)S(1)}, u32[]{:S(2)}, u32[]{:S(2)}) collective-permute-start(f32[240,128]{1,0:T(8,128)S(1)} %get-tuple-element.53), channel_id=1, source_target_pairs={{0,1},{1,2},{2,3},{3,4},{4,5},{5,6},{6,7},{8,9},{9,10},{10,11},{11... | collective-permute-start | bytes 368648 | tf_op jit(solution)/shard_map/ppermute | solution.py:324
  63.8 6.2 %collective-permute-start.9 = (f32[240,128]{1,0:T(8,128)S(1)}, f32[240,128]{1,0:T(8,128)S(1)}, u32[]{:S(2)}, u32[]{:S(2)}) collective-permute-start(f32[240,128]{1,0:T(8,128)S(1)} %get-tuple-element.54), channel_id=1, source_target_pairs={{1,0},{2,1},{3,2},{4,3},{5,4},{6,5},{7,6},{9,8},{10,9},{11,10},{12... | collective-permute-start | bytes 368648 | tf_op jit(solution)/shard_map/ppermute | solution.py:324
  70.5 4.5 %collective-permute-start.10 = (f32[128,128]{1,0:T(8,128)S(1)}, f32[128,128]{1,0:T(8,128)S(1)}, u32[]{:S(2)}, u32[]{:S(2)}) collective-permute-start(f32[128,128]{1,0:T(8,128)S(1)} %get-tuple-element.55), channel_id=1, source_target_pairs={{0,8},{8,16},{16,24},{1,9},{9,17},{17,25},{2,10},{10,18},{18,26},{... | collective-permute-start | bytes 196616 | tf_op jit(solution)/shard_map/ppermute | solution.py:324
  73.6 5.3 %collective-permute-start.11 = (f32[128,128]{1,0:T(8,128)S(1)}, f32[128,128]{1,0:T(8,128)S(1)}, u32[]{:S(2)}, u32[]{:S(2)}) collective-permute-start(f32[128,128]{1,0:T(8,128)S(1)} %get-tuple-element.56), channel_id=1, source_target_pairs={{8,0},{16,8},{24,16},{9,1},{17,9},{25,17},{10,2},{18,10},{26,18},{... | collective-permute-start | bytes 196616 | tf_op jit(solution)/shard_map/ppermute | solution.py:324
  82.2 20.1 %all-to-all-start = ((f32[128,8,128]{2,1,0:T(8,128)}), f32[128,8,128]{2,1,0:T(8,128)S(1)}, u32[]{:S(2)}, u32[]{:S(2)}) async-start(f32[128,8,128]{2,1,0:T(8,128)} %get-tuple-element.59), calls=%async_computation | async-start | bytes 1048576 | tf_op jit(solution)/shard_map/all_to_all | solution.py:788
  88.7 11.3 %collective-permute-start.12 = (f32[568,128]{1,0:T(8,128)S(1)}, f32[568,128]{1,0:T(8,128)S(1)}, u32[]{:S(2)}, u32[]{:S(2)}) collective-permute-start(f32[568,128]{1,0:T(8,128)S(1)} %get-tuple-element.68), channel_id=1, source_target_pairs={{0,1},{1,2},{2,3},{3,4},{4,5},{5,6},{6,7},{8,9},{9,10},{10,11},{11... | collective-permute-start | bytes 872456 | tf_op jit(solution)/shard_map/ppermute | solution.py:324
  92.4 9.9 %collective-permute-start.13 = (f32[568,128]{1,0:T(8,128)S(1)}, f32[568,128]{1,0:T(8,128)S(1)}, u32[]{:S(2)}, u32[]{:S(2)}) collective-permute-start(f32[568,128]{1,0:T(8,128)S(1)} %get-tuple-element.69), channel_id=1, source_target_pairs={{1,0},{2,1},{3,2},{4,3},{5,4},{6,5},{7,6},{9,8},{10,9},{11,10},{12... | collective-permute-start | bytes 872456 | tf_op jit(solution)/shard_map/ppermute | solution.py:324
  94.6 1.2 copy-start
Sparse Core Ops, SparseCore 0:
  20.1 67.2 all-gather.2

commit v6 on v5

--- a/solution.py
+++ b/solution.py
@@ -324,7 +324,7 @@
     return lax.ppermute(high, axis, forward), lax.ppermute(low, axis, backward)
 
 
-def exchange(items, arrays, low, high, beside=None):
+def exchange(items, arrays, low, high):
     count = len(items)
     from_low, from_high = shift(low, high, "gx")
     shapes = [(item.n, item.z, item.xt, LANES) for item in items]
@@ -336,7 +336,6 @@
         pack_z(items, outs, c, d)
 
     *arrays, low, high = call(after_x, shapes + [message] * 2, [], *arrays, from_low, from_high)
-    extra = beside(low) if beside else None
     z_low, z_high = shift(low, high, "gz")
     message = (total(item.rows_y for item in items), LANES)
 
@@ -344,8 +343,7 @@
         pack_y(items, planes_of(items, refs[:count], *refs[count : count + 2]), *refs[count + 2 :])
 
     low, high = call(after_z, [message] * 2, [], *arrays, z_low, z_high)
-    received = (*arrays, z_low, z_high, *shift(low, high, "gy"))
-    return (received, extra) if beside else received
+    return (*arrays, z_low, z_high, *shift(low, high, "gy"))
 
 
 STIFFNESS = Item(1, Z0, X0, XT0, W0, "full", True, edge=1)
@@ -445,7 +443,7 @@
     loop(first, last, step, 4)
 
 
-def prepare(far, stiffness, forcing, mass, coarse, low, high, tall):
+def prepare(far, place, stiffness, forcing, mass, coarse, low, high, packed2, tall):
     out = None
     for ref, scale, target in ((stiffness, 0.25, 0), (mass, 1.0, Y1)):
         for z in range(Z1):
@@ -456,16 +454,13 @@
     for z in range(Z1):
         coarse[0, z] = out[z * X1 : (z + 1) * X1, :]
     pack_x(FIRST, (stiffness, forcing, mass, coarse), low, high)
-
-
-def prepare_coarse(far, coarse, packed2, tall):
     for part, scale in ((0, 0.25), (1, 1.0)):
         packed2[part * 8 : part * 8 + 8, :] = scale * pack_coarse(
-            lambda z: coarse[0, z], part * Y1, tall
+            place, lambda z: coarse[0, z], part * Y1, tall
         )
 
 
-def pack_coarse(plane, first, tall):
+def pack_coarse(place, plane, first, tall):
     for z in range(Z1 // 2):
         tall[z * X1 : (z + 1) * X1, :] = plane(2 * z) + plane(2 * z + 1)
     count = Z1 // 2 * X1 // 2
@@ -474,7 +469,7 @@
     for z in range(Z1 // 2):
         part = rows[z * X1 // 2 : (z + 1) * X1 // 2, :]
         out = out + fold_lanes(part, first, Y1, z * Y1 // 2)
-    return out
+    return pltpu.roll(out, place[2] * 32, 1)
 
 
 def parts(ref, planes, count=5):
@@ -512,7 +507,7 @@
 
 
 def presmooth1(
-    far, g_x, v0_x, z_low, z_high, from_low, from_high, s, m,
+    far, place, g_x, v0_x, z_low, z_high, from_low, from_high, s, m,
     v_own, v0, copies, op, low, high,
     va, vb, tall,
 ):
@@ -528,7 +523,7 @@
     sweep(va, vb, op, 4, ZT1 - 4, 10)
     sweep(vb, va, op, 5, ZT1 - 5, 10)
     sweep(va, vb, op, 6, ZT1 - 6, 10)
-    packed = pack_coarse(lambda z: remain(vb, op, W1 + z)[0:X1, :], 0, tall)
+    packed = pack_coarse(place, lambda z: remain(vb, op, W1 + z)[0:X1, :], 0, tall)
     for d in range(copies.shape[0]):
         copies[d] = packed
     for z in range(Z1):
@@ -551,13 +546,12 @@
 
     def body(step):
         gz, gx = step // 4, step % 4
+        tiles = [blocks[step * 4 + gy, first : first + 8, :] for gy in range(4)]
         for z in range(4):
-            plane = None
-            for gy in range(4):
-                block = blocks[step * 4 + gy, first : first + 8, :]
-                moved = roll(block, (gy - z) * 32, 1)
-                plane = moved if plane is None else jnp.where(group == gy, moved, plane)
-            out[gz * 4 + z, pl.ds(pl.multiple_of(gx * 8, 8), 8), :] = plane
+            plane = tiles[0]
+            for gy in range(1, 4):
+                plane = jnp.where(group == (z + gy) % 4, tiles[gy], plane)
+            out[gz * 4 + z, pl.ds(pl.multiple_of(gx * 8, 8), 8), :] = roll(plane, -32 * z, 1)
 
     loop(0, 32, body, 4)
 
@@ -758,16 +752,14 @@
     stiffness = conductivity * wet
     mass = 0.005 * stiffness + 8.0 * stiffness * surface + 0.02 * (1.0 - wet)
     fields = [array.reshape(own0) for array in (stiffness, source * wet, mass)]
-    coarse, low, high = call(
-        prepare, [own1] + [x_message(FIRST)] * 2, [(Z1 * X0, LANES)], *fields
+    coarse, low, high, packed2 = call(
+        prepare,
+        [own1] + [x_message(FIRST)] * 2 + [(16, LANES)],
+        [(Z1 * X0, LANES)],
+        *fields, place=place,
     )
-
-    def gather_coarse(message):
-        block, _ = lax.optimization_barrier((coarse, message))
-        (packed2,) = call(prepare_coarse, [(16, LANES)], [(Z1 // 2 * X1, LANES)], block)
-        return lax.all_gather(packed2, everywhere, axis=0)
-
-    received, operators2 = exchange(FIRST, (*fields, coarse), low, high, gather_coarse)
+    operators2 = lax.all_gather(packed2, everywhere, axis=0)
+    received = exchange(FIRST, (*fields, coarse), low, high)
     v0, g1, op0, s1, m1, low, high = call(
         presmooth0,
         [own0, own1, (5 * ZT0, XT0, 2 * LANES)] + [ext1] * 2 + [x_message(SECOND)] * 2,
@@ -782,7 +774,7 @@
         presmooth1,
         [(Z1, XT1, LANES), (Z0, XT0, 2 * LANES), (devices, 8, LANES), stack1] + [message] * 2,
         [ext1] * 2 + [(Z1 // 2 * X1, LANES)],
-        *received, s1, m1, far_out=(3,),
+        *received, s1, m1, place=place, far_out=(3,),
     )
     _, operators2 = lax.optimization_barrier((copies, operators2))
     forcing2 = lax.all_to_all(copies, everywhere, 0, 0)

time: 125 us -> 127 us (1.016)
  waiting for transfers between devices: 29.7 us -> 32.5 us
    ppermute x7, starting transfers between devices: 13 us -> 11.1 us  [shift(): lax.ppermute(low, axis, backward)]
    ppermute x7, waiting for transfers between devices: 3.38 us -> 5.15 us  [shift(): lax.ppermute(high, axis, forward)]
    ppermute x7, starting transfers between devices: 27.1 us -> 28.5 us  [shift(): lax.ppermute(high, axis, forward)]
    pallas_call x10 -> x9, Pallas kernels: 31.3 us -> 31.9 us  [call(): pl.pallas_call(wrapped, out_shape=shapes, in_specs=specs, out_specs=out_s...]
where the time goes in v6:
time: 127 us; the launch traced here: 126 us
  starting transfers between devices  45.4 us (36%)
  waiting for transfers between devices  32.5 us (26%)
  Pallas kernels  31.9 us (25%)
  between operations  14.3 us (11%)
  other arithmetic  1.31 us (1%)
    pallas_call x9, Pallas kernels, call(): pl.pallas_call(wrapped, out_shape=shapes, in_specs=specs, out_specs=out_s...  31.9 us
    ppermute x7, starting transfers between devices, shift(): lax.ppermute(high, axis, forward)  28.5 us
    ppermute x7, waiting for transfers between devices, shift(): lax.ppermute(low, axis, backward)  27.3 us
    ppermute x7, starting transfers between devices, shift(): lax.ppermute(low, axis, backward)  11.1 us
    all_to_all x1, starting transfers between devices, shards(): forcing2 = lax.all_to_all(copies, everywhere, 0, 0)  5.71 us
    ppermute x7, waiting for transfers between devices, shift(): lax.ppermute(high, axis, forward)  5.15 us
  transfers between devices with their start and end apart: 16, of which 11 were waited for; matrix products, arithmetic and copies ran while one was open for 0% of the time, Pallas kernels for 12%

profile of v6, /device:TPU:1, one launch (start us, length us, event | category | flops | bytes accessed | tf_op | source)
XLA Modules:
  0.0 126.5 jit_solution(2602531499053891595)
XLA Ops:
  7.2 0.0 all-gather.3.cloned.1.call-start
  7.2 0.1 pad_add_fusion.refs_0_
  7.3 1.2 fusion.3
  8.5 1.5 %shard_map.50 = (f32[1,8,16,128]{3,2,1,0:T(8,128)S(1)}, f32[296,128]{1,0:T(8,128)S(1)}, f32[296,128]{1,0:T(8,128)S(1)}, f32[16,128]{1,0:T(8,128)}) custom-call(s32[3]{0:T(128)S(1)} %pad_add_fusion.refs_0_, f32[1,16,32,128]{3,2,1,0:T(8,128)S(1)} %get-tuple-element.71.refs_1_.refs_0_, f32[1,16,32,128]{3,2,1,0:T(8,128)S(1)} %get-tuple-element.72.refs_2_.refs_1_, ...), custom_call_target="tpu_custom_call" | custom-call | tf_op jit(solution)/shard_map/pallas_call | solution.py:139
  10.0 0.0 all-gather.3.cloned.1.call-update
  10.1 4.0 %collective-permute-start = (f32[296,128]{1,0:T(8,128)S(1)}, f32[296,128]{1,0:T(8,128)S(1)}, u32[]{:S(2)}, u32[]{:S(2)}) collective-permute-start(f32[296,128]{1,0:T(8,128)S(1)} %get-tuple-element.37), channel_id=1, source_target_pairs={{0,32},{32,64},{64,96},{1,33},{33,65},{65,97},{2,34},{34,66},{66,9... | collective-permute-start | bytes 454664 | tf_op jit(solution)/shard_map/ppermute | solution.py:324
  14.0 1.3 %collective-permute-start.1 = (f32[296,128]{1,0:T(8,128)S(1)}, f32[296,128]{1,0:T(8,128)S(1)}, u32[]{:S(2)}, u32[]{:S(2)}) collective-permute-start(f32[296,128]{1,0:T(8,128)S(1)} %get-tuple-element.38), channel_id=1, source_target_pairs={{32,0},{64,32},{96,64},{33,1},{65,33},{97,65},{34,2},{66,34},{98,6... | collective-permute-start | bytes 454664 | tf_op jit(solution)/shard_map/ppermute | solution.py:324
  15.3 1.3 %collective-permute-done.refs_4_ = f32[296,128]{1,0:T(8,128)S(1)} collective-permute-done((f32[296,128]{1,0:T(8,128)S(1)}, f32[296,128]{1,0:T(8,128)S(1)}, u32[]{:S(2)}, u32[]{:S(2)}) %collective-permute-start) | collective-permute-done | bytes 151584 | tf_op jit(solution)/shard_map/ppermute | solution.py:324
  16.6 3.8 %collective-permute-done.1.refs_5_ = f32[296,128]{1,0:T(8,128)S(1)} collective-permute-done((f32[296,128]{1,0:T(8,128)S(1)}, f32[296,128]{1,0:T(8,128)S(1)}, u32[]{:S(2)}, u32[]{:S(2)}) %collective-permute-start.1) | collective-permute-done | bytes 151584 | tf_op jit(solution)/shard_map/ppermute | solution.py:324
  20.4 0.2 shard_map.51
  20.6 5.3 %collective-permute-start.2 = (f32[800,128]{1,0:T(8,128)S(1)}, f32[800,128]{1,0:T(8,128)S(1)}, u32[]{:S(2)}, u32[]{:S(2)}) collective-permute-start(f32[800,128]{1,0:T(8,128)S(1)} %get-tuple-element.43), channel_id=1, source_target_pairs={{0,1},{1,2},{2,3},{3,4},{4,5},{5,6},{6,7},{8,9},{9,10},{10,11},{11... | collective-permute-start | bytes 1228808 | tf_op jit(solution)/shard_map/ppermute | solution.py:324
  25.9 1.9 %collective-permute-start.3 = (f32[800,128]{1,0:T(8,128)S(1)}, f32[800,128]{1,0:T(8,128)S(1)}, u32[]{:S(2)}, u32[]{:S(2)}) collective-permute-start(f32[800,128]{1,0:T(8,128)S(1)} %get-tuple-element.44), channel_id=1, source_target_pairs={{1,0},{2,1},{3,2},{4,3},{5,4},{6,5},{7,6},{9,8},{10,9},{11,10},{12... | collective-permute-start | bytes 1228808 | tf_op jit(solution)/shard_map/ppermute | solution.py:324
  27.9 3.0 %collective-permute-done.2.refs_4_ = f32[800,128]{1,0:T(8,128)S(1)} collective-permute-done((f32[800,128]{1,0:T(8,128)S(1)}, f32[800,128]{1,0:T(8,128)S(1)}, u32[]{:S(2)}, u32[]{:S(2)}) %collective-permute-start.2) | collective-permute-done | bytes 409632 | tf_op jit(solution)/shard_map/ppermute | solution.py:324
  30.8 4.4 %collective-permute-done.3.refs_5_ = f32[800,128]{1,0:T(8,128)S(1)} collective-permute-done((f32[800,128]{1,0:T(8,128)S(1)}, f32[800,128]{1,0:T(8,128)S(1)}, u32[]{:S(2)}, u32[]{:S(2)}) %collective-permute-start.3) | collective-permute-done | bytes 409632 | tf_op jit(solution)/shard_map/ppermute | solution.py:324
  35.2 1.3 %shard_map.52 = (f32[280,128]{1,0:T(8,128)S(1)}, f32[280,128]{1,0:T(8,128)S(1)}) custom-call(f32[1,16,48,128]{3,2,1,0:T(8,128)S(1)} %get-tuple-element.39.refs_0_, f32[1,16,48,128]{3,2,1,0:T(8,128)S(1)} %get-tuple-element.40.refs_1_, f32[1,16,48,128]{3,2,1,0:T(8,128)S(1)} %get-tuple-element.41.refs_2_, f32[1,8,40,128]{3,2,1,0:T(8,128)S(1)} %get-tuple-element.42.refs_3_, ...), custom_call_target="tpu_custom_call" | custom-call | tf_op jit(solution)/shard_map/pallas_call | solution.py:139
  36.5 3.2 %collective-permute-start.4 = (f32[280,128]{1,0:T(8,128)S(1)}, f32[280,128]{1,0:T(8,128)S(1)}, u32[]{:S(2)}, u32[]{:S(2)}) collective-permute-start(f32[280,128]{1,0:T(8,128)S(1)} %get-tuple-element.45), channel_id=1, source_target_pairs={{0,8},{8,16},{16,24},{1,9},{9,17},{17,25},{2,10},{10,18},{18,26},{... | collective-permute-start | bytes 430088 | tf_op jit(solution)/shard_map/ppermute | solution.py:324
  39.7 1.3 %collective-permute-start.5 = (f32[280,128]{1,0:T(8,128)S(1)}, f32[280,128]{1,0:T(8,128)S(1)}, u32[]{:S(2)}, u32[]{:S(2)}) collective-permute-start(f32[280,128]{1,0:T(8,128)S(1)} %get-tuple-element.46), channel_id=1, source_target_pairs={{8,0},{16,8},{24,16},{9,1},{17,9},{25,17},{10,2},{18,10},{26,18},{... | collective-permute-start | bytes 430088 | tf_op jit(solution)/shard_map/ppermute | solution.py:324
  41.0 0.7 collective-permute-done.4.refs_6_
  41.8 3.8 %collective-permute-done.5.refs_7_ = f32[280,128]{1,0:T(8,128)S(1)} collective-permute-done((f32[280,128]{1,0:T(8,128)S(1)}, f32[280,128]{1,0:T(8,128)S(1)}, u32[]{:S(2)}, u32[]{:S(2)}) %collective-permute-start.5) | collective-permute-done | bytes 143392 | tf_op jit(solution)/shard_map/ppermute | solution.py:324
  45.6 5.7 %shard_map.53 = (f32[1,16,32,128]{3,2,1,0:T(8,128)S(1)}, f32[1,8,16,128]{3,2,1,0:T(8,128)S(1)}, f32[150,48,256]{2,1,0:T(8,128)}, f32[22,40,128]{2,1,0:T(8,128)S(...) custom-call(f32[1,16,48,128]{3,2,1,0:T(8,128)S(1)} %get-tuple-element.39.refs_0_, ...), custom_call_target="tpu_custom_call" | custom-call | tf_op jit(solution)/shard_map/pallas_call | solution.py:139
  51.3 3.5 %collective-permute-start.6 = (f32[160,128]{1,0:T(8,128)S(1)}, f32[160,128]{1,0:T(8,128)S(1)}, u32[]{:S(2)}, u32[]{:S(2)}) collective-permute-start(f32[160,128]{1,0:T(8,128)S(1)} %get-tuple-element.49), channel_id=1, source_target_pairs={{0,32},{32,64},{64,96},{1,33},{33,65},{65,97},{2,34},{34,66},{66,9... | collective-permute-start | bytes 245768 | tf_op jit(solution)/shard_map/ppermute | solution.py:324
  54.8 1.3 %collective-permute-start.7 = (f32[160,128]{1,0:T(8,128)S(1)}, f32[160,128]{1,0:T(8,128)S(1)}, u32[]{:S(2)}, u32[]{:S(2)}) collective-permute-start(f32[160,128]{1,0:T(8,128)S(1)} %get-tuple-element.50), channel_id=1, source_target_pairs={{32,0},{64,32},{96,64},{33,1},{65,33},{97,65},{34,2},{66,34},{98,6... | collective-permute-start | bytes 245768 | tf_op jit(solution)/shard_map/ppermute | solution.py:324
  56.1 0.2 collective-permute-done.6.refs_2_
  56.3 3.7 %collective-permute-done.7.refs_3_ = f32[160,128]{1,0:T(8,128)S(1)} collective-permute-done((f32[160,128]{1,0:T(8,128)S(1)}, f32[160,128]{1,0:T(8,128)S(1)}, u32[]{:S(2)}, u32[]{:S(2)}) %collective-permute-start.7) | collective-permute-done | bytes 81952 | tf_op jit(solution)/shard_map/ppermute | solution.py:324
  60.0 0.1 shard_map.54
  60.1 5.6 %collective-permute-start.8 = (f32[240,128]{1,0:T(8,128)S(1)}, f32[240,128]{1,0:T(8,128)S(1)}, u32[]{:S(2)}, u32[]{:S(2)}) collective-permute-start(f32[240,128]{1,0:T(8,128)S(1)} %get-tuple-element.53), channel_id=1, source_target_pairs={{0,1},{1,2},{2,3},{3,4},{4,5},{5,6},{6,7},{8,9},{9,10},{10,11},{11... | collective-permute-start | bytes 368648 | tf_op jit(solution)/shard_map/ppermute | solution.py:324
  65.7 1.9 %collective-permute-start.9 = (f32[240,128]{1,0:T(8,128)S(1)}, f32[240,128]{1,0:T(8,128)S(1)}, u32[]{:S(2)}, u32[]{:S(2)}) collective-permute-start(f32[240,128]{1,0:T(8,128)S(1)} %get-tuple-element.54), channel_id=1, source_target_pairs={{1,0},{2,1},{3,2},{4,3},{5,4},{6,5},{7,6},{9,8},{10,9},{11,10},{12... | collective-permute-start | bytes 368648 | tf_op jit(solution)/shard_map/ppermute | solution.py:324
  67.7 0.0 collective-permute-done.8.refs_2_.refs_3_
  67.7 4.9 %collective-permute-done.9.refs_3_.refs_4_ = f32[240,128]{1,0:T(8,128)S(1)} collective-permute-done((f32[240,128]{1,0:T(8,128)S(1)}, f32[240,128]{1,0:T(8,128)S(1)}, u32[]{:S(2)}, u32[]{:S(2)}) %collective-permute-start.9) | collective-permute-done | bytes 122912 | tf_op jit(solution)/shard_map/ppermute | solution.py:324
  72.6 0.5 shard_map.55
  73.1 3.2 %collective-permute-start.10 = (f32[128,128]{1,0:T(8,128)S(1)}, f32[128,128]{1,0:T(8,128)S(1)}, u32[]{:S(2)}, u32[]{:S(2)}) collective-permute-start(f32[128,128]{1,0:T(8,128)S(1)} %get-tuple-element.55), channel_id=1, source_target_pairs={{0,8},{8,16},{16,24},{1,9},{9,17},{17,25},{2,10},{10,18},{18,26},{... | collective-permute-start | bytes 196616 | tf_op jit(solution)/shard_map/ppermute | solution.py:324
  76.3 1.3 %collective-permute-start.11 = (f32[128,128]{1,0:T(8,128)S(1)}, f32[128,128]{1,0:T(8,128)S(1)}, u32[]{:S(2)}, u32[]{:S(2)}) collective-permute-start(f32[128,128]{1,0:T(8,128)S(1)} %get-tuple-element.56), channel_id=1, source_target_pairs={{8,0},{16,8},{24,16},{9,1},{17,9},{25,17},{10,2},{18,10},{26,18},{... | collective-permute-start | bytes 196616 | tf_op jit(solution)/shard_map/ppermute | solution.py:324
  77.6 0.0 collective-permute-done.10.refs_5_
  77.6 3.7 %collective-permute-done.11.refs_6_ = f32[128,128]{1,0:T(8,128)S(1)} collective-permute-done((f32[128,128]{1,0:T(8,128)S(1)}, f32[128,128]{1,0:T(8,128)S(1)}, u32[]{:S(2)}, u32[]{:S(2)}) %collective-permute-start.11) | collective-permute-done | bytes 65568 | tf_op jit(solution)/shard_map/ppermute | solution.py:324
  81.3 3.7 %shard_map.56 = (f32[8,40,128]{2,1,0:T(8,128)S(1)}, f32[16,48,256]{2,1,0:T(8,128)S(1)}, f32[128,8,128]{2,1,0:T(8,128)}, f32[359,40,128]{2,1,0:T(8,128)}, f32[568,128]{1,0:T(8,128)S(1)}, /*index=5*/f32[568,128]{1,0:T(8,128)S(1)}) custom-call(s32[3]{0:T(128)S(1)} %pad_add_fusion.refs_0_, f32[1,8,40,128]{3,2,1,0:T(8,128)S(1)} %get-tuple-element.51.refs_0_.refs_1_, ...), custom_call_target="tpu_custom_call" | custom-call | tf_op jit(solution)/shard_map/pallas_call | solution.py:139
  85.1 5.7 %all-to-all-start = ((f32[128,8,128]{2,1,0:T(8,128)}), f32[128,8,128]{2,1,0:T(8,128)S(1)}, u32[]{:S(2)}, u32[]{:S(2)}) async-start(f32[128,8,128]{2,1,0:T(8,128)} %get-tuple-element.59), calls=%async_computation | async-start | bytes 1048576 | tf_op jit(solution)/shard_map/all_to_all | solution.py:780
  90.8 3.7 %collective-permute-start.12 = (f32[568,128]{1,0:T(8,128)S(1)}, f32[568,128]{1,0:T(8,128)S(1)}, u32[]{:S(2)}, u32[]{:S(2)}) collective-permute-start(f32[568,128]{1,0:T(8,128)S(1)} %get-tuple-element.68), channel_id=1, source_target_pairs={{0,1},{1,2},{2,3},{3,4},{4,5},{5,6},{6,7},{8,9},{9,10},{10,11},{11... | collective-permute-start | bytes 872456 | tf_op jit(solution)/shard_map/ppermute | solution.py:324
  94.4 2.1 %collective-permute-start.13 = (f32[568,128]{1,0:T(8,128)S(1)}, f32[568,128]{1,0:T(8,128)S(1)}, u32[]{:S(2)}, u32[]{:S(2)}) collective-permute-start(f32[568,128]{1,0:T(8,128)S(1)} %get-tuple-element.69), channel_id=1, source_target_pairs={{1,0},{2,1},{3,2},{4,3},{5,4},{6,5},{7,6},{9,8},{10,9},{11,10},{12... | collective-permute-start | bytes 872456 | tf_op jit(solution)/shard_map/ppermute | solution.py:324
  96.6 0.0 all-gather.3.cloned.1.call-done
  96.6 0.0 copy-start
  96.6 1.2 copy-done
  97.8 3.6 %shard_map.57 = (f32[448,32,128]{2,1,0:T(8,128)}, f32[448,32,128]{2,1,0:T(8,128)}) custom-call(f32[128,16,128]{2,1,0:T(8,128)S(1)} %bitcast.10), custom_call_target="tpu_custom_call" | custom-call | tf_op jit(solution)/shard_map/pallas_call | solution.py:139
  101.4 0.0 collective-permute-done.12.refs_8_
  101.4 2.9 %collective-permute-done.13.refs_9_ = f32[568,128]{1,0:T(8,128)S(1)} collective-permute-done((f32[568,128]{1,0:T(8,128)S(1)}, f32[568,128]{1,0:T(8,128)S(1)}, u32[]{:S(2)}, u32[]{:S(2)}) %collective-permute-start.13) | collective-permute-done | bytes 290848 | tf_op jit(solution)/shard_map/ppermute | solution.py:324
  104.3 0.0 all-to-all-done.refs_5_
  104.3 15.3 %shard_map.58 = (f32[16,32,128]{2,1,0:T(8,128)}, f32[16,32,128]{2,1,0:T(8,128)}) custom-call(s32[3]{0:T(128)S(1)} %pad_add_fusion.refs_0_, f32[448,32,128]{2,1,0:T(8,128)} %get-tuple-element.62.refs_1_, f32[359,40,128]{2,1,0:T(8,128)} %get-tuple-element.63.refs_2_, f32[150,48,256]{2,1,0:T(8,128)} %get-tuple-element.64.refs_3_, ...), custom_call_target="tpu_custom_call" | custom-call | tf_op jit(solution)/shard_map/pallas_call | solution.py:139
Async XLA Ops:
  7.2 89.4 %all-gather.3.cloned.1.call-start = ((), (), s32[]{:S(2)}) async-start(), calls=%async_computation.1 | async-start | bytes 1056768 | tf_op jit(solution)/shard_map/all_gather | solution.py:761
  10.1 6.5 %collective-permute-start = (f32[296,128]{1,0:T(8,128)S(1)}, f32[296,128]{1,0:T(8,128)S(1)}, u32[]{:S(2)}, u32[]{:S(2)}) collective-permute-start(f32[296,128]{1,0:T(8,128)S(1)} %get-tuple-element.37), channel_id=1, source_target_pairs={{0,32},{32,64},{64,96},{1,33},{33,65},{65,97},{2,34},{34,66},{66,9... | collective-permute-start | bytes 454664 | tf_op jit(solution)/shard_map/ppermute | solution.py:324
  14.0 6.4 %collective-permute-start.1 = (f32[296,128]{1,0:T(8,128)S(1)}, f32[296,128]{1,0:T(8,128)S(1)}, u32[]{:S(2)}, u32[]{:S(2)}) collective-permute-start(f32[296,128]{1,0:T(8,128)S(1)} %get-tuple-element.38), channel_id=1, source_target_pairs={{32,0},{64,32},{96,64},{33,1},{65,33},{97,65},{34,2},{66,34},{98,6... | collective-permute-start | bytes 454664 | tf_op jit(solution)/shard_map/ppermute | solution.py:324
  20.6 10.2 %collective-permute-start.2 = (f32[800,128]{1,0:T(8,128)S(1)}, f32[800,128]{1,0:T(8,128)S(1)}, u32[]{:S(2)}, u32[]{:S(2)}) collective-permute-start(f32[800,128]{1,0:T(8,128)S(1)} %get-tuple-element.43), channel_id=1, source_target_pairs={{0,1},{1,2},{2,3},{3,4},{4,5},{5,6},{6,7},{8,9},{9,10},{10,11},{11... | collective-permute-start | bytes 1228808 | tf_op jit(solution)/shard_map/ppermute | solution.py:324
  25.9 9.3 %collective-permute-start.3 = (f32[800,128]{1,0:T(8,128)S(1)}, f32[800,128]{1,0:T(8,128)S(1)}, u32[]{:S(2)}, u32[]{:S(2)}) collective-permute-start(f32[800,128]{1,0:T(8,128)S(1)} %get-tuple-element.44), channel_id=1, source_target_pairs={{1,0},{2,1},{3,2},{4,3},{5,4},{6,5},{7,6},{9,8},{10,9},{11,10},{12... | collective-permute-start | bytes 1228808 | tf_op jit(solution)/shard_map/ppermute | solution.py:324
  36.5 5.3 %collective-permute-start.4 = (f32[280,128]{1,0:T(8,128)S(1)}, f32[280,128]{1,0:T(8,128)S(1)}, u32[]{:S(2)}, u32[]{:S(2)}) collective-permute-start(f32[280,128]{1,0:T(8,128)S(1)} %get-tuple-element.45), channel_id=1, source_target_pairs={{0,8},{8,16},{16,24},{1,9},{9,17},{17,25},{2,10},{10,18},{18,26},{... | collective-permute-start | bytes 430088 | tf_op jit(solution)/shard_map/ppermute | solution.py:324
  39.7 5.8 %collective-permute-start.5 = (f32[280,128]{1,0:T(8,128)S(1)}, f32[280,128]{1,0:T(8,128)S(1)}, u32[]{:S(2)}, u32[]{:S(2)}) collective-permute-start(f32[280,128]{1,0:T(8,128)S(1)} %get-tuple-element.46), channel_id=1, source_target_pairs={{8,0},{16,8},{24,16},{9,1},{17,9},{25,17},{10,2},{18,10},{26,18},{... | collective-permute-start | bytes 430088 | tf_op jit(solution)/shard_map/ppermute | solution.py:324
  51.3 5.0 %collective-permute-start.6 = (f32[160,128]{1,0:T(8,128)S(1)}, f32[160,128]{1,0:T(8,128)S(1)}, u32[]{:S(2)}, u32[]{:S(2)}) collective-permute-start(f32[160,128]{1,0:T(8,128)S(1)} %get-tuple-element.49), channel_id=1, source_target_pairs={{0,32},{32,64},{64,96},{1,33},{33,65},{65,97},{2,34},{34,66},{66,9... | collective-permute-start | bytes 245768 | tf_op jit(solution)/shard_map/ppermute | solution.py:324
  54.8 5.2 %collective-permute-start.7 = (f32[160,128]{1,0:T(8,128)S(1)}, f32[160,128]{1,0:T(8,128)S(1)}, u32[]{:S(2)}, u32[]{:S(2)}) collective-permute-start(f32[160,128]{1,0:T(8,128)S(1)} %get-tuple-element.50), channel_id=1, source_target_pairs={{32,0},{64,32},{96,64},{33,1},{65,33},{97,65},{34,2},{66,34},{98,6... | collective-permute-start | bytes 245768 | tf_op jit(solution)/shard_map/ppermute | solution.py:324
  60.1 7.6 %collective-permute-start.8 = (f32[240,128]{1,0:T(8,128)S(1)}, f32[240,128]{1,0:T(8,128)S(1)}, u32[]{:S(2)}, u32[]{:S(2)}) collective-permute-start(f32[240,128]{1,0:T(8,128)S(1)} %get-tuple-element.53), channel_id=1, source_target_pairs={{0,1},{1,2},{2,3},{3,4},{4,5},{5,6},{6,7},{8,9},{9,10},{10,11},{11... | collective-permute-start | bytes 368648 | tf_op jit(solution)/shard_map/ppermute | solution.py:324
  65.7 6.9 %collective-permute-start.9 = (f32[240,128]{1,0:T(8,128)S(1)}, f32[240,128]{1,0:T(8,128)S(1)}, u32[]{:S(2)}, u32[]{:S(2)}) collective-permute-start(f32[240,128]{1,0:T(8,128)S(1)} %get-tuple-element.54), channel_id=1, source_target_pairs={{1,0},{2,1},{3,2},{4,3},{5,4},{6,5},{7,6},{9,8},{10,9},{11,10},{12... | collective-permute-start | bytes 368648 | tf_op jit(solution)/shard_map/ppermute | solution.py:324
  73.1 4.6 %collective-permute-start.10 = (f32[128,128]{1,0:T(8,128)S(1)}, f32[128,128]{1,0:T(8,128)S(1)}, u32[]{:S(2)}, u32[]{:S(2)}) collective-permute-start(f32[128,128]{1,0:T(8,128)S(1)} %get-tuple-element.55), channel_id=1, source_target_pairs={{0,8},{8,16},{16,24},{1,9},{9,17},{17,25},{2,10},{10,18},{18,26},{... | collective-permute-start | bytes 196616 | tf_op jit(solution)/shard_map/ppermute | solution.py:324
  76.3 5.0 %collective-permute-start.11 = (f32[128,128]{1,0:T(8,128)S(1)}, f32[128,128]{1,0:T(8,128)S(1)}, u32[]{:S(2)}, u32[]{:S(2)}) collective-permute-start(f32[128,128]{1,0:T(8,128)S(1)} %get-tuple-element.56), channel_id=1, source_target_pairs={{8,0},{16,8},{24,16},{9,1},{17,9},{25,17},{10,2},{18,10},{26,18},{... | collective-permute-start | bytes 196616 | tf_op jit(solution)/shard_map/ppermute | solution.py:324
  85.1 19.3 %all-to-all-start = ((f32[128,8,128]{2,1,0:T(8,128)}), f32[128,8,128]{2,1,0:T(8,128)S(1)}, u32[]{:S(2)}, u32[]{:S(2)}) async-start(f32[128,8,128]{2,1,0:T(8,128)} %get-tuple-element.59), calls=%async_computation | async-start | bytes 1048576 | tf_op jit(solution)/shard_map/all_to_all | solution.py:780
  90.8 10.7 %collective-permute-start.12 = (f32[568,128]{1,0:T(8,128)S(1)}, f32[568,128]{1,0:T(8,128)S(1)}, u32[]{:S(2)}, u32[]{:S(2)}) collective-permute-start(f32[568,128]{1,0:T(8,128)S(1)} %get-tuple-element.68), channel_id=1, source_target_pairs={{0,1},{1,2},{2,3},{3,4},{4,5},{5,6},{6,7},{8,9},{9,10},{10,11},{11... | collective-permute-start | bytes 872456 | tf_op jit(solution)/shard_map/ppermute | solution.py:324
  94.4 9.9 %collective-permute-start.13 = (f32[568,128]{1,0:T(8,128)S(1)}, f32[568,128]{1,0:T(8,128)S(1)}, u32[]{:S(2)}, u32[]{:S(2)}) collective-permute-start(f32[568,128]{1,0:T(8,128)S(1)} %get-tuple-element.69), channel_id=1, source_target_pairs={{1,0},{2,1},{3,2},{4,3},{5,4},{6,5},{7,6},{9,8},{10,9},{11,10},{12... | collective-permute-start | bytes 872456 | tf_op jit(solution)/shard_map/ppermute | solution.py:324
  96.6 1.2 copy-start
Sparse Core Ops, SparseCore 0:
  11.4 67.2 all-gather.2

commit v7 on v5

--- a/solution.py
+++ b/solution.py
@@ -99,7 +99,7 @@
     return (max(shape[0], -(-7 * MIB // plane)), *shape[1:])
 
 
-def call(body, outs, scratch, *args, place=None, far_in={}, far_out=(), late=(), grant=48, pad=True):
+def call(body, outs, scratch, *args, far_in={}, far_out=(), late=(), grant=48, pad=True):
     shapes = [
         jax.ShapeDtypeStruct(padded(shape) if pad and k in far_out else shape, F32)
         for k, shape in enumerate(outs)
@@ -113,12 +113,10 @@
     extra = len(far_in) + len(far_out)
     if extra:
         held.append(pltpu.SemaphoreType.DMA((extra,)))
-    placed = place is not None
     count = len(args)
 
     def wrapped(*refs):
         refs = list(refs)
-        head = [refs.pop(0)] if placed else []
         ins, results = refs[:count], refs[count : count + len(outs)]
         rest = refs[count + len(outs) :]
         mine, rest = rest[: len(scratch)], rest[len(scratch) :]
@@ -130,12 +128,9 @@
             copies_out[k] = (rest[j], results[k].at[0 : outs[k][0]], rest[extra].at[j])
             results[k] = rest[j]
         far = Far(copies_in, copies_out, late)
-        body(far, *head, *ins, *results, *mine)
+        body(far, *ins, *results, *mine)
         far.finish()
 
-    if placed:
-        specs = [pl.BlockSpec(memory_space=pltpu.SMEM)] + specs
-        args = (place,) + args
     return pl.pallas_call(
         wrapped,
         out_shape=shapes,
@@ -474,7 +469,7 @@
     for z in range(Z1 // 2):
         part = rows[z * X1 // 2 : (z + 1) * X1 // 2, :]
         out = out + fold_lanes(part, first, Y1, z * Y1 // 2)
-    return out
+    return pltpu.roll(out, lax.axis_index("gy") * 32, 1)
 
 
 def parts(ref, planes, count=5):
@@ -551,13 +546,12 @@
 
     def body(step):
         gz, gx = step // 4, step % 4
+        tiles = [blocks[step * 4 + gy, first : first + 8, :] for gy in range(4)]
         for z in range(4):
-            plane = None
-            for gy in range(4):
-                block = blocks[step * 4 + gy, first : first + 8, :]
-                moved = roll(block, (gy - z) * 32, 1)
-                plane = moved if plane is None else jnp.where(group == gy, moved, plane)
-            out[gz * 4 + z, pl.ds(pl.multiple_of(gx * 8, 8), 8), :] = plane
+            plane = tiles[0]
+            for gy in range(1, 4):
+                plane = jnp.where(group == (z + gy) % 4, tiles[gy], plane)
+            out[gz * 4 + z, pl.ds(pl.multiple_of(gx * 8, 8), 8), :] = roll(plane, -32 * z, 1)
 
     loop(0, 32, body, 4)
 
@@ -678,7 +672,7 @@
 
 
 def finish(
-    far, place, stacked2, stacked1, stacked0, stacked34, forcing, v1, v0_zx, from_low, from_high,
+    far, stacked2, stacked1, stacked0, stacked34, forcing, v1, v0_zx, from_low, from_high,
     potential, residual,
     va1, vb1, v0, vb0, correction, f2, vb2, f3, va3, vb3, f4, vb4, tall,
 ):
@@ -697,7 +691,7 @@
             va1[W1 + z] = v1[z]
 
     coarse_cycle(far, forcing, stacked2, stacked34, correction, f2, vb2, f3, va3, vb3, f4, vb4, tall, meanwhile)
-    gz, gx, gy = place[0], place[1], place[2]
+    gz, gx, gy = (lax.axis_index(axis) for axis in ("gz", "gx", "gy"))
     planes = []
     for k in range(12):
         plane = correction[(gz * 4 + 28 + k) % 32]
@@ -752,7 +746,6 @@
     ext0, ext1 = (ZT0, XT0, 2 * LANES), (ZT1, XT1, LANES)
     everywhere = ("gz", "gx", "gy")
     devices = math.prod(lax.axis_size(axis) for axis in everywhere)
-    place = jnp.stack([lax.axis_index(axis) for axis in everywhere]).astype(jnp.int32)
     wet = jnp.where(cell_kind > 0, 1.0, 0.0).astype(F32)
     surface = jnp.where(cell_kind == 2, 1.0, 0.0).astype(F32)
     stiffness = conductivity * wet
@@ -799,7 +792,7 @@
         [(Z0, X0, Y0)] * 2,
         [ext1, ext1, ext0, ext0] + [level2] * 3 + [level3] * 3 + [level4] * 2 + [(14 * XT0, LANES)],
         operators, op1, op0, operators34, forcing2, v1, v0, from_low, from_high,
-        place=place, far_in={0: stack2, 1: stack1, 2: stack0, 3: stack34}, late=(1, 2),
+        far_in={0: stack2, 1: stack1, 2: stack0, 3: stack34}, late=(1, 2),
         far_out=(0, 1), pad=False,
     )
 

time: 125 us -> 125 us (level)
  waiting for transfers between devices: 29.7 us -> 33 us
  starting transfers between devices: 46.6 us -> 44.8 us
    ppermute x7, starting transfers between devices: 13 us -> 11.1 us  [shift(): lax.ppermute(low, axis, backward)]
    ppermute x7, waiting for transfers between devices: 3.38 us -> 5.14 us  [shift(): lax.ppermute(high, axis, forward)]
    ppermute x7, waiting for transfers between devices: 26.3 us -> 27.8 us  [shift(): lax.ppermute(low, axis, backward)]
  transfers between devices with their start and end apart: 16 -> 16, of which waited for: 11 -> 11; matrix products, arithmetic and copies ran while one was open for 0% -> 0% of each run, Pallas kernels for 12% -> 11%
where the time goes in v7:
time: 125 us
  starting transfers between devices  44.8 us (36%)
  waiting for transfers between devices  33 us (26%)
  Pallas kernels  30.3 us (24%)
  between operations  14.2 us (11%)
    pallas_call x10, Pallas kernels, call(): pl.pallas_call(wrapped, out_shape=shapes, in_specs=specs, out_specs=out_s...  30.3 us
    ppermute x7, waiting for transfers between devices, shift(): lax.ppermute(low, axis, backward)  27.8 us
    ppermute x7, starting transfers between devices, shift(): lax.ppermute(high, axis, forward)  27.2 us
    ppermute x7, starting transfers between devices, shift(): lax.ppermute(low, axis, backward)  11.1 us
    all_to_all x1, starting transfers between devices, shards(): forcing2 = lax.all_to_all(copies, everywhere, 0, 0)  6.38 us
    ppermute x7, waiting for transfers between devices, shift(): lax.ppermute(high, axis, forward)  5.14 us
  transfers between devices with their start and end apart: 16, of which 11 were waited for; matrix products, arithmetic and copies ran while one was open for 0% of the time, Pallas kernels for 11%

profile of v7, /device:TPU:1, one launch (start us, length us, event | category | flops | bytes accessed | tf_op | source)
XLA Modules:
  0.0 124.7 jit_solution(4614386131753644547)
XLA Ops:
  7.2 0.0 all-gather.3.cloned.1.call-start
  7.2 1.2 fusion.3
  8.4 0.2 shard_map.50
  8.6 4.0 %collective-permute-start = (f32[296,128]{1,0:T(8,128)S(1)}, f32[296,128]{1,0:T(8,128)S(1)}, u32[]{:S(2)}, u32[]{:S(2)}) collective-permute-start(f32[296,128]{1,0:T(8,128)S(1)} %get-tuple-element.37), channel_id=1, source_target_pairs={{0,32},{32,64},{64,96},{1,33},{33,65},{65,97},{2,34},{34,66},{66,9... | collective-permute-start | bytes 454664 | tf_op jit(solution)/shard_map/ppermute | solution.py:319
  12.6 1.3 %collective-permute-start.1 = (f32[296,128]{1,0:T(8,128)S(1)}, f32[296,128]{1,0:T(8,128)S(1)}, u32[]{:S(2)}, u32[]{:S(2)}) collective-permute-start(f32[296,128]{1,0:T(8,128)S(1)} %get-tuple-element.38), channel_id=1, source_target_pairs={{32,0},{64,32},{96,64},{33,1},{65,33},{97,65},{34,2},{66,34},{98,6... | collective-permute-start | bytes 454664 | tf_op jit(solution)/shard_map/ppermute | solution.py:319
  13.9 1.3 %collective-permute-done.refs_4_ = f32[296,128]{1,0:T(8,128)S(1)} collective-permute-done((f32[296,128]{1,0:T(8,128)S(1)}, f32[296,128]{1,0:T(8,128)S(1)}, u32[]{:S(2)}, u32[]{:S(2)}) %collective-permute-start) | collective-permute-done | bytes 151584 | tf_op jit(solution)/shard_map/ppermute | solution.py:319
  15.2 3.8 %collective-permute-done.1.refs_5_ = f32[296,128]{1,0:T(8,128)S(1)} collective-permute-done((f32[296,128]{1,0:T(8,128)S(1)}, f32[296,128]{1,0:T(8,128)S(1)}, u32[]{:S(2)}, u32[]{:S(2)}) %collective-permute-start.1) | collective-permute-done | bytes 151584 | tf_op jit(solution)/shard_map/ppermute | solution.py:319
  19.0 0.2 shard_map.51
  19.2 0.8 shard_map.57
  20.0 0.0 all-gather.3.cloned.1.call-update
  20.0 5.3 %collective-permute-start.2 = (f32[800,128]{1,0:T(8,128)S(1)}, f32[800,128]{1,0:T(8,128)S(1)}, u32[]{:S(2)}, u32[]{:S(2)}) collective-permute-start(f32[800,128]{1,0:T(8,128)S(1)} %get-tuple-element.43), channel_id=1, source_target_pairs={{0,1},{1,2},{2,3},{3,4},{4,5},{5,6},{6,7},{8,9},{9,10},{10,11},{11... | collective-permute-start | bytes 1228808 | tf_op jit(solution)/shard_map/ppermute | solution.py:319
  25.3 1.9 %collective-permute-start.3 = (f32[800,128]{1,0:T(8,128)S(1)}, f32[800,128]{1,0:T(8,128)S(1)}, u32[]{:S(2)}, u32[]{:S(2)}) collective-permute-start(f32[800,128]{1,0:T(8,128)S(1)} %get-tuple-element.44), channel_id=1, source_target_pairs={{1,0},{2,1},{3,2},{4,3},{5,4},{6,5},{7,6},{9,8},{10,9},{11,10},{12... | collective-permute-start | bytes 1228808 | tf_op jit(solution)/shard_map/ppermute | solution.py:319
  27.2 2.9 %collective-permute-done.2.refs_4_ = f32[800,128]{1,0:T(8,128)S(1)} collective-permute-done((f32[800,128]{1,0:T(8,128)S(1)}, f32[800,128]{1,0:T(8,128)S(1)}, u32[]{:S(2)}, u32[]{:S(2)}) %collective-permute-start.2) | collective-permute-done | bytes 409632 | tf_op jit(solution)/shard_map/ppermute | solution.py:319
  30.2 4.4 %collective-permute-done.3.refs_5_ = f32[800,128]{1,0:T(8,128)S(1)} collective-permute-done((f32[800,128]{1,0:T(8,128)S(1)}, f32[800,128]{1,0:T(8,128)S(1)}, u32[]{:S(2)}, u32[]{:S(2)}) %collective-permute-start.3) | collective-permute-done | bytes 409632 | tf_op jit(solution)/shard_map/ppermute | solution.py:319
  34.6 1.3 %shard_map.52 = (f32[280,128]{1,0:T(8,128)S(1)}, f32[280,128]{1,0:T(8,128)S(1)}) custom-call(f32[1,16,48,128]{3,2,1,0:T(8,128)S(1)} %get-tuple-element.39.refs_0_, f32[1,16,48,128]{3,2,1,0:T(8,128)S(1)} %get-tuple-element.40.refs_1_, f32[1,16,48,128]{3,2,1,0:T(8,128)S(1)} %get-tuple-element.41.refs_2_, f32[1,8,40,128]{3,2,1,0:T(8,128)S(1)} %get-tuple-element.42.refs_3_, ...), custom_call_target="tpu_custom_call" | custom-call | tf_op jit(solution)/shard_map/pallas_call | solution.py:134
  35.9 3.2 %collective-permute-start.4 = (f32[280,128]{1,0:T(8,128)S(1)}, f32[280,128]{1,0:T(8,128)S(1)}, u32[]{:S(2)}, u32[]{:S(2)}) collective-permute-start(f32[280,128]{1,0:T(8,128)S(1)} %get-tuple-element.45), channel_id=1, source_target_pairs={{0,8},{8,16},{16,24},{1,9},{9,17},{17,25},{2,10},{10,18},{18,26},{... | collective-permute-start | bytes 430088 | tf_op jit(solution)/shard_map/ppermute | solution.py:319
  39.1 1.3 %collective-permute-start.5 = (f32[280,128]{1,0:T(8,128)S(1)}, f32[280,128]{1,0:T(8,128)S(1)}, u32[]{:S(2)}, u32[]{:S(2)}) collective-permute-start(f32[280,128]{1,0:T(8,128)S(1)} %get-tuple-element.46), channel_id=1, source_target_pairs={{8,0},{16,8},{24,16},{9,1},{17,9},{25,17},{10,2},{18,10},{26,18},{... | collective-permute-start | bytes 430088 | tf_op jit(solution)/shard_map/ppermute | solution.py:319
  40.4 0.7 collective-permute-done.4.refs_6_
  41.1 4.2 %collective-permute-done.5.refs_7_ = f32[280,128]{1,0:T(8,128)S(1)} collective-permute-done((f32[280,128]{1,0:T(8,128)S(1)}, f32[280,128]{1,0:T(8,128)S(1)}, u32[]{:S(2)}, u32[]{:S(2)}) %collective-permute-start.5) | collective-permute-done | bytes 143392 | tf_op jit(solution)/shard_map/ppermute | solution.py:319
  45.3 5.7 %shard_map.53 = (f32[1,16,32,128]{3,2,1,0:T(8,128)S(1)}, f32[1,8,16,128]{3,2,1,0:T(8,128)S(1)}, f32[150,48,256]{2,1,0:T(8,128)}, f32[22,40,128]{2,1,0:T(8,128)S(...) custom-call(f32[1,16,48,128]{3,2,1,0:T(8,128)S(1)} %get-tuple-element.39.refs_0_, ...), custom_call_target="tpu_custom_call" | custom-call | tf_op jit(solution)/shard_map/pallas_call | solution.py:134
  51.1 3.0 %collective-permute-start.6 = (f32[160,128]{1,0:T(8,128)S(1)}, f32[160,128]{1,0:T(8,128)S(1)}, u32[]{:S(2)}, u32[]{:S(2)}) collective-permute-start(f32[160,128]{1,0:T(8,128)S(1)} %get-tuple-element.49), channel_id=1, source_target_pairs={{0,32},{32,64},{64,96},{1,33},{33,65},{65,97},{2,34},{34,66},{66,9... | collective-permute-start | bytes 245768 | tf_op jit(solution)/shard_map/ppermute | solution.py:319
  54.1 1.3 %collective-permute-start.7 = (f32[160,128]{1,0:T(8,128)S(1)}, f32[160,128]{1,0:T(8,128)S(1)}, u32[]{:S(2)}, u32[]{:S(2)}) collective-permute-start(f32[160,128]{1,0:T(8,128)S(1)} %get-tuple-element.50), channel_id=1, source_target_pairs={{32,0},{64,32},{96,64},{33,1},{65,33},{97,65},{34,2},{66,34},{98,6... | collective-permute-start | bytes 245768 | tf_op jit(solution)/shard_map/ppermute | solution.py:319
  55.4 0.2 collective-permute-done.6.refs_2_
  55.5 4.2 %collective-permute-done.7.refs_3_ = f32[160,128]{1,0:T(8,128)S(1)} collective-permute-done((f32[160,128]{1,0:T(8,128)S(1)}, f32[160,128]{1,0:T(8,128)S(1)}, u32[]{:S(2)}, u32[]{:S(2)}) %collective-permute-start.7) | collective-permute-done | bytes 81952 | tf_op jit(solution)/shard_map/ppermute | solution.py:319
  59.7 0.1 shard_map.54
  59.8 4.9 %collective-permute-start.8 = (f32[240,128]{1,0:T(8,128)S(1)}, f32[240,128]{1,0:T(8,128)S(1)}, u32[]{:S(2)}, u32[]{:S(2)}) collective-permute-start(f32[240,128]{1,0:T(8,128)S(1)} %get-tuple-element.53), channel_id=1, source_target_pairs={{0,1},{1,2},{2,3},{3,4},{4,5},{5,6},{6,7},{8,9},{9,10},{10,11},{11... | collective-permute-start | bytes 368648 | tf_op jit(solution)/shard_map/ppermute | solution.py:319
  64.7 1.9 %collective-permute-start.9 = (f32[240,128]{1,0:T(8,128)S(1)}, f32[240,128]{1,0:T(8,128)S(1)}, u32[]{:S(2)}, u32[]{:S(2)}) collective-permute-start(f32[240,128]{1,0:T(8,128)S(1)} %get-tuple-element.54), channel_id=1, source_target_pairs={{1,0},{2,1},{3,2},{4,3},{5,4},{6,5},{7,6},{9,8},{10,9},{11,10},{12... | collective-permute-start | bytes 368648 | tf_op jit(solution)/shard_map/ppermute | solution.py:319
  66.6 0.0 collective-permute-done.8.refs_2_
  66.6 4.3 %collective-permute-done.9.refs_3_ = f32[240,128]{1,0:T(8,128)S(1)} collective-permute-done((f32[240,128]{1,0:T(8,128)S(1)}, f32[240,128]{1,0:T(8,128)S(1)}, u32[]{:S(2)}, u32[]{:S(2)}) %collective-permute-start.9) | collective-permute-done | bytes 122912 | tf_op jit(solution)/shard_map/ppermute | solution.py:319
  70.9 0.5 shard_map.55
  71.4 3.2 %collective-permute-start.10 = (f32[128,128]{1,0:T(8,128)S(1)}, f32[128,128]{1,0:T(8,128)S(1)}, u32[]{:S(2)}, u32[]{:S(2)}) collective-permute-start(f32[128,128]{1,0:T(8,128)S(1)} %get-tuple-element.55), channel_id=1, source_target_pairs={{0,8},{8,16},{16,24},{1,9},{9,17},{17,25},{2,10},{10,18},{18,26},{... | collective-permute-start | bytes 196616 | tf_op jit(solution)/shard_map/ppermute | solution.py:319
  74.6 1.3 %collective-permute-start.11 = (f32[128,128]{1,0:T(8,128)S(1)}, f32[128,128]{1,0:T(8,128)S(1)}, u32[]{:S(2)}, u32[]{:S(2)}) collective-permute-start(f32[128,128]{1,0:T(8,128)S(1)} %get-tuple-element.56), channel_id=1, source_target_pairs={{8,0},{16,8},{24,16},{9,1},{17,9},{25,17},{10,2},{18,10},{26,18},{... | collective-permute-start | bytes 196616 | tf_op jit(solution)/shard_map/ppermute | solution.py:319
  75.9 0.0 collective-permute-done.10.refs_4_
  75.9 4.1 %collective-permute-done.11.refs_5_ = f32[128,128]{1,0:T(8,128)S(1)} collective-permute-done((f32[128,128]{1,0:T(8,128)S(1)}, f32[128,128]{1,0:T(8,128)S(1)}, u32[]{:S(2)}, u32[]{:S(2)}) %collective-permute-start.11) | collective-permute-done | bytes 65568 | tf_op jit(solution)/shard_map/ppermute | solution.py:319
  80.0 3.2 %shard_map.56 = (f32[8,40,128]{2,1,0:T(8,128)S(1)}, f32[16,48,256]{2,1,0:T(8,128)S(1)}, f32[128,8,128]{2,1,0:T(8,128)}, f32[359,40,128]{2,1,0:T(8,128)}, f32[568,128]{1,0:T(8,128)S(1)}, /*index=5*/f32[568,128]{1,0:T(8,128)S(1)}) custom-call(f32[1,8,40,128]{3,2,1,0:T(8,128)S(1)} %get-tuple-element.51.refs_0_, ...), custom_call_target="tpu_custom_call" | custom-call | tf_op jit(solution)/shard_map/pallas_call | solution.py:134
  83.2 6.4 %all-to-all-start = ((f32[128,8,128]{2,1,0:T(8,128)}), f32[128,8,128]{2,1,0:T(8,128)S(1)}, u32[]{:S(2)}, u32[]{:S(2)}) async-start(f32[128,8,128]{2,1,0:T(8,128)} %get-tuple-element.59), calls=%async_computation | async-start | bytes 1048576 | tf_op jit(solution)/shard_map/all_to_all | solution.py:781
  89.6 3.7 %collective-permute-start.12 = (f32[568,128]{1,0:T(8,128)S(1)}, f32[568,128]{1,0:T(8,128)S(1)}, u32[]{:S(2)}, u32[]{:S(2)}) collective-permute-start(f32[568,128]{1,0:T(8,128)S(1)} %get-tuple-element.68), channel_id=1, source_target_pairs={{0,1},{1,2},{2,3},{3,4},{4,5},{5,6},{6,7},{8,9},{9,10},{10,11},{11... | collective-permute-start | bytes 872456 | tf_op jit(solution)/shard_map/ppermute | solution.py:319
  93.2 2.1 %collective-permute-start.13 = (f32[568,128]{1,0:T(8,128)S(1)}, f32[568,128]{1,0:T(8,128)S(1)}, u32[]{:S(2)}, u32[]{:S(2)}) collective-permute-start(f32[568,128]{1,0:T(8,128)S(1)} %get-tuple-element.69), channel_id=1, source_target_pairs={{1,0},{2,1},{3,2},{4,3},{5,4},{6,5},{7,6},{9,8},{10,9},{11,10},{12... | collective-permute-start | bytes 872456 | tf_op jit(solution)/shard_map/ppermute | solution.py:319
  95.3 0.0 all-gather.3.cloned.1.call-done
  95.4 0.0 copy-start
  95.4 1.2 copy-done
  96.6 3.6 %shard_map.58 = (f32[448,32,128]{2,1,0:T(8,128)}, f32[448,32,128]{2,1,0:T(8,128)}) custom-call(f32[128,16,128]{2,1,0:T(8,128)S(1)} %bitcast.7), custom_call_target="tpu_custom_call" | custom-call | tf_op jit(solution)/shard_map/pallas_call | solution.py:134
  100.2 0.0 collective-permute-done.12.refs_7_
  100.2 2.9 %collective-permute-done.13.refs_8_ = f32[568,128]{1,0:T(8,128)S(1)} collective-permute-done((f32[568,128]{1,0:T(8,128)S(1)}, f32[568,128]{1,0:T(8,128)S(1)}, u32[]{:S(2)}, u32[]{:S(2)}) %collective-permute-start.13) | collective-permute-done | bytes 290848 | tf_op jit(solution)/shard_map/ppermute | solution.py:319
  103.1 0.0 all-to-all-done.refs_4_
  103.1 14.8 %shard_map.59 = (f32[16,32,128]{2,1,0:T(8,128)}, f32[16,32,128]{2,1,0:T(8,128)}) custom-call(f32[448,32,128]{2,1,0:T(8,128)} %get-tuple-element.62.refs_0_, f32[359,40,128]{2,1,0:T(8,128)} %get-tuple-element.63.refs_1_, f32[150,48,256]{2,1,0:T(8,128)} %get-tuple-element.64.refs_2_, f32[448,32,128]{2,1,0:T(8,128)} %get-tuple-element.65.refs_3_, ...), custom_call_target="tpu_custom_call" | custom-call | tf_op jit(solution)/shard_map/pallas_call | solution.py:134
Async XLA Ops:
  7.2 88.2 %all-gather.3.cloned.1.call-start = ((), (), s32[]{:S(2)}) async-start(), calls=%async_computation.1 | async-start | bytes 1056768 | tf_op jit(solution)/shard_map/all_gather | solution.py:761
  8.6 6.5 %collective-permute-start = (f32[296,128]{1,0:T(8,128)S(1)}, f32[296,128]{1,0:T(8,128)S(1)}, u32[]{:S(2)}, u32[]{:S(2)}) collective-permute-start(f32[296,128]{1,0:T(8,128)S(1)} %get-tuple-element.37), channel_id=1, source_target_pairs={{0,32},{32,64},{64,96},{1,33},{33,65},{65,97},{2,34},{34,66},{66,9... | collective-permute-start | bytes 454664 | tf_op jit(solution)/shard_map/ppermute | solution.py:319
  12.6 6.4 %collective-permute-start.1 = (f32[296,128]{1,0:T(8,128)S(1)}, f32[296,128]{1,0:T(8,128)S(1)}, u32[]{:S(2)}, u32[]{:S(2)}) collective-permute-start(f32[296,128]{1,0:T(8,128)S(1)} %get-tuple-element.38), channel_id=1, source_target_pairs={{32,0},{64,32},{96,64},{33,1},{65,33},{97,65},{34,2},{66,34},{98,6... | collective-permute-start | bytes 454664 | tf_op jit(solution)/shard_map/ppermute | solution.py:319
  20.0 10.2 %collective-permute-start.2 = (f32[800,128]{1,0:T(8,128)S(1)}, f32[800,128]{1,0:T(8,128)S(1)}, u32[]{:S(2)}, u32[]{:S(2)}) collective-permute-start(f32[800,128]{1,0:T(8,128)S(1)} %get-tuple-element.43), channel_id=1, source_target_pairs={{0,1},{1,2},{2,3},{3,4},{4,5},{5,6},{6,7},{8,9},{9,10},{10,11},{11... | collective-permute-start | bytes 1228808 | tf_op jit(solution)/shard_map/ppermute | solution.py:319
  25.3 9.3 %collective-permute-start.3 = (f32[800,128]{1,0:T(8,128)S(1)}, f32[800,128]{1,0:T(8,128)S(1)}, u32[]{:S(2)}, u32[]{:S(2)}) collective-permute-start(f32[800,128]{1,0:T(8,128)S(1)} %get-tuple-element.44), channel_id=1, source_target_pairs={{1,0},{2,1},{3,2},{4,3},{5,4},{6,5},{7,6},{9,8},{10,9},{11,10},{12... | collective-permute-start | bytes 1228808 | tf_op jit(solution)/shard_map/ppermute | solution.py:319
  35.9 5.3 %collective-permute-start.4 = (f32[280,128]{1,0:T(8,128)S(1)}, f32[280,128]{1,0:T(8,128)S(1)}, u32[]{:S(2)}, u32[]{:S(2)}) collective-permute-start(f32[280,128]{1,0:T(8,128)S(1)} %get-tuple-element.45), channel_id=1, source_target_pairs={{0,8},{8,16},{16,24},{1,9},{9,17},{17,25},{2,10},{10,18},{18,26},{... | collective-permute-start | bytes 430088 | tf_op jit(solution)/shard_map/ppermute | solution.py:319
  39.1 6.3 %collective-permute-start.5 = (f32[280,128]{1,0:T(8,128)S(1)}, f32[280,128]{1,0:T(8,128)S(1)}, u32[]{:S(2)}, u32[]{:S(2)}) collective-permute-start(f32[280,128]{1,0:T(8,128)S(1)} %get-tuple-element.46), channel_id=1, source_target_pairs={{8,0},{16,8},{24,16},{9,1},{17,9},{25,17},{10,2},{18,10},{26,18},{... | collective-permute-start | bytes 430088 | tf_op jit(solution)/shard_map/ppermute | solution.py:319
  51.1 4.5 %collective-permute-start.6 = (f32[160,128]{1,0:T(8,128)S(1)}, f32[160,128]{1,0:T(8,128)S(1)}, u32[]{:S(2)}, u32[]{:S(2)}) collective-permute-start(f32[160,128]{1,0:T(8,128)S(1)} %get-tuple-element.49), channel_id=1, source_target_pairs={{0,32},{32,64},{64,96},{1,33},{33,65},{65,97},{2,34},{34,66},{66,9... | collective-permute-start | bytes 245768 | tf_op jit(solution)/shard_map/ppermute | solution.py:319
  54.1 5.6 %collective-permute-start.7 = (f32[160,128]{1,0:T(8,128)S(1)}, f32[160,128]{1,0:T(8,128)S(1)}, u32[]{:S(2)}, u32[]{:S(2)}) collective-permute-start(f32[160,128]{1,0:T(8,128)S(1)} %get-tuple-element.50), channel_id=1, source_target_pairs={{32,0},{64,32},{96,64},{33,1},{65,33},{97,65},{34,2},{66,34},{98,6... | collective-permute-start | bytes 245768 | tf_op jit(solution)/shard_map/ppermute | solution.py:319
  59.8 6.8 %collective-permute-start.8 = (f32[240,128]{1,0:T(8,128)S(1)}, f32[240,128]{1,0:T(8,128)S(1)}, u32[]{:S(2)}, u32[]{:S(2)}) collective-permute-start(f32[240,128]{1,0:T(8,128)S(1)} %get-tuple-element.53), channel_id=1, source_target_pairs={{0,1},{1,2},{2,3},{3,4},{4,5},{5,6},{6,7},{8,9},{9,10},{10,11},{11... | collective-permute-start | bytes 368648 | tf_op jit(solution)/shard_map/ppermute | solution.py:319
  64.7 6.2 %collective-permute-start.9 = (f32[240,128]{1,0:T(8,128)S(1)}, f32[240,128]{1,0:T(8,128)S(1)}, u32[]{:S(2)}, u32[]{:S(2)}) collective-permute-start(f32[240,128]{1,0:T(8,128)S(1)} %get-tuple-element.54), channel_id=1, source_target_pairs={{1,0},{2,1},{3,2},{4,3},{5,4},{6,5},{7,6},{9,8},{10,9},{11,10},{12... | collective-permute-start | bytes 368648 | tf_op jit(solution)/shard_map/ppermute | solution.py:319
  71.4 4.5 %collective-permute-start.10 = (f32[128,128]{1,0:T(8,128)S(1)}, f32[128,128]{1,0:T(8,128)S(1)}, u32[]{:S(2)}, u32[]{:S(2)}) collective-permute-start(f32[128,128]{1,0:T(8,128)S(1)} %get-tuple-element.55), channel_id=1, source_target_pairs={{0,8},{8,16},{16,24},{1,9},{9,17},{17,25},{2,10},{10,18},{18,26},{... | collective-permute-start | bytes 196616 | tf_op jit(solution)/shard_map/ppermute | solution.py:319
  74.6 5.4 %collective-permute-start.11 = (f32[128,128]{1,0:T(8,128)S(1)}, f32[128,128]{1,0:T(8,128)S(1)}, u32[]{:S(2)}, u32[]{:S(2)}) collective-permute-start(f32[128,128]{1,0:T(8,128)S(1)} %get-tuple-element.56), channel_id=1, source_target_pairs={{8,0},{16,8},{24,16},{9,1},{17,9},{25,17},{10,2},{18,10},{26,18},{... | collective-permute-start | bytes 196616 | tf_op jit(solution)/shard_map/ppermute | solution.py:319
  83.2 20.0 %all-to-all-start = ((f32[128,8,128]{2,1,0:T(8,128)}), f32[128,8,128]{2,1,0:T(8,128)S(1)}, u32[]{:S(2)}, u32[]{:S(2)}) async-start(f32[128,8,128]{2,1,0:T(8,128)} %get-tuple-element.59), calls=%async_computation | async-start | bytes 1048576 | tf_op jit(solution)/shard_map/all_to_all | solution.py:781
  89.6 10.7 %collective-permute-start.12 = (f32[568,128]{1,0:T(8,128)S(1)}, f32[568,128]{1,0:T(8,128)S(1)}, u32[]{:S(2)}, u32[]{:S(2)}) collective-permute-start(f32[568,128]{1,0:T(8,128)S(1)} %get-tuple-element.68), channel_id=1, source_target_pairs={{0,1},{1,2},{2,3},{3,4},{4,5},{5,6},{6,7},{8,9},{9,10},{10,11},{11... | collective-permute-start | bytes 872456 | tf_op jit(solution)/shard_map/ppermute | solution.py:319
  93.2 9.9 %collective-permute-start.13 = (f32[568,128]{1,0:T(8,128)S(1)}, f32[568,128]{1,0:T(8,128)S(1)}, u32[]{:S(2)}, u32[]{:S(2)}) collective-permute-start(f32[568,128]{1,0:T(8,128)S(1)} %get-tuple-element.69), channel_id=1, source_target_pairs={{1,0},{2,1},{3,2},{4,3},{5,4},{6,5},{7,6},{9,8},{10,9},{11,10},{12... | collective-permute-start | bytes 872456 | tf_op jit(solution)/shard_map/ppermute | solution.py:319
  95.4 1.2 copy-start
Sparse Core Ops, SparseCore 0:
  20.1 67.2 all-gather.2

commit v8 on v7

--- a/solution.py
+++ b/solution.py
@@ -469,7 +469,7 @@
     for z in range(Z1 // 2):
         part = rows[z * X1 // 2 : (z + 1) * X1 // 2, :]
         out = out + fold_lanes(part, first, Y1, z * Y1 // 2)
-    return pltpu.roll(out, lax.axis_index("gy") * 32, 1)
+    return out
 
 
 def parts(ref, planes, count=5):
@@ -546,12 +546,13 @@
 
     def body(step):
         gz, gx = step // 4, step % 4
-        tiles = [blocks[step * 4 + gy, first : first + 8, :] for gy in range(4)]
         for z in range(4):
-            plane = tiles[0]
-            for gy in range(1, 4):
-                plane = jnp.where(group == (z + gy) % 4, tiles[gy], plane)
-            out[gz * 4 + z, pl.ds(pl.multiple_of(gx * 8, 8), 8), :] = roll(plane, -32 * z, 1)
+            plane = None
+            for gy in range(4):
+                block = blocks[step * 4 + gy, first : first + 8, :]
+                moved = roll(block, (gy - z) * 32, 1)
+                plane = moved if plane is None else jnp.where(group == gy, moved, plane)
+            out[gz * 4 + z, pl.ds(pl.multiple_of(gx * 8, 8), 8), :] = plane
 
     loop(0, 32, body, 4)
 

time: 125 us -> 125 us (level)
  transfers between devices with their start and end apart: 16 -> 16, of which waited for: 11 -> 11; matrix products, arithmetic and copies ran while one was open for 0% -> 0% of each run, Pallas kernels for 11% -> 12%
where the time goes in v8:
time: 125 us
  starting transfers between devices  44.8 us (36%)
  waiting for transfers between devices  32.4 us (26%)
  Pallas kernels  30.8 us (25%)
  between operations  14.3 us (11%)
    pallas_call x10, Pallas kernels, call(): pl.pallas_call(wrapped, out_shape=shapes, in_specs=specs, out_specs=out_s...  30.8 us
    ppermute x7, waiting for transfers between devices, shift(): lax.ppermute(low, axis, backward)  27.2 us
    ppermute x7, starting transfers between devices, shift(): lax.ppermute(high, axis, forward)  27.2 us
    ppermute x7, starting transfers between devices, shift(): lax.ppermute(low, axis, backward)  11.1 us
    all_to_all x1, starting transfers between devices, shards(): forcing2 = lax.all_to_all(copies, everywhere, 0, 0)  6.38 us
    ppermute x7, waiting for transfers between devices, shift(): lax.ppermute(high, axis, forward)  5.14 us
  transfers between devices with their start and end apart: 16, of which 11 were waited for; matrix products, arithmetic and copies ran while one was open for 0% of the time, Pallas kernels for 12%

profile of v8, /device:TPU:1, one launch (start us, length us, event | category | flops | bytes accessed | tf_op | source)
XLA Modules:
  0.0 124.7 jit_solution(9563006098996997311)
XLA Ops:
  7.2 0.0 all-gather.3.cloned.1.call-start
  7.2 1.2 fusion.3
  8.4 0.2 shard_map.50
  8.6 4.0 %collective-permute-start = (f32[296,128]{1,0:T(8,128)S(1)}, f32[296,128]{1,0:T(8,128)S(1)}, u32[]{:S(2)}, u32[]{:S(2)}) collective-permute-start(f32[296,128]{1,0:T(8,128)S(1)} %get-tuple-element.37), channel_id=1, source_target_pairs={{0,32},{32,64},{64,96},{1,33},{33,65},{65,97},{2,34},{34,66},{66,9... | collective-permute-start | bytes 454664 | tf_op jit(solution)/shard_map/ppermute | solution.py:319
  12.6 1.3 %collective-permute-start.1 = (f32[296,128]{1,0:T(8,128)S(1)}, f32[296,128]{1,0:T(8,128)S(1)}, u32[]{:S(2)}, u32[]{:S(2)}) collective-permute-start(f32[296,128]{1,0:T(8,128)S(1)} %get-tuple-element.38), channel_id=1, source_target_pairs={{32,0},{64,32},{96,64},{33,1},{65,33},{97,65},{34,2},{66,34},{98,6... | collective-permute-start | bytes 454664 | tf_op jit(solution)/shard_map/ppermute | solution.py:319
  13.9 1.3 %collective-permute-done.refs_4_ = f32[296,128]{1,0:T(8,128)S(1)} collective-permute-done((f32[296,128]{1,0:T(8,128)S(1)}, f32[296,128]{1,0:T(8,128)S(1)}, u32[]{:S(2)}, u32[]{:S(2)}) %collective-permute-start) | collective-permute-done | bytes 151584 | tf_op jit(solution)/shard_map/ppermute | solution.py:319
  15.2 3.8 %collective-permute-done.1.refs_5_ = f32[296,128]{1,0:T(8,128)S(1)} collective-permute-done((f32[296,128]{1,0:T(8,128)S(1)}, f32[296,128]{1,0:T(8,128)S(1)}, u32[]{:S(2)}, u32[]{:S(2)}) %collective-permute-start.1) | collective-permute-done | bytes 151584 | tf_op jit(solution)/shard_map/ppermute | solution.py:319
  19.0 0.2 shard_map.51
  19.2 0.7 shard_map.57
  19.9 0.0 all-gather.3.cloned.1.call-update
  19.9 5.3 %collective-permute-start.2 = (f32[800,128]{1,0:T(8,128)S(1)}, f32[800,128]{1,0:T(8,128)S(1)}, u32[]{:S(2)}, u32[]{:S(2)}) collective-permute-start(f32[800,128]{1,0:T(8,128)S(1)} %get-tuple-element.43), channel_id=1, source_target_pairs={{0,1},{1,2},{2,3},{3,4},{4,5},{5,6},{6,7},{8,9},{9,10},{10,11},{11... | collective-permute-start | bytes 1228808 | tf_op jit(solution)/shard_map/ppermute | solution.py:319
  25.2 1.9 %collective-permute-start.3 = (f32[800,128]{1,0:T(8,128)S(1)}, f32[800,128]{1,0:T(8,128)S(1)}, u32[]{:S(2)}, u32[]{:S(2)}) collective-permute-start(f32[800,128]{1,0:T(8,128)S(1)} %get-tuple-element.44), channel_id=1, source_target_pairs={{1,0},{2,1},{3,2},{4,3},{5,4},{6,5},{7,6},{9,8},{10,9},{11,10},{12... | collective-permute-start | bytes 1228808 | tf_op jit(solution)/shard_map/ppermute | solution.py:319
  27.2 2.9 %collective-permute-done.2.refs_4_ = f32[800,128]{1,0:T(8,128)S(1)} collective-permute-done((f32[800,128]{1,0:T(8,128)S(1)}, f32[800,128]{1,0:T(8,128)S(1)}, u32[]{:S(2)}, u32[]{:S(2)}) %collective-permute-start.2) | collective-permute-done | bytes 409632 | tf_op jit(solution)/shard_map/ppermute | solution.py:319
  30.1 4.4 %collective-permute-done.3.refs_5_ = f32[800,128]{1,0:T(8,128)S(1)} collective-permute-done((f32[800,128]{1,0:T(8,128)S(1)}, f32[800,128]{1,0:T(8,128)S(1)}, u32[]{:S(2)}, u32[]{:S(2)}) %collective-permute-start.3) | collective-permute-done | bytes 409632 | tf_op jit(solution)/shard_map/ppermute | solution.py:319
  34.5 1.3 %shard_map.52 = (f32[280,128]{1,0:T(8,128)S(1)}, f32[280,128]{1,0:T(8,128)S(1)}) custom-call(f32[1,16,48,128]{3,2,1,0:T(8,128)S(1)} %get-tuple-element.39.refs_0_, f32[1,16,48,128]{3,2,1,0:T(8,128)S(1)} %get-tuple-element.40.refs_1_, f32[1,16,48,128]{3,2,1,0:T(8,128)S(1)} %get-tuple-element.41.refs_2_, f32[1,8,40,128]{3,2,1,0:T(8,128)S(1)} %get-tuple-element.42.refs_3_, ...), custom_call_target="tpu_custom_call" | custom-call | tf_op jit(solution)/shard_map/pallas_call | solution.py:134
  35.8 3.2 %collective-permute-start.4 = (f32[280,128]{1,0:T(8,128)S(1)}, f32[280,128]{1,0:T(8,128)S(1)}, u32[]{:S(2)}, u32[]{:S(2)}) collective-permute-start(f32[280,128]{1,0:T(8,128)S(1)} %get-tuple-element.45), channel_id=1, source_target_pairs={{0,8},{8,16},{16,24},{1,9},{9,17},{17,25},{2,10},{10,18},{18,26},{... | collective-permute-start | bytes 430088 | tf_op jit(solution)/shard_map/ppermute | solution.py:319
  39.0 1.3 %collective-permute-start.5 = (f32[280,128]{1,0:T(8,128)S(1)}, f32[280,128]{1,0:T(8,128)S(1)}, u32[]{:S(2)}, u32[]{:S(2)}) collective-permute-start(f32[280,128]{1,0:T(8,128)S(1)} %get-tuple-element.46), channel_id=1, source_target_pairs={{8,0},{16,8},{24,16},{9,1},{17,9},{25,17},{10,2},{18,10},{26,18},{... | collective-permute-start | bytes 430088 | tf_op jit(solution)/shard_map/ppermute | solution.py:319
  40.3 0.7 collective-permute-done.4.refs_6_
  41.1 4.2 %collective-permute-done.5.refs_7_ = f32[280,128]{1,0:T(8,128)S(1)} collective-permute-done((f32[280,128]{1,0:T(8,128)S(1)}, f32[280,128]{1,0:T(8,128)S(1)}, u32[]{:S(2)}, u32[]{:S(2)}) %collective-permute-start.5) | collective-permute-done | bytes 143392 | tf_op jit(solution)/shard_map/ppermute | solution.py:319
  45.3 5.7 %shard_map.53 = (f32[1,16,32,128]{3,2,1,0:T(8,128)S(1)}, f32[1,8,16,128]{3,2,1,0:T(8,128)S(1)}, f32[150,48,256]{2,1,0:T(8,128)}, f32[22,40,128]{2,1,0:T(8,128)S(...) custom-call(f32[1,16,48,128]{3,2,1,0:T(8,128)S(1)} %get-tuple-element.39.refs_0_, ...), custom_call_target="tpu_custom_call" | custom-call | tf_op jit(solution)/shard_map/pallas_call | solution.py:134
  51.0 3.0 %collective-permute-start.6 = (f32[160,128]{1,0:T(8,128)S(1)}, f32[160,128]{1,0:T(8,128)S(1)}, u32[]{:S(2)}, u32[]{:S(2)}) collective-permute-start(f32[160,128]{1,0:T(8,128)S(1)} %get-tuple-element.49), channel_id=1, source_target_pairs={{0,32},{32,64},{64,96},{1,33},{33,65},{65,97},{2,34},{34,66},{66,9... | collective-permute-start | bytes 245768 | tf_op jit(solution)/shard_map/ppermute | solution.py:319
  54.0 1.3 %collective-permute-start.7 = (f32[160,128]{1,0:T(8,128)S(1)}, f32[160,128]{1,0:T(8,128)S(1)}, u32[]{:S(2)}, u32[]{:S(2)}) collective-permute-start(f32[160,128]{1,0:T(8,128)S(1)} %get-tuple-element.50), channel_id=1, source_target_pairs={{32,0},{64,32},{96,64},{33,1},{65,33},{97,65},{34,2},{66,34},{98,6... | collective-permute-start | bytes 245768 | tf_op jit(solution)/shard_map/ppermute | solution.py:319
  55.3 0.2 collective-permute-done.6.refs_2_
  55.5 4.2 %collective-permute-done.7.refs_3_ = f32[160,128]{1,0:T(8,128)S(1)} collective-permute-done((f32[160,128]{1,0:T(8,128)S(1)}, f32[160,128]{1,0:T(8,128)S(1)}, u32[]{:S(2)}, u32[]{:S(2)}) %collective-permute-start.7) | collective-permute-done | bytes 81952 | tf_op jit(solution)/shard_map/ppermute | solution.py:319
  59.6 0.1 shard_map.54
  59.7 4.9 %collective-permute-start.8 = (f32[240,128]{1,0:T(8,128)S(1)}, f32[240,128]{1,0:T(8,128)S(1)}, u32[]{:S(2)}, u32[]{:S(2)}) collective-permute-start(f32[240,128]{1,0:T(8,128)S(1)} %get-tuple-element.53), channel_id=1, source_target_pairs={{0,1},{1,2},{2,3},{3,4},{4,5},{5,6},{6,7},{8,9},{9,10},{10,11},{11... | collective-permute-start | bytes 368648 | tf_op jit(solution)/shard_map/ppermute | solution.py:319
  64.6 1.9 %collective-permute-start.9 = (f32[240,128]{1,0:T(8,128)S(1)}, f32[240,128]{1,0:T(8,128)S(1)}, u32[]{:S(2)}, u32[]{:S(2)}) collective-permute-start(f32[240,128]{1,0:T(8,128)S(1)} %get-tuple-element.54), channel_id=1, source_target_pairs={{1,0},{2,1},{3,2},{4,3},{5,4},{6,5},{7,6},{9,8},{10,9},{11,10},{12... | collective-permute-start | bytes 368648 | tf_op jit(solution)/shard_map/ppermute | solution.py:319
  66.5 0.0 collective-permute-done.8.refs_2_
  66.6 4.3 %collective-permute-done.9.refs_3_ = f32[240,128]{1,0:T(8,128)S(1)} collective-permute-done((f32[240,128]{1,0:T(8,128)S(1)}, f32[240,128]{1,0:T(8,128)S(1)}, u32[]{:S(2)}, u32[]{:S(2)}) %collective-permute-start.9) | collective-permute-done | bytes 122912 | tf_op jit(solution)/shard_map/ppermute | solution.py:319
  70.8 0.5 shard_map.55
  71.3 3.2 %collective-permute-start.10 = (f32[128,128]{1,0:T(8,128)S(1)}, f32[128,128]{1,0:T(8,128)S(1)}, u32[]{:S(2)}, u32[]{:S(2)}) collective-permute-start(f32[128,128]{1,0:T(8,128)S(1)} %get-tuple-element.55), channel_id=1, source_target_pairs={{0,8},{8,16},{16,24},{1,9},{9,17},{17,25},{2,10},{10,18},{18,26},{... | collective-permute-start | bytes 196616 | tf_op jit(solution)/shard_map/ppermute | solution.py:319
  74.5 1.3 %collective-permute-start.11 = (f32[128,128]{1,0:T(8,128)S(1)}, f32[128,128]{1,0:T(8,128)S(1)}, u32[]{:S(2)}, u32[]{:S(2)}) collective-permute-start(f32[128,128]{1,0:T(8,128)S(1)} %get-tuple-element.56), channel_id=1, source_target_pairs={{8,0},{16,8},{24,16},{9,1},{17,9},{25,17},{10,2},{18,10},{26,18},{... | collective-permute-start | bytes 196616 | tf_op jit(solution)/shard_map/ppermute | solution.py:319
  75.8 0.0 collective-permute-done.10.refs_4_
  75.8 4.1 %collective-permute-done.11.refs_5_ = f32[128,128]{1,0:T(8,128)S(1)} collective-permute-done((f32[128,128]{1,0:T(8,128)S(1)}, f32[128,128]{1,0:T(8,128)S(1)}, u32[]{:S(2)}, u32[]{:S(2)}) %collective-permute-start.11) | collective-permute-done | bytes 65568 | tf_op jit(solution)/shard_map/ppermute | solution.py:319
  79.9 3.2 %shard_map.56 = (f32[8,40,128]{2,1,0:T(8,128)S(1)}, f32[16,48,256]{2,1,0:T(8,128)S(1)}, f32[128,8,128]{2,1,0:T(8,128)}, f32[359,40,128]{2,1,0:T(8,128)}, f32[568,128]{1,0:T(8,128)S(1)}, /*index=5*/f32[568,128]{1,0:T(8,128)S(1)}) custom-call(f32[1,8,40,128]{3,2,1,0:T(8,128)S(1)} %get-tuple-element.51.refs_0_, ...), custom_call_target="tpu_custom_call" | custom-call | tf_op jit(solution)/shard_map/pallas_call | solution.py:134
  83.1 6.4 %all-to-all-start = ((f32[128,8,128]{2,1,0:T(8,128)}), f32[128,8,128]{2,1,0:T(8,128)S(1)}, u32[]{:S(2)}, u32[]{:S(2)}) async-start(f32[128,8,128]{2,1,0:T(8,128)} %get-tuple-element.59), calls=%async_computation | async-start | bytes 1048576 | tf_op jit(solution)/shard_map/all_to_all | solution.py:782
  89.5 3.7 %collective-permute-start.12 = (f32[568,128]{1,0:T(8,128)S(1)}, f32[568,128]{1,0:T(8,128)S(1)}, u32[]{:S(2)}, u32[]{:S(2)}) collective-permute-start(f32[568,128]{1,0:T(8,128)S(1)} %get-tuple-element.68), channel_id=1, source_target_pairs={{0,1},{1,2},{2,3},{3,4},{4,5},{5,6},{6,7},{8,9},{9,10},{10,11},{11... | collective-permute-start | bytes 872456 | tf_op jit(solution)/shard_map/ppermute | solution.py:319
  93.2 2.1 %collective-permute-start.13 = (f32[568,128]{1,0:T(8,128)S(1)}, f32[568,128]{1,0:T(8,128)S(1)}, u32[]{:S(2)}, u32[]{:S(2)}) collective-permute-start(f32[568,128]{1,0:T(8,128)S(1)} %get-tuple-element.69), channel_id=1, source_target_pairs={{1,0},{2,1},{3,2},{4,3},{5,4},{6,5},{7,6},{9,8},{10,9},{11,10},{12... | collective-permute-start | bytes 872456 | tf_op jit(solution)/shard_map/ppermute | solution.py:319
  95.3 0.0 all-gather.3.cloned.1.call-done
  95.3 0.0 copy-start
  95.3 1.2 copy-done
  96.5 4.2 %shard_map.58 = (f32[448,32,128]{2,1,0:T(8,128)}, f32[448,32,128]{2,1,0:T(8,128)}) custom-call(f32[128,16,128]{2,1,0:T(8,128)S(1)} %bitcast.7), custom_call_target="tpu_custom_call" | custom-call | tf_op jit(solution)/shard_map/pallas_call | solution.py:134
  100.7 0.0 collective-permute-done.12.refs_7_
  100.7 2.3 %collective-permute-done.13.refs_8_ = f32[568,128]{1,0:T(8,128)S(1)} collective-permute-done((f32[568,128]{1,0:T(8,128)S(1)}, f32[568,128]{1,0:T(8,128)S(1)}, u32[]{:S(2)}, u32[]{:S(2)}) %collective-permute-start.13) | collective-permute-done | bytes 290848 | tf_op jit(solution)/shard_map/ppermute | solution.py:319
  103.0 0.0 all-to-all-done.refs_4_
  103.0 14.8 %shard_map.59 = (f32[16,32,128]{2,1,0:T(8,128)}, f32[16,32,128]{2,1,0:T(8,128)}) custom-call(f32[448,32,128]{2,1,0:T(8,128)} %get-tuple-element.62.refs_0_, f32[359,40,128]{2,1,0:T(8,128)} %get-tuple-element.63.refs_1_, f32[150,48,256]{2,1,0:T(8,128)} %get-tuple-element.64.refs_2_, f32[448,32,128]{2,1,0:T(8,128)} %get-tuple-element.65.refs_3_, ...), custom_call_target="tpu_custom_call" | custom-call | tf_op jit(solution)/shard_map/pallas_call | solution.py:134
Async XLA Ops:
  7.2 88.1 %all-gather.3.cloned.1.call-start = ((), (), s32[]{:S(2)}) async-start(), calls=%async_computation.1 | async-start | bytes 1056768 | tf_op jit(solution)/shard_map/all_gather | solution.py:762
  8.6 6.5 %collective-permute-start = (f32[296,128]{1,0:T(8,128)S(1)}, f32[296,128]{1,0:T(8,128)S(1)}, u32[]{:S(2)}, u32[]{:S(2)}) collective-permute-start(f32[296,128]{1,0:T(8,128)S(1)} %get-tuple-element.37), channel_id=1, source_target_pairs={{0,32},{32,64},{64,96},{1,33},{33,65},{65,97},{2,34},{34,66},{66,9... | collective-permute-start | bytes 454664 | tf_op jit(solution)/shard_map/ppermute | solution.py:319
  12.6 6.4 %collective-permute-start.1 = (f32[296,128]{1,0:T(8,128)S(1)}, f32[296,128]{1,0:T(8,128)S(1)}, u32[]{:S(2)}, u32[]{:S(2)}) collective-permute-start(f32[296,128]{1,0:T(8,128)S(1)} %get-tuple-element.38), channel_id=1, source_target_pairs={{32,0},{64,32},{96,64},{33,1},{65,33},{97,65},{34,2},{66,34},{98,6... | collective-permute-start | bytes 454664 | tf_op jit(solution)/shard_map/ppermute | solution.py:319
  19.9 10.2 %collective-permute-start.2 = (f32[800,128]{1,0:T(8,128)S(1)}, f32[800,128]{1,0:T(8,128)S(1)}, u32[]{:S(2)}, u32[]{:S(2)}) collective-permute-start(f32[800,128]{1,0:T(8,128)S(1)} %get-tuple-element.43), channel_id=1, source_target_pairs={{0,1},{1,2},{2,3},{3,4},{4,5},{5,6},{6,7},{8,9},{9,10},{10,11},{11... | collective-permute-start | bytes 1228808 | tf_op jit(solution)/shard_map/ppermute | solution.py:319
  25.2 9.3 %collective-permute-start.3 = (f32[800,128]{1,0:T(8,128)S(1)}, f32[800,128]{1,0:T(8,128)S(1)}, u32[]{:S(2)}, u32[]{:S(2)}) collective-permute-start(f32[800,128]{1,0:T(8,128)S(1)} %get-tuple-element.44), channel_id=1, source_target_pairs={{1,0},{2,1},{3,2},{4,3},{5,4},{6,5},{7,6},{9,8},{10,9},{11,10},{12... | collective-permute-start | bytes 1228808 | tf_op jit(solution)/shard_map/ppermute | solution.py:319
  35.8 5.3 %collective-permute-start.4 = (f32[280,128]{1,0:T(8,128)S(1)}, f32[280,128]{1,0:T(8,128)S(1)}, u32[]{:S(2)}, u32[]{:S(2)}) collective-permute-start(f32[280,128]{1,0:T(8,128)S(1)} %get-tuple-element.45), channel_id=1, source_target_pairs={{0,8},{8,16},{16,24},{1,9},{9,17},{17,25},{2,10},{10,18},{18,26},{... | collective-permute-start | bytes 430088 | tf_op jit(solution)/shard_map/ppermute | solution.py:319
  39.0 6.3 %collective-permute-start.5 = (f32[280,128]{1,0:T(8,128)S(1)}, f32[280,128]{1,0:T(8,128)S(1)}, u32[]{:S(2)}, u32[]{:S(2)}) collective-permute-start(f32[280,128]{1,0:T(8,128)S(1)} %get-tuple-element.46), channel_id=1, source_target_pairs={{8,0},{16,8},{24,16},{9,1},{17,9},{25,17},{10,2},{18,10},{26,18},{... | collective-permute-start | bytes 430088 | tf_op jit(solution)/shard_map/ppermute | solution.py:319
  51.0 4.5 %collective-permute-start.6 = (f32[160,128]{1,0:T(8,128)S(1)}, f32[160,128]{1,0:T(8,128)S(1)}, u32[]{:S(2)}, u32[]{:S(2)}) collective-permute-start(f32[160,128]{1,0:T(8,128)S(1)} %get-tuple-element.49), channel_id=1, source_target_pairs={{0,32},{32,64},{64,96},{1,33},{33,65},{65,97},{2,34},{34,66},{66,9... | collective-permute-start | bytes 245768 | tf_op jit(solution)/shard_map/ppermute | solution.py:319
  54.0 5.6 %collective-permute-start.7 = (f32[160,128]{1,0:T(8,128)S(1)}, f32[160,128]{1,0:T(8,128)S(1)}, u32[]{:S(2)}, u32[]{:S(2)}) collective-permute-start(f32[160,128]{1,0:T(8,128)S(1)} %get-tuple-element.50), channel_id=1, source_target_pairs={{32,0},{64,32},{96,64},{33,1},{65,33},{97,65},{34,2},{66,34},{98,6... | collective-permute-start | bytes 245768 | tf_op jit(solution)/shard_map/ppermute | solution.py:319
  59.7 6.8 %collective-permute-start.8 = (f32[240,128]{1,0:T(8,128)S(1)}, f32[240,128]{1,0:T(8,128)S(1)}, u32[]{:S(2)}, u32[]{:S(2)}) collective-permute-start(f32[240,128]{1,0:T(8,128)S(1)} %get-tuple-element.53), channel_id=1, source_target_pairs={{0,1},{1,2},{2,3},{3,4},{4,5},{5,6},{6,7},{8,9},{9,10},{10,11},{11... | collective-permute-start | bytes 368648 | tf_op jit(solution)/shard_map/ppermute | solution.py:319
  64.6 6.2 %collective-permute-start.9 = (f32[240,128]{1,0:T(8,128)S(1)}, f32[240,128]{1,0:T(8,128)S(1)}, u32[]{:S(2)}, u32[]{:S(2)}) collective-permute-start(f32[240,128]{1,0:T(8,128)S(1)} %get-tuple-element.54), channel_id=1, source_target_pairs={{1,0},{2,1},{3,2},{4,3},{5,4},{6,5},{7,6},{9,8},{10,9},{11,10},{12... | collective-permute-start | bytes 368648 | tf_op jit(solution)/shard_map/ppermute | solution.py:319
  71.3 4.5 %collective-permute-start.10 = (f32[128,128]{1,0:T(8,128)S(1)}, f32[128,128]{1,0:T(8,128)S(1)}, u32[]{:S(2)}, u32[]{:S(2)}) collective-permute-start(f32[128,128]{1,0:T(8,128)S(1)} %get-tuple-element.55), channel_id=1, source_target_pairs={{0,8},{8,16},{16,24},{1,9},{9,17},{17,25},{2,10},{10,18},{18,26},{... | collective-permute-start | bytes 196616 | tf_op jit(solution)/shard_map/ppermute | solution.py:319
  74.5 5.4 %collective-permute-start.11 = (f32[128,128]{1,0:T(8,128)S(1)}, f32[128,128]{1,0:T(8,128)S(1)}, u32[]{:S(2)}, u32[]{:S(2)}) collective-permute-start(f32[128,128]{1,0:T(8,128)S(1)} %get-tuple-element.56), channel_id=1, source_target_pairs={{8,0},{16,8},{24,16},{9,1},{17,9},{25,17},{10,2},{18,10},{26,18},{... | collective-permute-start | bytes 196616 | tf_op jit(solution)/shard_map/ppermute | solution.py:319
  83.1 20.0 %all-to-all-start = ((f32[128,8,128]{2,1,0:T(8,128)}), f32[128,8,128]{2,1,0:T(8,128)S(1)}, u32[]{:S(2)}, u32[]{:S(2)}) async-start(f32[128,8,128]{2,1,0:T(8,128)} %get-tuple-element.59), calls=%async_computation | async-start | bytes 1048576 | tf_op jit(solution)/shard_map/all_to_all | solution.py:782
  89.5 11.2 %collective-permute-start.12 = (f32[568,128]{1,0:T(8,128)S(1)}, f32[568,128]{1,0:T(8,128)S(1)}, u32[]{:S(2)}, u32[]{:S(2)}) collective-permute-start(f32[568,128]{1,0:T(8,128)S(1)} %get-tuple-element.68), channel_id=1, source_target_pairs={{0,1},{1,2},{2,3},{3,4},{4,5},{5,6},{6,7},{8,9},{9,10},{10,11},{11... | collective-permute-start | bytes 872456 | tf_op jit(solution)/shard_map/ppermute | solution.py:319
  93.2 9.9 %collective-permute-start.13 = (f32[568,128]{1,0:T(8,128)S(1)}, f32[568,128]{1,0:T(8,128)S(1)}, u32[]{:S(2)}, u32[]{:S(2)}) collective-permute-start(f32[568,128]{1,0:T(8,128)S(1)} %get-tuple-element.69), channel_id=1, source_target_pairs={{1,0},{2,1},{3,2},{4,3},{5,4},{6,5},{7,6},{9,8},{10,9},{11,10},{12... | collective-permute-start | bytes 872456 | tf_op jit(solution)/shard_map/ppermute | solution.py:319
  95.3 1.2 copy-start
Sparse Core Ops, SparseCore 0:
  20.1 67.2 all-gather.2
